TPU v7x, 32 devices: a whole 2x2x4 slice. The times are simulated.
32 devices in a mesh: seq: 16 (over z, y, x), tensor: 2 (over core).
Axes of the slice: x: 2, y: 2, z: 4, core: 2. Of those that a mesh axis runs over, the one named last changes fastest.
Arguments:
- inputs: bfloat16 [4096, 2560], P('seq'), may hold values from -6 to 6
- segment_ids: int32 [4096], P('seq'), may hold values from 0 to 20, as said below
- cotangent: bfloat16 [4096, 2560], P('seq'), may hold values from -6 to 6
- attn_gain: bfloat16 [2560], P(('seq', 'tensor')), may hold values from 0.5 to 1.5
- query_weight: bfloat16 [2560, 2560], P('seq', 'tensor'), may hold values from -0.125 to 0.125
- key_value_weight: bfloat16 [2560, 512], P(('seq', 'tensor')), may hold values from -0.125 to 0.125
- out_weight: bfloat16 [2560, 2560], P('tensor', 'seq'), may hold values from -2.5 to 2.5
- out_bias: bfloat16 [2560], P(('seq', 'tensor')), may hold values from -1.5 to 1.5
- mlp_gain: bfloat16 [2560], P(('seq', 'tensor')), may hold values from 0.5 to 1.5
- gate_up_weight: bfloat16 [2, 2560, 7680], P(None, 'seq', 'tensor'), may hold values from -0.125 to 0.125
- gate_up_bias: bfloat16 [2, 7680], P(None, ('seq', 'tensor')), may hold values from -1.5 to 1.5
- down_weight: bfloat16 [7680, 2560], P('tensor', 'seq'), may hold values from -0.0625 to 0.0625
- down_bias: bfloat16 [2560], P(('seq', 'tensor')), may hold values from -1.5 to 1.5
Outputs:
- output: bfloat16 [4096, 2560], P('seq')
- input_grad: float32 [4096, 2560], P('seq')
- attn_gain_grad: float32 [2560], P(('seq', 'tensor'))
- query_grad: float32 [2560, 2560], P('seq', 'tensor')
- key_value_grad: float32 [2560, 512], P(('seq', 'tensor'))
- out_grad: float32 [2560, 2560], P('tensor', 'seq')
- out_bias_grad: float32 [2560], P(('seq', 'tensor'))
- mlp_gain_grad: float32 [2560], P(('seq', 'tensor'))
- gate_up_grad: float32 [2, 2560, 7680], P(None, 'seq', 'tensor')
- gate_up_bias_grad: float32 [2, 7680], P(None, ('seq', 'tensor'))
- down_grad: float32 [7680, 2560], P('tensor', 'seq')
- down_bias_grad: float32 [2560], P(('seq', 'tensor'))
Inputs may be any that keep to these rules, and one draw needn't show every extreme that they name: `segment_ids`: segment numbers never fall along the tokens, and a new segment begins at every multiple of 4096 tokens.
All inputs are finite; a program needn't handle non-finite values.
Results may differ from a plain program's by a relative error of at most 0.019.
Values may be sent and summed in bfloat16 or wider, within the bound.
A program may use at most 512 MiB of HBM per device.

v0:
```python
import jax
import jax.numpy as jnp
from jax import lax
from jax.sharding import PartitionSpec as P

HD = 256
FF = 7680
W = 2048
SEQ_LEN = 4096


epsilon = 1e-06


def from_behind(block, axis, distance):
    devices = range(lax.axis_size(axis))
    route = [(i - distance, i) for i in devices if i - distance in devices]
    return lax.ppermute(block, axis, route)


def normalize(stream, scale_vec):
    return (
        stream * lax.rsqrt(jnp.mean(stream * stream, axis=-1, keepdims=True) + epsilon) * scale_vec
    )


def rotate(values, places, head_count, direction):
    head_size = values.shape[1] // head_count
    shaped = values.reshape(values.shape[0], head_count, head_size)
    quarter = head_size // 4
    first_part = shaped[..., :quarter]
    second = shaped[..., quarter : 2 * quarter]
    remainder = shaped[..., 2 * quarter :]
    frequency = 10000.0 ** (-jnp.arange(quarter, dtype=jnp.float32) / quarter)
    angles = places.astype(jnp.float32)[:, None] * frequency[None, :]
    cosine = jnp.cos(angles)[:, None, :]
    sine_part = direction * jnp.sin(angles)[:, None, :]
    turned = jnp.concatenate(
        [
            first_part * cosine - second * sine_part,
            second * cosine + first_part * sine_part,
            remainder,
        ],
        axis=-1,
    )
    return turned.reshape(values.shape)


def body(
    inputs,
    segment_ids,
    cotangent,
    attn_gain,
    query_weight,
    key_value_weight,
    out_weight,
    out_bias,
    mlp_gain,
    gate_up_weight,
    gate_up_bias,
    down_weight,
    down_bias,
):
    seq_index = lax.axis_index("seq")
    tensor_index = lax.axis_index("tensor")
    tokens_here = inputs.shape[0]
    local_heads = query_weight.shape[1] // HD
    local_hidden = gate_up_weight.shape[2]
    reach_blocks = (W + tokens_here - 2) // tokens_here
    key_span = (reach_blocks + 1) * tokens_here
    scale_factor = HD ** (-0.5)
    kv_full, gain_one, bias_out, gain_two, bias_gate_up, bias_down = (
        lax.all_gather(key_value_weight, ("seq", "tensor"), axis=0, tiled=True),
        lax.all_gather(attn_gain, ("seq", "tensor"), axis=0, tiled=True),
        lax.all_gather(out_bias, ("seq", "tensor"), axis=0, tiled=True),
        lax.all_gather(mlp_gain, ("seq", "tensor"), axis=0, tiled=True),
        lax.all_gather(gate_up_bias, ("seq", "tensor"), axis=1, tiled=True),
        lax.all_gather(down_bias, ("seq", "tensor"), axis=0, tiled=True),
    )
    gain_one = gain_one.astype(jnp.float32)
    gain_two = gain_two.astype(jnp.float32)
    bias_out = bias_out.astype(jnp.float32)
    bias_down = bias_down.astype(jnp.float32)
    bias_local = lax.dynamic_slice_in_dim(
        bias_gate_up.astype(jnp.float32), tensor_index * local_hidden, local_hidden, 1
    )
    query_full, output_full = (
        lax.all_gather(query_weight, "seq", axis=0, tiled=True),
        lax.all_gather(out_weight, "seq", axis=1, tiled=True),
    )
    stream = inputs.astype(jnp.float32)
    places_global = seq_index * tokens_here + jnp.arange(tokens_here, dtype=jnp.int32)
    places = places_global % SEQ_LEN
    normed = normalize(stream, gain_one).astype(jnp.bfloat16)
    query_lin = jnp.dot(normed, query_full, preferred_element_type=jnp.float32)
    queries = (rotate(query_lin, places, local_heads, 1.0) * scale_factor).astype(jnp.bfloat16)
    key_value = jnp.dot(normed, kv_full, preferred_element_type=jnp.float32)
    keys_own = rotate(key_value[:, :HD], places, 1, 1.0).astype(jnp.bfloat16)
    values_own = key_value[:, HD:].astype(jnp.bfloat16)
    own_block = jnp.concatenate([keys_own, values_own], axis=1)
    own_marks = jnp.stack([segment_ids // 256, segment_ids % 256]).astype(jnp.bfloat16)
    window_start = (
        jnp.zeros((reach_blocks + 1, tokens_here, 2 * HD), jnp.bfloat16)
        .at[reach_blocks]
        .set(own_block)
    )
    marks_start = (
        jnp.zeros((reach_blocks + 1, 2, tokens_here), jnp.bfloat16).at[reach_blocks].set(own_marks)
    )

    def relay_step(step_index, relay_carry):
        key_block, mark_block, window, mark_window = relay_carry
        key_block, mark_block = from_behind((key_block, mark_block), "seq", 1)
        window = lax.dynamic_update_index_in_dim(window, key_block, reach_blocks - step_index, 0)
        mark_window = lax.dynamic_update_index_in_dim(
            mark_window, mark_block, reach_blocks - step_index, 0
        )
        return (key_block, mark_block, window, mark_window)

    relay_carry = lax.fori_loop(
        1, reach_blocks + 1, relay_step, (own_block, own_marks, window_start, marks_start)
    )
    window_keys = relay_carry[2].reshape(key_span, 2 * HD)
    window_marks = jnp.transpose(relay_carry[3], (1, 0, 2)).reshape(2, key_span)
    key_places = (seq_index - reach_blocks) * tokens_here + jnp.arange(key_span, dtype=jnp.int32)
    key_gap = places_global[:, None] - key_places[None, :]
    visible = (key_gap >= 0) & (key_gap < W) & (key_places[None, :] >= 0)
    visible = (
        visible
        & (own_marks[0][:, None] == window_marks[0][None, :])
        & (own_marks[1][:, None] == window_marks[1][None, :])
    )
    key_win = window_keys[:, :HD]
    value_win = window_keys[:, HD:]
    query_heads = queries.reshape(tokens_here, local_heads, HD)
    scores = jnp.einsum("qhd,kd->hqk", query_heads, key_win, preferred_element_type=jnp.float32)
    scores = jnp.where(visible[None], scores, -1e30)
    row_top = jnp.max(scores, axis=-1, keepdims=True)
    exponent = jnp.exp(scores - row_top)
    row_total = jnp.sum(exponent, axis=-1, keepdims=True)
    log_total = row_top + jnp.log(row_total)
    probs_low = (exponent / row_total).astype(jnp.bfloat16)
    mixed_low = (
        jnp.einsum("hqk,kd->qhd", probs_low, value_win, preferred_element_type=jnp.float32)
        .reshape(tokens_here, local_heads * HD)
        .astype(jnp.bfloat16)
    )
    branch = lax.psum(
        jnp.dot(mixed_low, output_full, preferred_element_type=jnp.float32).astype(jnp.bfloat16),
        "tensor",
    ).astype(jnp.float32)
    middle = stream + branch + bias_out
    gate_up_full, down_full = (
        lax.all_gather(gate_up_weight, "seq", axis=1, tiled=True),
        lax.all_gather(down_weight, "seq", axis=1, tiled=True),
    )
    normed_two = normalize(middle, gain_two).astype(jnp.bfloat16)
    gate_up_pre = jnp.einsum(
        "td,gdf->gtf", normed_two, gate_up_full, preferred_element_type=jnp.float32
    )
    gate_pre = gate_up_pre[0] + bias_local[0]
    up_pre = gate_up_pre[1] + bias_local[1]
    hidden = (jax.nn.gelu(gate_pre, approximate=True) * up_pre).astype(jnp.bfloat16)
    mlp_out = lax.psum(
        jnp.dot(hidden, down_full, preferred_element_type=jnp.float32).astype(jnp.bfloat16),
        "tensor",
    ).astype(jnp.float32)
    output = (middle + mlp_out + bias_down).astype(jnp.bfloat16)
    query_full, output_full = (
        lax.all_gather(query_weight, "seq", axis=0, tiled=True),
        lax.all_gather(out_weight, "seq", axis=1, tiled=True),
    )
    gate_up_full, down_full = (
        lax.all_gather(gate_up_weight, "seq", axis=1, tiled=True),
        lax.all_gather(down_weight, "seq", axis=1, tiled=True),
    )
    cot_full = cotangent.astype(jnp.float32)
    hidden_grad = jnp.dot(cotangent, down_full.T, preferred_element_type=jnp.float32)
    unit_value, unit_pull = jax.vjp(
        lambda gate_in, up_in: jax.nn.gelu(gate_in, approximate=True) * up_in, gate_pre, up_pre
    )
    gate_grad, up_grad = unit_pull(hidden_grad)
    gate_up_low = jnp.stack([gate_grad, up_grad]).astype(jnp.bfloat16)
    gate_up_term = jnp.einsum(
        "td,gtf->gdf", normed_two, gate_up_low, preferred_element_type=jnp.float32
    )
    down_term = jnp.dot(hidden.T, cotangent, preferred_element_type=jnp.float32)
    normed_two_grad = jnp.einsum(
        "gtf,gdf->td", gate_up_low, gate_up_full, preferred_element_type=jnp.float32
    )
    norm_two_value, norm_two_pull = jax.vjp(normalize, middle, gain_two)
    middle_part, gain_two_grad = norm_two_pull(normed_two_grad)
    middle_grad = cot_full + lax.psum(middle_part.astype(jnp.bfloat16), "tensor").astype(
        jnp.float32
    )
    middle_low = middle_grad.astype(jnp.bfloat16)
    out_weight_term = jnp.dot(mixed_low.T, middle_low, preferred_element_type=jnp.float32)
    mixed_grad = (
        jnp.dot(middle_low, output_full.T, preferred_element_type=jnp.float32)
        .astype(jnp.bfloat16)
        .reshape(tokens_here, local_heads, HD)
    )
    scores_again = jnp.einsum(
        "qhd,kd->hqk", query_heads, key_win, preferred_element_type=jnp.float32
    )
    probs_again = jnp.where(visible[None], jnp.exp(scores_again - log_total), 0.0)
    probs_again_low = probs_again.astype(jnp.bfloat16)
    prob_grad = jnp.einsum("qhd,kd->hqk", mixed_grad, value_win, preferred_element_type=jnp.float32)
    value_grad = jnp.einsum(
        "hqk,qhd->kd", probs_again_low, mixed_grad, preferred_element_type=jnp.float32
    )
    row_inner = jnp.sum(probs_again * prob_grad, axis=-1, keepdims=True)
    score_grad = (probs_again * (prob_grad - row_inner)).astype(jnp.bfloat16)
    query_grad_raw = jnp.einsum(
        "hqk,kd->qhd", score_grad, key_win, preferred_element_type=jnp.float32
    ).reshape(tokens_here, local_heads * HD)
    key_grad_raw = jnp.einsum(
        "hqk,qhd->kd", score_grad, query_heads, preferred_element_type=jnp.float32
    )
    window_grad = jnp.concatenate([key_grad_raw, value_grad], axis=1).reshape(
        reach_blocks + 1, tokens_here, 2 * HD
    )

    def return_step(step_index, traveling):
        arrived = from_behind(traveling.astype(jnp.bfloat16), "seq", -1).astype(traveling.dtype)
        return arrived + lax.dynamic_index_in_dim(window_grad, step_index, 0, keepdims=False)

    own_grad = lax.fori_loop(1, reach_blocks + 1, return_step, window_grad[0])
    key_lin_grad = rotate(own_grad[:, :HD], places, 1, -1.0)
    kv_grad_low = jnp.concatenate([key_lin_grad, own_grad[:, HD:]], axis=1).astype(jnp.bfloat16)
    query_lin_grad = (rotate(query_grad_raw, places, local_heads, -1.0) * scale_factor).astype(
        jnp.bfloat16
    )
    normed_grad = jnp.dot(
        query_lin_grad, query_full.T, preferred_element_type=jnp.float32
    ) + jnp.dot(kv_grad_low, kv_full.T, preferred_element_type=jnp.float32)
    norm_one_value, norm_one_pull = jax.vjp(normalize, stream, gain_one)
    stream_part, gain_one_grad = norm_one_pull(normed_grad)
    input_grad = middle_grad + lax.psum(stream_part.astype(jnp.bfloat16), "tensor").astype(
        jnp.float32
    )
    first_device = (tensor_index == 0).astype(jnp.float32)
    bias_out_term = jnp.sum(middle_grad, axis=0) * first_device
    bias_down_term = jnp.sum(cot_full, axis=0) * first_device
    gate_up_bias_local = jnp.sum(gate_up_low.astype(jnp.float32), axis=1)
    gate_up_bias_term = lax.dynamic_update_slice_in_dim(
        jnp.zeros((2, FF), jnp.float32), gate_up_bias_local, tensor_index * local_hidden, 1
    )
    kv_term = jnp.dot(normed.T, kv_grad_low, preferred_element_type=jnp.float32)
    query_term = jnp.dot(normed.T, query_lin_grad, preferred_element_type=jnp.float32)
    query_grad, out_grad, gate_up_grad, down_grad = (
        lax.psum_scatter(query_term, "seq", scatter_dimension=0, tiled=True),
        lax.psum_scatter(out_weight_term, "seq", scatter_dimension=1, tiled=True),
        lax.psum_scatter(gate_up_term, "seq", scatter_dimension=1, tiled=True),
        lax.psum_scatter(down_term, "seq", scatter_dimension=1, tiled=True),
    )
    (
        key_value_grad,
        attn_gain_grad,
        out_bias_grad,
        mlp_gain_grad,
        gate_up_bias_grad,
        down_bias_grad,
    ) = (
        lax.psum_scatter(kv_term, ("seq", "tensor"), scatter_dimension=0, tiled=True),
        lax.psum_scatter(gain_one_grad, ("seq", "tensor"), scatter_dimension=0, tiled=True),
        lax.psum_scatter(bias_out_term, ("seq", "tensor"), scatter_dimension=0, tiled=True),
        lax.psum_scatter(gain_two_grad, ("seq", "tensor"), scatter_dimension=0, tiled=True),
        lax.psum_scatter(gate_up_bias_term, ("seq", "tensor"), scatter_dimension=1, tiled=True),
        lax.psum_scatter(bias_down_term, ("seq", "tensor"), scatter_dimension=0, tiled=True),
    )
    return (
        output,
        input_grad,
        attn_gain_grad,
        query_grad,
        key_value_grad,
        out_grad,
        out_bias_grad,
        mlp_gain_grad,
        gate_up_grad,
        gate_up_bias_grad,
        down_grad,
        down_bias_grad,
    )


def solution(mesh):
    in_specs = (
        P("seq", None),
        P("seq"),
        P("seq", None),
        P(("seq", "tensor")),
        P("seq", "tensor"),
        P(("seq", "tensor"), None),
        P("tensor", "seq"),
        P(("seq", "tensor")),
        P(("seq", "tensor")),
        P(None, "seq", "tensor"),
        P(None, ("seq", "tensor")),
        P("tensor", "seq"),
        P(("seq", "tensor")),
    )
    out_specs = (
        P("seq", None),
        P("seq", None),
        P(("seq", "tensor")),
        P("seq", "tensor"),
        P(("seq", "tensor"), None),
        P("tensor", "seq"),
        P(("seq", "tensor")),
        P(("seq", "tensor")),
        P(None, "seq", "tensor"),
        P(None, ("seq", "tensor")),
        P("tensor", "seq"),
        P(("seq", "tensor")),
    )
    return jax.shard_map(body, mesh=mesh, in_specs=in_specs, out_specs=out_specs, check_vma=False)
```

profile of v0, /device:TPU:0, one launch (start us, length us, event | category | flops | bytes accessed | tf_op | source)
XLA Modules:
  0.0 4614.6 jit_solution(4879342786181157978)
XLA Ops:
  13.6 42.9 all-reduce.12
  59.6 12.0 all-gather.7.cloned.1.call-done
  76.9 111.7 %while.36 = (s32[]{:T(128)}, bf16[256,512]{1,0:T(8,128)(2,1)S(1)}, bf16[2,256]{1,0:T(2,128)(2,1)S(1)}, bf16[9,256,512]{2,1,0:T(8,128)(2,1)}, bf16[9,2,256]{2,1,0...) while((s32[]{:T(128)}, bf16[256,512]{1,0:T(8,128)(2,1)S(1)}, ...), condition=%wide.region_2.3_spmd, body=%wide.region_1.2_spmd.sunk | while | flops 6 | bytes 2105571 | solution.py:120
  213.7 78.9 %all-gather.11.cloned.1.call-done = bf16[1280,2560]{0,1:T(8,128)(2,1)} async-done(((bf16[1280,160]{0,1:T(8,128)(2,1)}), bf16[1280,2560]{0,1:T(8,128)(2,1)}) %all-gather.11.cloned.1.call-update) | async-done | bytes 6553616 | tf_op jit(solution)/shard_map/all_gather | solution.py:89
  300.3 38.8 all-gather
  341.4 385.5 %all-gather.13.cloned.1.call-done = bf16[2,2560,3840]{2,1,0:T(8,128)(2,1)} async-done(((bf16[2,160,3840]{2,1,0:T(8,128)(2,1)}), bf16[2,2560,3840]{2,1,0:T(8,128)(2,1)}) %all-gather.13.cloned.1.call-update) | async-done | bytes 39321616 | tf_op jit(solution)/shard_map/all_gather | solution.py:154
  726.9 20.9 convolution_bitcast_fusion.1
  747.8 199.3 %all-gather.15.cloned.1.call-done = bf16[3840,2560]{0,1:T(8,128)(2,1)} async-done(((bf16[3840,160]{0,1:T(8,128)(2,1)}), bf16[3840,2560]{0,1:T(8,128)(2,1)}) %all-gather.15.cloned.1.call-update) | async-done | bytes 19660816 | tf_op jit(solution)/shard_map/all_gather | solution.py:155
  947.1 18.3 fusion.42
  965.4 20.9 multiply_reduce_fusion
  995.9 10.9 convolution_convert_fusion.1
  1057.0 103.2 %while.37 = (s32[]{:T(128)}, f32[256,512]{1,0:T(8,128)S(1)}, f32[9,256,512]{2,1,0:T(8,128)}, s32[]{:T(128)}, s32[]{:T(128)}, /*index=5*/s32[]{:T(128)}) while((s32[]{:T(128)}, f32[256,512]{1,0:T(8,128)S(1)}, f32[9,256,512]{2,1,0:T(8,128)}, s32[]{:T(128)}, s32[]{:T(128)}, /*index=5*/s32[]{:T(128)}) %tuple.137), condition=%wide.region_12.13_spmd, body=%wide.region_11.12_spmd.sunk | while | flops 393221 | bytes 4194479 | solution.py:228
  1058.3 11.4 collective-permute-done.2
  1096.2 9.9 collective-permute-done.2
  1109.4 13.9 collective-permute-done.2
  1177.8 32.9 convolution_bitcast_fusion
  1210.7 112.6 %copy.108 = f32[2,2560,3840]{2,0,1:T(2,128)} copy(f32[2,2560,3840]{1,2,0:T(8,128)} %convolution_bitcast_fusion) | data formatting | bytes 157286400 | tf_op jit(solution)/shard_map/td,gtf->gdf/transpose | solution.py:184
  1342.2 17.3 fusion.100
  1367.2 51.9 %all-reduce.11 = (f32[2560]{0:T(1024)S(1)}, f32[2560]{0:T(1024)S(1)}, f32[2560]{0:T(1024)S(1)}, f32[2560]{0:T(1024)S(1)}) all-reduce(f32[2560]{0:T(1024)S(1)} %copy-done.27, f32[2560]{0:T(1024)S(1)} %broadcast_multiply_fusion.2, f32[2560]{0:T(1024)S(1)} %copy-done.28, ...), channel_id=2, replica_groups=mesh['seq'=16,'tensor'=2] {'seq','tensor'}, use_global_device_ids=true, to_apply=%region_16.17.clone | all-reduce | flops 10240 | bytes 81920
  1424.5 1908.4 %all-reduce.23.cloned.1.call-done = f32[2,2560,3840]{2,0,1:T(2,128)} async-done(((f32[2,2560,3840]{2,0,1:T(2,128)}), f32[2,2560,3840]{2,0,1:T(2,128)}) %all-reduce.23.cloned.1.call-update) | async-done | bytes 78643216
  3339.5 138.2 %reduce-scatter.10.cloned.1.call-done = f32[80,512]{1,0:T(8,128)} async-done(((f32[2560,512]{1,0:T(8,128)}), f32[80,512]{1,0:T(8,128)}) %reduce-scatter.10.cloned.1.call-update) | async-done | bytes 163856 | tf_op jit(solution)/shard_map/reduce_scatter | solution.py:265
  3477.7 271.2 %reduce-scatter.12.cloned.1.call-done = f32[1280,160]{0,1:T(8,128)} async-done(((f32[1280,2560]{0,1:T(8,128)}), f32[1280,160]{0,1:T(8,128)}) %reduce-scatter.12.cloned.1.call-update) | async-done | bytes 819216 | tf_op jit(solution)/shard_map/reduce_scatter | solution.py:253
  3748.9 280.4 %reduce-scatter.8.cloned.1.call-done = f32[160,1280]{1,0:T(8,128)} async-done(((f32[2560,1280]{1,0:T(8,128)}), f32[160,1280]{1,0:T(8,128)}) %reduce-scatter.8.cloned.1.call-update) | async-done | bytes 819216 | tf_op jit(solution)/shard_map/reduce_scatter | solution.py:252
  4029.3 578.6 %reduce-scatter.14.cloned.1.call-done = f32[3840,160]{0,1:T(8,128)} async-done(((f32[3840,2560]{0,1:T(8,128)}), f32[3840,160]{0,1:T(8,128)}) %reduce-scatter.14.cloned.1.call-update) | async-done | bytes 2457616 | tf_op jit(solution)/shard_map/reduce_scatter | solution.py:255
  (330 shorter events, 343.4 us)
Async XLA Ops:
  7.2 64.4 %all-gather.7.cloned.1.call-start = ((), (), s32[]{:S(2)}) async-start(), calls=%async_computation.5 | async-start | bytes 2703360 | tf_op jit(solution)/shard_map/all_gather | solution.py:73
  7.9 183.7 %all-gather.9.cloned.1.call-start = ((), (), s32[]{:S(2)}) async-start(), calls=%async_computation.6 | async-start | bytes 6963200 | tf_op jit(solution)/shard_map/all_gather | solution.py:88
  8.7 284.0 %all-gather.11.cloned.1.call-start = ((), (), s32[]{:S(2)}) async-start(), calls=%async_computation.7 | async-start | bytes 6963200 | tf_op jit(solution)/shard_map/all_gather | solution.py:89
  9.4 330.0 %all-reduce.19.cloned.1.call-start = ((), (), s32[]{:S(2)}) async-start(), calls=%async_computation.8 | async-start | bytes 2621440 | tf_op jit(solution)/shard_map/psum | solution.py:148
  76.9 12.1 collective-permute-start
  100.8 15.5 collective-permute-start
  105.0 11.3 collective-permute-start.1
  117.0 11.8 collective-permute-start
  139.5 17.2 collective-permute-start
  157.5 15.9 collective-permute-start
  174.2 13.8 collective-permute-start
  299.1 427.8 %all-gather.13.cloned.1.call-start = ((), (), s32[]{:S(2)}) async-start(), calls=%async_computation.9 | async-start | bytes 41779200 | tf_op jit(solution)/shard_map/all_gather | solution.py:154
  299.7 647.4 %all-gather.15.cloned.1.call-start = ((), (), s32[]{:S(2)}) async-start(), calls=%async_computation.10 | async-start | bytes 20889600 | tf_op jit(solution)/shard_map/all_gather | solution.py:155
  300.2 708.2 %all-reduce.21.cloned.1.call-start = ((), (), s32[]{:S(2)}) async-start(), calls=%async_computation.11 | async-start | bytes 2621440 | tf_op jit(solution)/shard_map/psum | solution.py:193
  990.1 371.3 %reduce-scatter.16.cloned.1.call-start = ((), (), s32[]{:S(2)}) async-start(), calls=%async_computation.16 | async-start | bytes 4055040
  995.9 367.1 %all-reduce.25.cloned.1.call-start = ((), (), s32[]{:S(2)}) async-start(), calls=%async_computation.18 | async-start | bytes 5242880 | tf_op jit(solution)/shard_map/psum | solution.py:164
  1057.0 12.8 collective-permute-start.2
  1094.9 11.2 collective-permute-start.2
  1108.0 15.2 collective-permute-start.2
  1177.7 2155.2 %all-reduce.23.cloned.1.call-start = ((), (), s32[]{:S(2)}) async-start(), calls=%async_computation.17 | async-start | bytes 157286400
  1323.3 2154.4 %reduce-scatter.10.cloned.1.call-start = ((), (), s32[]{:S(2)}) async-start(), calls=%async_computation.13 | async-start | bytes 5406720 | tf_op jit(solution)/shard_map/reduce_scatter | solution.py:265
  1326.7 2422.3 %reduce-scatter.12.cloned.1.call-start = ((), (), s32[]{:S(2)}) async-start(), calls=%async_computation.14 | async-start | bytes 13926400 | tf_op jit(solution)/shard_map/reduce_scatter | solution.py:253
  1335.3 2694.0 %reduce-scatter.8.cloned.1.call-start = ((), (), s32[]{:S(2)}) async-start(), calls=%async_computation.12 | async-start | bytes 13926400 | tf_op jit(solution)/shard_map/reduce_scatter | solution.py:252
  1342.1 3265.8 %reduce-scatter.14.cloned.1.call-start = ((), (), s32[]{:S(2)}) async-start(), calls=%async_computation.15 | async-start | bytes 41779200 | tf_op jit(solution)/shard_map/reduce_scatter | solution.py:255
  (64 other events, 3427.7 us)
Sparse Core Ops, SparseCore 0:
  10.9 60.6 all-gather.6
  74.3 117.2 all-gather.8
  194.2 98.3 all-gather.10
  299.2 18.2 all-reduce.18
  320.3 406.5 all-gather.12
  729.9 217.1 all-gather.14
  990.2 18.1 all-reduce.20
  1013.8 111.6 reduce-scatter.15
  1177.8 29.5 all-reduce.24
  1323.4 2009.4 all-reduce.22
  3335.7 141.9 reduce-scatter.9
  3480.4 268.4 reduce-scatter.11
  3751.8 277.4 reduce-scatter.7
  4035.8 572.0 reduce-scatter.13
where the time goes:
time: 4620 us; the launch traced here: 4610 us
  waiting for transfers between devices  3960 us (86%)
  matrix products  199 us (4%)
  local copies, waits for them, and re-layouts  166 us (4%)
  blocking collectives  134 us (3%)
  starting transfers between devices  96 us (2%)
  other arithmetic  48.8 us (1%)
    unnamed x16, waiting for transfers between devices  1910 us
    reduce_scatter x1, waiting for transfers between devices, body(): lax.psum_scatter(down_term, 'seq', scatter_dimension=1, tiled=True)  579 us
    all_gather x1, waiting for transfers between devices, body(): lax.all_gather(gate_up_weight, 'seq', axis=1, tiled=True)  385 us
    reduce_scatter x1, waiting for transfers between devices, body(): lax.psum_scatter(query_term, 'seq', scatter_dimension=0, tiled=True)  280 us
    reduce_scatter x1, waiting for transfers between devices, body(): lax.psum_scatter(out_weight_term, 'seq', scatter_dimension=1, tiled=True)  271 us
    all_gather x1, waiting for transfers between devices, body(): lax.all_gather(down_weight, 'seq', axis=1, tiled=True)  199 us
    reduce_scatter x1, waiting for transfers between devices, body(): lax.psum_scatter(kv_term, ('seq', 'tensor'), scatter_dimension=0, tiled=T...  138 us
    transpose x1, local copies, waits for them, and re-layouts, body(): jnp.einsum('td,gtf->gdf', normed_two, gate_up_low, preferred_element_type...  113 us
  transfers between devices with their start and end apart: 38, of which 26 were waited for; matrix products, arithmetic and copies ran while one was open for 8% of the time, Pallas kernels for 0%

commit v1 on v0

v1 whole, which is shorter than its diff:
```python
import functools

import jax
import jax.numpy as jnp
from jax import lax
from jax.experimental import pallas as pl
from jax.experimental.pallas import tpu as pltpu
from jax.sharding import PartitionSpec as P

HD = 256
W = 2048
SEQ_LEN = 4096
LINE = 4
RING = 16
LANES = 128

epsilon = 1e-06
bf16 = jnp.bfloat16
f32 = jnp.float32
MESH = pl.DeviceIdType.MESH
ANY = pl.BlockSpec(memory_space=pl.ANY)


class Place:
    def __init__(self):
        seq = lax.axis_index("seq")
        self.t = lax.axis_index("tensor")
        self.r = lax.rem(seq, RING)
        self.base = seq - self.r
        self.z = lax.div(self.r, 4)
        self.q = lax.rem(self.r, 4)
        self.xq = self.q + 1 - 2 * lax.rem(self.q, 2)
        self.yq = self.q + 2 - 4 * lax.div(self.q, 2)
        self.dq = 3 - self.q
        self.half = lax.div(self.z, 2)
        self.inner = self.z + self.half * (3 - 2 * self.z)

    def at(self, z, q):
        return (self.base + 4 * z + q, self.t)

    def other(self):
        return (self.base + self.r, 1 - self.t)

    def order(self, j):
        v = j + self.inner * (1 - 2 * j if j < 2 else 0)
        return v + self.half * (3 - 2 * v)

    def greet(self, whole=False):
        barrier = pltpu.get_barrier_semaphore()
        if whole:
            peers = [
                (self.base + lax.rem(self.r + k, RING), self.t) for k in range(1, RING)
            ]
        else:
            peers = [self.at(lax.rem(self.z + k, 4), self.q) for k in range(1, 4)]
            peers += [self.at(self.z, self.xq), self.at(self.z, self.yq)]
        peers.append(self.other())
        for peer in peers:
            pl.semaphore_signal(barrier, inc=1, device_id=peer, device_id_type=MESH)
        pl.semaphore_wait(barrier, len(peers))


def remote(src, dst, send, recv, device):
    return pltpu.make_async_remote_copy(
        src_ref=src, dst_ref=dst, send_sem=send, recv_sem=recv, device_id=device, device_id_type=MESH
    )


def run(steps):
    steps = list(steps)
    while steps:
        for step in list(steps):
            try:
                next(step)
            except StopIteration:
                steps.remove(step)


GATHER_SEMS = [
    pltpu.SemaphoreType.DMA((4, 6)),
    pltpu.SemaphoreType.DMA((4, 5)),
    pltpu.SemaphoreType.DMA,
]


def gather(me, own, slot, part, sems, pieces=None):
    snd, rcv, loc = sems
    local = pltpu.make_async_copy(own, slot(me.z, me.q), loc)
    local.start()

    def line(z, k, src, to):
        return remote(src, slot(z, me.q), snd.at[z, k], rcv.at[z, 0], me.at(to, me.q))

    def across(z, k, src):
        q = (me.xq, me.yq)[k]
        return remote(src, slot(z, me.q), snd.at[z, 2 + k], rcv.at[z, 1 + k], me.at(me.z, q))

    def corner(z, k):
        src = part(z, (me.xq, me.yq)[k], k)
        return remote(src, src, snd.at[z, 4 + k], rcv.at[z, 3 + k], me.at(me.z, (me.yq, me.xq)[k]))

    if pieces is None:

        @pl.when(me.z < 3)
        def _():
            line(me.z, 0, own, me.z + 1).start()

        @pl.when(me.z > 0)
        def _():
            line(me.z, 1, own, me.z - 1).start()

    else:
        for j in range(1, 4):
            z = me.order(j)
            remote(
                pieces(z), slot(me.z, me.q), snd.at[z, 0], rcv.at[me.z, 0], me.at(z, me.q)
            ).start()
    for k in range(2):
        across(me.z, k, own).start()
    yield
    for j in range(1, 5):
        if j < 4:
            z = me.order(j)
            remote(
                slot(z, me.q), slot(z, me.q), snd.at[z, 0], rcv.at[z, 0], me.at(me.z, me.q)
            ).wait_recv()
            if pieces is None:

                @pl.when(me.inner == 1)
                def _():
                    step = 3 - 2 * me.z if j == 1 else 2 * me.z - 3
                    line(z, 0, slot(z, me.q), me.z + step).start()

            for k in range(2):
                across(z, k, slot(z, me.q)).start()
        z = me.order(j - 1)
        for k in range(2):
            q = (me.xq, me.yq)[k]
            remote(
                slot(z, q), slot(z, q), snd.at[z, 2 + k], rcv.at[z, 1 + k], me.at(me.z, q)
            ).wait_recv()
            corner(z, k).start()
        yield
    for j in range(4):
        z = me.order(j)
        for k in range(2):
            src = part(z, me.dq, k)
            remote(src, src, snd.at[z, 4 + k], rcv.at[z, 3 + k], me.at(me.z, me.xq)).wait_recv()
    local.wait()
    for j in range(4):
        z = me.order(j)
        for k in range(2):
            across(z, k, slot(z, me.q)).wait_send()
            corner(z, k).wait_send()
    if pieces is None:

        @pl.when(me.z < 3)
        def _():
            line(me.z, 0, own, me.z + 1).wait_send()

        @pl.when(me.z > 0)
        def _():
            line(me.z, 1, own, me.z - 1).wait_send()

        @pl.when(me.inner == 1)
        def _():
            for j in range(1, 4):
                z = me.order(j)
                line(z, 0, slot(z, me.q), me.z).wait_send()

    else:
        for j in range(1, 4):
            z = me.order(j)
            remote(pieces(z), pieces(z), snd.at[z, 0], rcv.at[z, 0], me.at(z, me.q)).wait_send()


SPREAD_SEMS = [
    pltpu.SemaphoreType.DMA((4, 3)),
    pltpu.SemaphoreType.DMA((4, 2)),
    pltpu.SemaphoreType.DMA,
]


def spread(me, src, dst, sems):
    snd, rcv, loc = sems
    rows = src.shape[0] // 2
    mine = pl.ds(pl.multiple_of(me.t * rows, rows), rows)
    local = pltpu.make_async_copy(src, dst.at[me.z], loc)
    local.start()

    def slot(z):
        return dst.at[z, mine]

    def line(z, k, source, to):
        return remote(source, slot(z), snd.at[z, k], rcv.at[z, 0], me.at(to, me.q))

    def share(z):
        return remote(slot(z), slot(z), snd.at[z, 2], rcv.at[z, 1], me.other())

    @pl.when(me.z < 3)
    def _():
        line(me.z, 0, src.at[mine], me.z + 1).start()

    @pl.when(me.z > 0)
    def _():
        line(me.z, 1, src.at[mine], me.z - 1).start()

    yield
    for j in range(1, 4):
        z = me.order(j)
        line(z, 0, slot(z), me.z).wait_recv()

        @pl.when(me.inner == 1)
        def _():
            step = 3 - 2 * me.z if j == 1 else 2 * me.z - 3
            line(z, 0, slot(z), me.z + step).start()

        share(z).start()
        yield
    other = pl.ds(pl.multiple_of((1 - me.t) * rows, rows), rows)
    for j in range(1, 4):
        z = me.order(j)
        remote(
            dst.at[z, other], dst.at[z, other], snd.at[z, 2], rcv.at[z, 1], me.other()
        ).wait_recv()
        share(z).wait_send()
    local.wait()

    @pl.when(me.z < 3)
    def _():
        line(me.z, 0, src.at[mine], me.z + 1).wait_send()

    @pl.when(me.z > 0)
    def _():
        line(me.z, 1, src.at[mine], me.z - 1).wait_send()

    @pl.when(me.inner == 1)
    def _():
        for j in range(1, 4):
            z = me.order(j)
            line(z, 0, slot(z), me.z).wait_send()


def swap(me, src, dst, sems):
    copy = remote(src, dst, sems[0], sems[1], me.other())
    copy.start()
    yield
    copy.wait()


SWAP_SEMS = [pltpu.SemaphoreType.DMA, pltpu.SemaphoreType.DMA]


def add_rows(out, terms):
    rows = out.shape[0]
    step = 16

    @pl.loop(0, rows // step)
    def _(i):
        at = pl.ds(pl.multiple_of(i * step, step), step)
        total = terms[0][at].astype(f32)
        for term in terms[1:]:
            total += term[at].astype(f32)
        out[at] = total.astype(out.dtype)


def reduce_scratch(slots, rows, columns, dtype):
    return [
        pltpu.VMEM((slots, rows, columns), bf16),
        pltpu.VMEM((slots, rows, columns), bf16),
        pltpu.VMEM((slots, rows, columns), bf16),
        pltpu.VMEM((rows, columns), dtype),
        pltpu.SemaphoreType.DMA((slots, 3)),
        pltpu.SemaphoreType.DMA((slots, 2)),
        pltpu.SemaphoreType.DMA((3,)),
    ]


def reduce_line(me, src, out, scratch):
    here, there, landed, total, snd, rcv, end = scratch
    rows = here.shape[1]
    mine = pl.ds(pl.multiple_of(me.t * rows, rows), rows)
    theirs = pl.ds(pl.multiple_of((1 - me.t) * rows, rows), rows)

    def cross(z):
        return remote(src.at[z, theirs], there.at[z], snd.at[z, 0], rcv.at[z, 0], me.other())

    def local(z):
        return pltpu.make_async_copy(src.at[z, mine], here.at[z], snd.at[z, 1])

    def line(z):
        return remote(here.at[z], landed.at[me.z], snd.at[z, 2], rcv.at[me.z, 1], me.at(z, me.q))

    for j in (3, 2, 1, 0):
        z = me.order(j)
        cross(z).start()
        local(z).start()
    yield
    for j in (3, 2, 1, 0):
        z = me.order(j)
        local(z).wait()
        cross(z).wait_recv()
        add_rows(here.at[z], (here.at[z], there.at[z]))
        if j:
            line(z).start()
        yield
    for j in range(1, 4):
        z = me.order(j)
        remote(landed.at[z], landed.at[z], snd.at[z, 2], rcv.at[z, 1], me.at(z, me.q)).wait_recv()
    add_rows(total, [here.at[me.z]] + [landed.at[me.order(j)] for j in range(1, 4)])
    keep = pltpu.make_async_copy(total, out.at[mine], end.at[0])
    give = remote(total, out.at[mine], end.at[1], end.at[2], me.other())
    keep.start()
    give.start()
    yield
    for j in range(4):
        z = me.order(j)
        cross(z).wait_send()
        if j:
            line(z).wait_send()
    keep.wait()
    give.wait()


def reduce_window(me, reach, src, out, scratch):
    here, there, landed, total, snd, rcv, end = scratch
    rows = here.shape[1]
    slots = reach + 1
    mine = pl.ds(pl.multiple_of(me.t * rows, rows), rows)
    theirs = pl.ds(pl.multiple_of((1 - me.t) * rows, rows), rows)
    start = jnp.maximum(me.r - reach, 0)

    def cross(j):
        return remote(src.at[j, theirs], there.at[j], snd.at[j, 0], rcv.at[j, 0], me.other())

    def local(j):
        return pltpu.make_async_copy(src.at[j, mine], here.at[j], snd.at[j, 1])

    def back(k):
        j = me.r - k - start
        return remote(
            here.at[j], landed.at[k], snd.at[k, 2], rcv.at[k, 1], (me.base + me.r - k, me.t)
        )

    for j in range(slots):
        cross(j).start()
        local(j).start()
    yield
    for j in range(slots):
        local(j).wait()
        cross(j).wait_recv()
        add_rows(here.at[j], (here.at[j], there.at[j]))
    for k in range(reach, 0, -1):

        @pl.when(me.r >= k)
        def _():
            back(k).start()

    yield
    add_rows(total, [here.at[me.r - start]])
    for k in range(1, slots):

        @pl.when(me.r + k < RING)
        def _():
            remote(
                landed.at[k], landed.at[k], snd.at[k, 2], rcv.at[k, 1], me.at(me.z, me.q)
            ).wait_recv()
            add_rows(total, (total, landed.at[k]))

    keep = pltpu.make_async_copy(total, out.at[mine], end.at[0])
    give = remote(total, out.at[mine], end.at[1], end.at[2], me.other())
    keep.start()
    give.start()
    yield
    for j in range(slots):
        cross(j).wait_send()
    for k in range(1, slots):

        @pl.when(me.r >= k)
        def _():
            back(k).wait_send()

    keep.wait()
    give.wait()


PLANE_SEMS = [pltpu.SemaphoreType.DMA((4,)), pltpu.SemaphoreType.DMA((4,))]


def plane_first(me, src, got, sems):
    snd, rcv = sems
    rows = src.shape[-2] // 2
    copies = []
    lead = (slice(None),) * (len(src.shape) - 3)
    for h in range(2):
        q = (me.xq, me.yq)[h]
        for i in range(2):
            place = (q, me.dq)[i]
            n = 2 * h + i
            view = src.at[lead + (place, pl.ds(h * rows, rows))]
            copies.append(remote(view, got.at[h, i], snd.at[n], rcv.at[n], me.at(me.z, q)))
    for copy in copies:
        copy.start()
    yield
    for copy in copies:
        copy.wait()


def plane_second(me, src, got, sems):
    snd, rcv = sems
    copies = [
        remote(src.at[h], got.at[h], snd.at[h], rcv.at[h], me.at(me.z, (me.yq, me.xq)[h]))
        for h in range(2)
    ]
    for copy in copies:
        copy.start()
    yield
    for copy in copies:
        copy.wait()


LINE_SEMS = [pltpu.SemaphoreType.DMA((4,)), pltpu.SemaphoreType.DMA((4,)), pltpu.SemaphoreType.DMA]


def line_exchange(me, piece, got, sems):
    snd, rcv, loc = sems
    local = pltpu.make_async_copy(piece(me.z), got.at[me.z], loc)
    local.start()

    def send(j):
        z = me.order(j)
        return remote(piece(z), got.at[me.z], snd.at[z], rcv.at[me.z], me.at(z, me.q))

    for j in (3, 2, 1):
        send(j).start()
    yield
    for j in range(1, 4):
        z = me.order(j)
        remote(got.at[z], got.at[z], snd.at[z], rcv.at[z], me.at(z, me.q)).wait_recv()
    for j in range(1, 4):
        send(j).wait_send()
    local.wait()


def transfer(number, inputs, outputs, scratch, steps, whole=False):
    flat = [item for group in scratch for item in group]
    sizes = [len(group) for group in scratch]

    def kernel(*refs):
        ins = refs[: len(inputs)]
        outs = refs[len(inputs) : len(inputs) + len(outputs)]
        rest = refs[len(inputs) + len(outputs) :]
        groups = []
        for size in sizes:
            groups.append(rest[:size])
            rest = rest[size:]
        me = Place()
        me.greet(whole)
        run(steps(me, ins, outs, groups))

    return pl.pallas_call(
        kernel,
        out_shape=[jax.ShapeDtypeStruct(shape, dtype) for shape, dtype in outputs],
        in_specs=[ANY] * len(inputs),
        out_specs=[ANY] * len(outputs),
        scratch_shapes=flat,
        compiler_params=pltpu.CompilerParams(
            collective_id=number, has_side_effects=True, vmem_limit_bytes=48 * 2**20
        ),
    )(*inputs)


def gather_rows(me, src, dst, sems):
    half = src.shape[0] // 2
    return gather(
        me,
        src,
        lambda z, q: dst.at[4 * z + q],
        lambda z, q, h: dst.at[4 * z + q, pl.ds(h * half, half)],
        sems,
    )


def gather_pieces(me, src, dst, sems):
    half = src.shape[1] // 2
    width = dst.shape[-1]

    def piece(z):
        return src.at[:, :, pl.ds(pl.multiple_of(z * width, width), width)]

    return gather(
        me,
        piece(me.z),
        lambda z, q: dst.at[:, 4 * z + q],
        lambda z, q, h: dst.at[:, 4 * z + q, pl.ds(h * half, half)],
        sems,
        piece,
    )


def group_lists(groups):
    return [[r + RING * g for g in range(groups)] for r in range(RING)]


def grow(x, axis, groups):
    if groups == 1:
        return x
    return lax.all_gather(x, "seq", axis=axis, tiled=True, axis_index_groups=group_lists(groups))


def shrink(x, axis, groups):
    if groups == 1:
        return x
    return lax.psum_scatter(
        x, "seq", scatter_dimension=axis, tiled=True, axis_index_groups=group_lists(groups)
    )


def merge(blocks, axis, groups):
    shape = blocks.shape
    rows = shape[axis + 1]
    if groups > 1:
        blocks = blocks.reshape(shape[: axis + 1] + (groups, rows // groups) + shape[axis + 2 :])
        blocks = jnp.moveaxis(blocks, axis + 1, axis)
    return blocks.reshape(shape[:axis] + (shape[axis] * rows,) + shape[axis + 2 :])


def split(full, axis, places, groups):
    shape = full.shape
    rows = shape[axis] // (places * groups)
    blocks = full.reshape(shape[:axis] + (groups, places, rows) + shape[axis + 1 :])
    if groups > 1:
        blocks = jnp.moveaxis(blocks, axis, axis + 1)
    return blocks.reshape(shape[:axis] + (places, groups * rows) + shape[axis + 1 :])


def normalize(stream, scale_vec):
    return (
        stream * lax.rsqrt(jnp.mean(stream * stream, axis=-1, keepdims=True) + epsilon) * scale_vec
    )


def rotate(values, places, head_count, direction):
    head_size = values.shape[1] // head_count
    shaped = values.reshape(values.shape[0], head_count, head_size)
    quarter = head_size // 4
    first_part = shaped[..., :quarter]
    second = shaped[..., quarter : 2 * quarter]
    remainder = shaped[..., 2 * quarter :]
    frequency = 10000.0 ** (-jnp.arange(quarter, dtype=jnp.float32) / quarter)
    angles = places.astype(jnp.float32)[:, None] * frequency[None, :]
    cosine = jnp.cos(angles)[:, None, :]
    sine_part = direction * jnp.sin(angles)[:, None, :]
    turned = jnp.concatenate(
        [
            first_part * cosine - second * sine_part,
            second * cosine + first_part * sine_part,
            remainder,
        ],
        axis=-1,
    )
    return turned.reshape(values.shape)


def dot(a, b, ca=1, cb=0):
    return lax.dot_general(a, b, (((ca,), (cb,)), ((), ())), preferred_element_type=f32)


def body(
    inputs,
    segment_ids,
    cotangent,
    attn_gain,
    query_weight,
    key_value_weight,
    out_weight,
    out_bias,
    mlp_gain,
    gate_up_weight,
    gate_up_bias,
    down_weight,
    down_bias,
):
    seq_index = lax.axis_index("seq")
    t = lax.axis_index("tensor")
    r = seq_index % RING
    z = r // 4
    q = r % 4
    groups = lax.axis_size("seq") // RING
    tokens, width = inputs.shape
    heads = query_weight.shape[1] // HD
    hidden_half = gate_up_weight.shape[2]
    hidden_block = hidden_half // LINE
    hidden_pad = -(-hidden_block // LANES) * LANES
    reach = (W + tokens - 2) // tokens
    scale_factor = HD ** (-0.5)
    assert tokens * RING == SEQ_LEN and lax.axis_size("tensor") == 2

    kv_own = grow(key_value_weight, 0, groups)
    kv_rows = kv_own.shape[0]
    vectors = [grow(v, 0, groups) for v in (attn_gain, out_bias, mlp_gain, down_bias)]
    hidden_bias = grow(gate_up_bias, 1, groups)
    marks = jnp.stack([segment_ids // 256, segment_ids % 256]).astype(bf16)
    columns = kv_own.shape[1]

    def pad_to(x, n):
        return jnp.pad(x, ((0, 0), (0, n - x.shape[1])))

    small = jnp.concatenate(
        [
            pad_to(jnp.stack(vectors), columns),
            pad_to(hidden_bias, columns),
            pad_to(marks, columns),
            jnp.zeros((8, columns), bf16),
        ]
    )
    kv_block = jnp.concatenate([kv_own, small])
    query_own = grow(query_weight, 0, groups)
    out_own = grow(out_weight.T, 0, groups)
    ffn_own = grow(jnp.concatenate([gate_up_weight, down_weight.T[None]]), 1, groups)
    ffn_own = jnp.pad(
        ffn_own.reshape(3, -1, LINE, hidden_block),
        ((0, 0), (0, 0), (0, 0), (0, hidden_pad - hidden_block)),
    ).reshape(3, -1, LINE * hidden_pad)
    rows = query_own.shape[0]

    def first_steps(me, ins, outs, sems):
        def both():
            yield from gather_rows(me, ins[1], outs[1], sems[1])
            yield from swap(me, outs[1], outs[2], sems[2])

        return [gather_rows(me, ins[0], outs[0], sems[0]), both()]

    query_full, kv_mine, kv_theirs = transfer(
        0,
        [query_own, kv_block],
        [((RING,) + query_own.shape, bf16)] + [((RING,) + kv_block.shape, bf16)] * 2,
        [GATHER_SEMS, GATHER_SEMS, SWAP_SEMS],
        first_steps,
    )
    query_full = merge(query_full, 0, groups)
    kv_both = jnp.where(
        t == 0, jnp.stack([kv_mine, kv_theirs], 1), jnp.stack([kv_theirs, kv_mine], 1)
    )
    kv_full = merge(
        kv_both[:, :, :kv_rows]
        .reshape(RING, 2, groups, kv_rows // groups, columns)
        .swapaxes(1, 2)
        .reshape(RING, 2 * kv_rows, columns),
        0,
        groups,
    )

    def vector(row, count):
        piece = kv_both[:, :, kv_rows + row, :count].reshape(RING, 2, groups, count // groups)
        return jnp.transpose(piece, (2, 0, 1, 3)).reshape(-1).astype(f32)

    gain_one, bias_out, gain_two, bias_down = (vector(i, kv_rows) for i in range(4))
    bias_gate_up = jnp.stack([vector(4 + i, hidden_bias.shape[1]) for i in range(2)])
    bias_local = lax.dynamic_slice_in_dim(
        bias_gate_up, t * hidden_half + z * hidden_block, hidden_block, 1
    )
    bias_local = pad_to(bias_local, hidden_pad)
    all_marks = kv_both[:, 0, kv_rows + 6 : kv_rows + 8, :tokens].astype(f32)
    all_marks = (all_marks[:, 0] * 256.0 + all_marks[:, 1]).reshape(-1)

    stream = inputs.astype(f32)
    places = r * tokens + jnp.arange(tokens, dtype=jnp.int32)
    normed = normalize(stream, gain_one).astype(bf16)
    query_lin = dot(normed, query_full)
    queries = (rotate(query_lin, places, heads, 1.0) * scale_factor).astype(bf16)
    key_value = dot(normed, kv_full)
    keys_own = rotate(key_value[:, :HD], places, 1, 1.0).astype(bf16)
    values_own = key_value[:, HD:].astype(bf16)
    own_block = jnp.concatenate([keys_own, values_own], axis=1)

    def second_steps(me, ins, outs, sems):
        return [
            gather_rows(me, ins[0], outs[0], sems[0]),
            gather_rows(me, ins[1], outs[1], sems[1]),
            gather_pieces(me, ins[2], outs[2], sems[2]),
            spread(me, ins[3], outs[3], sems[3]),
        ]

    kv_all, out_full, ffn_full, cot_all = transfer(
        1,
        [own_block, out_own, ffn_own, cotangent],
        [
            ((RING,) + own_block.shape, bf16),
            ((RING,) + out_own.shape, bf16),
            ((3, RING, rows, hidden_pad), bf16),
            ((LINE,) + cotangent.shape, bf16),
        ],
        [GATHER_SEMS, GATHER_SEMS, GATHER_SEMS, SPREAD_SEMS],
        second_steps,
    )
    out_full = merge(out_full, 0, groups)
    ffn_full = merge(ffn_full, 1, groups)
    cot_all = cot_all.reshape(LINE * tokens, width)

    first_block = jnp.maximum(r - reach, 0)
    span = (reach + 1) * tokens
    window = lax.dynamic_slice_in_dim(
        kv_all.reshape(RING * tokens, 2 * HD), first_block * tokens, span, 0
    )
    window_marks = lax.dynamic_slice_in_dim(all_marks, first_block * tokens, span, 0)
    own_marks = lax.dynamic_slice_in_dim(all_marks, r * tokens, tokens, 0)
    key_places = first_block * tokens + jnp.arange(span, dtype=jnp.int32)
    key_gap = places[:, None] - key_places[None, :]
    visible = (key_gap >= 0) & (key_gap < W) & (own_marks[:, None] == window_marks[None, :])
    key_win = window[:, :HD]
    value_win = window[:, HD:]
    query_heads = queries.reshape(tokens, heads, HD)
    scores = jnp.einsum("qhd,kd->hqk", query_heads, key_win, preferred_element_type=f32)
    scores = jnp.where(visible[None], scores, -1e30)
    row_top = jnp.max(scores, axis=-1, keepdims=True)
    exponent = jnp.exp(scores - row_top)
    row_total = jnp.sum(exponent, axis=-1, keepdims=True)
    log_total = row_top + jnp.log(row_total)
    probs_low = (exponent / row_total).astype(bf16)
    mixed_low = (
        jnp.einsum("hqk,kd->qhd", probs_low, value_win, preferred_element_type=f32)
        .reshape(tokens, heads * HD)
        .astype(bf16)
    )

    def both_cores(number, part):
        (theirs,) = transfer(
            number,
            [part],
            [(part.shape, bf16)],
            [SWAP_SEMS],
            lambda me, ins, outs, sems: [swap(me, ins[0], outs[0], sems[0])],
        )
        return part.astype(f32) + theirs.astype(f32)

    branch = both_cores(2, dot(mixed_low, out_full, 1, 1).astype(bf16))
    middle = stream + branch + bias_out
    normed_two = normalize(middle, gain_two).astype(bf16)

    (normed_all,) = transfer(
        3,
        [normed_two],
        [((LINE,) + normed_two.shape, bf16)],
        [SPREAD_SEMS],
        lambda me, ins, outs, sems: [spread(me, ins[0], outs[0], sems[0])],
    )
    normed_all = normed_all.reshape(LINE * tokens, width)
    gate_pre = dot(normed_all, ffn_full[0]) + bias_local[0]
    up_pre = dot(normed_all, ffn_full[1]) + bias_local[1]
    hidden = (jax.nn.gelu(gate_pre, approximate=True) * up_pre).astype(bf16)
    mlp_part = dot(hidden, ffn_full[2], 1, 1).astype(bf16)
    hidden_grad = dot(cot_all, ffn_full[2])
    _, unit_pull = jax.vjp(
        lambda gate_in, up_in: jax.nn.gelu(gate_in, approximate=True) * up_in, gate_pre, up_pre
    )
    gate_grad, up_grad = unit_pull(hidden_grad)
    gate_low = gate_grad.astype(bf16)
    up_low = up_grad.astype(bf16)
    ffn_term = jnp.stack(
        [
            dot(normed_all, gate_low, 0, 0).astype(bf16),
            dot(normed_all, up_low, 0, 0).astype(bf16),
            dot(cot_all, hidden, 0, 0).astype(bf16),
        ]
    )
    ffn_term = split(ffn_term, 1, RING, groups).reshape(3, LINE, 4, rows, hidden_pad)
    normed_two_part = (dot(gate_low, ffn_full[0], 1, 1) + dot(up_low, ffn_full[1], 1, 1)).astype(
        bf16
    )
    hidden_bias_part = jnp.stack(
        [jnp.sum(gate_low.astype(f32), axis=0), jnp.sum(up_low.astype(f32), axis=0)]
    )
    hidden_bias_part = jnp.pad(hidden_bias_part, ((0, 14), (0, 0))).astype(bf16)

    def first_half(src, got):
        lead = src.ndim - 3
        half = rows_of(src)
        xq, yq = q + 1 - 2 * (q % 2), q + 2 - 4 * (q // 2)

        def own(place, h):
            piece = lax.dynamic_index_in_dim(src, place, lead, keepdims=False)
            return lax.slice_in_dim(piece, h * half, (h + 1) * half, axis=lead).astype(f32)

        kept = [own(q, h) + got[h, 0].astype(f32) for h in range(2)]
        passed = jnp.stack(
            [
                (own(yq, 0) + got[0, 1].astype(f32)).astype(bf16),
                (own(xq, 1) + got[1, 1].astype(f32)).astype(bf16),
            ]
        )
        return kept, passed

    def rows_of(src):
        return src.shape[-2] // 2

    def second_half(kept, got):
        return jnp.concatenate([kept[h] + got[h].astype(f32) for h in range(2)], axis=-2).astype(
            bf16
        )

    def first_shape(src):
        s = src.shape
        return (2, 2) + s[:-3] + (s[-2] // 2, s[-1])

    def third_steps(me, ins, outs, sems):
        return [
            plane_first(me, ins[1], outs[1], sems[1]),
            swap(me, ins[2], outs[2], sems[2]),
            reduce_line(me, ins[0], outs[0], sems[0]),
        ]

    normed_two_grad, ffn_got, bias_theirs = transfer(
        4,
        [normed_two_part.reshape(LINE, tokens, width), ffn_term, hidden_bias_part],
        [
            ((tokens, width), bf16),
            (first_shape(ffn_term), bf16),
            (hidden_bias_part.shape, bf16),
        ],
        [reduce_scratch(LINE, tokens // 2, width, bf16), PLANE_SEMS, SWAP_SEMS],
        third_steps,
    )
    ffn_kept, ffn_passed = first_half(ffn_term, ffn_got)
    cot_full = cotangent.astype(f32)
    _, norm_two_pull = jax.vjp(normalize, middle, gain_two)
    middle_part, gain_two_grad = norm_two_pull(normed_two_grad.astype(f32))
    middle_grad = cot_full + middle_part
    middle_low = middle_grad.astype(bf16)
    out_term = dot(middle_low, mixed_low, 0, 0).astype(bf16)
    out_term = split(out_term, 0, RING, groups).reshape(LINE, 4, rows, heads * HD)
    mixed_grad = dot(middle_low, out_full).astype(bf16).reshape(tokens, heads, HD)

    scores_again = jnp.einsum("qhd,kd->hqk", query_heads, key_win, preferred_element_type=f32)
    probs_again = jnp.where(visible[None], jnp.exp(scores_again - log_total), 0.0)
    probs_again_low = probs_again.astype(bf16)
    prob_grad = jnp.einsum("qhd,kd->hqk", mixed_grad, value_win, preferred_element_type=f32)
    value_grad = jnp.einsum("hqk,qhd->kd", probs_again_low, mixed_grad, preferred_element_type=f32)
    row_inner = jnp.sum(probs_again * prob_grad, axis=-1, keepdims=True)
    score_grad = (probs_again * (prob_grad - row_inner)).astype(bf16)
    query_grad_raw = jnp.einsum(
        "hqk,kd->qhd", score_grad, key_win, preferred_element_type=f32
    ).reshape(tokens, heads * HD)
    key_grad_raw = jnp.einsum("hqk,qhd->kd", score_grad, query_heads, preferred_element_type=f32)
    window_grad = (
        jnp.concatenate([key_grad_raw, value_grad], axis=1)
        .reshape(reach + 1, tokens, 2 * HD)
        .astype(bf16)
    )

    def fourth_steps(me, ins, outs, sems):
        return [
            reduce_window(me, reach, ins[0], outs[0], sems[0]),
            plane_second(me, ins[1], outs[1], sems[1]),
            plane_first(me, ins[2], outs[2], sems[2]),
            reduce_line(me, ins[3], outs[3], sems[3]),
        ]

    own_grad, ffn_got, out_got, mlp_out = transfer(
        5,
        [window_grad, ffn_passed, out_term, mlp_part.reshape(LINE, tokens, width)],
        [
            ((tokens, 2 * HD), f32),
            (ffn_passed.shape, bf16),
            (first_shape(out_term), bf16),
            ((tokens, width), bf16),
        ],
        [
            reduce_scratch(reach + 1, tokens // 2, 2 * HD, f32),
            PLANE_SEMS,
            PLANE_SEMS,
            reduce_scratch(LINE, tokens // 2, width, bf16),
        ],
        fourth_steps,
        whole=True,
    )
    output = (middle + mlp_out.astype(f32) + bias_down).astype(bf16)
    ffn_sum = second_half(ffn_kept, ffn_got)
    out_kept, out_passed = first_half(out_term, out_got)
    key_lin_grad = rotate(own_grad[:, :HD], places, 1, -1.0)
    kv_grad_low = jnp.concatenate([key_lin_grad, own_grad[:, HD:]], axis=1).astype(bf16)
    query_lin_grad = (rotate(query_grad_raw, places, heads, -1.0) * scale_factor).astype(bf16)
    normed_grad = both_cores(6, dot(query_lin_grad, query_full, 1, 1).astype(bf16)) + dot(
        kv_grad_low, kv_full, 1, 1
    )
    _, norm_one_pull = jax.vjp(normalize, stream, gain_one)
    stream_part, gain_one_grad = norm_one_pull(normed_grad)
    input_grad = middle_grad + stream_part
    query_term = dot(normed, query_lin_grad, 0, 0).astype(bf16)
    query_term = split(query_term, 0, RING, groups).reshape(LINE, 4, rows, heads * HD)

    def take_core(full):
        blocks = full.reshape(full.shape[0], groups, RING, 2, -1)
        mine = lax.dynamic_index_in_dim(blocks, t, 3, keepdims=False)
        return jnp.transpose(mine, (2, 0, 1, 3)).reshape(RING, full.shape[0], -1)

    kv_term = dot(normed, kv_grad_low, 0, 0)
    kv_term = jnp.moveaxis(take_core(kv_term.T), 1, 2)
    vector_terms = take_core(
        jnp.stack(
            [gain_one_grad, jnp.sum(middle_grad, axis=0), gain_two_grad, jnp.sum(cot_full, axis=0)]
        )
    )
    bias_pair = jnp.where(
        t == 0,
        jnp.stack([hidden_bias_part, bias_theirs]),
        jnp.stack([bias_theirs, hidden_bias_part]),
    )[:, :2, :hidden_block].astype(f32)
    bias_terms = lax.dynamic_update_slice_in_dim(
        jnp.zeros((2, 2, LINE, hidden_block), f32),
        jnp.swapaxes(bias_pair, 0, 1)[:, :, None],
        z,
        2,
    ).reshape(2, -1)
    bias_terms = take_core(bias_terms)

    def widen(x):
        return jnp.pad(x, ((0, 0), (0, 0), (0, columns - x.shape[2])))

    kv_term = jnp.concatenate(
        [kv_term, widen(vector_terms), widen(bias_terms), jnp.zeros((RING, 10, columns), f32)],
        axis=1,
    ).astype(bf16)
    kv_term = kv_term.reshape(LINE, 4, kv_rows + 16, columns)

    def fifth_steps(me, ins, outs, sems):
        return [
            line_exchange(me, lambda z: ins[0].at[:, z], outs[0], sems[0]),
            plane_second(me, ins[1], outs[1], sems[1]),
            plane_first(me, ins[2], outs[2], sems[2]),
            plane_first(me, ins[3], outs[3], sems[3]),
        ]

    ffn_done, out_got, query_got, kv_got = transfer(
        7,
        [ffn_sum, out_passed, query_term, kv_term],
        [
            ((LINE, 3, rows, hidden_pad), bf16),
            (out_passed.shape, bf16),
            (first_shape(query_term), bf16),
            (first_shape(kv_term), bf16),
        ],
        [LINE_SEMS, PLANE_SEMS, PLANE_SEMS, PLANE_SEMS],
        fifth_steps,
    )
    out_sum = second_half(out_kept, out_got)
    query_kept, query_passed = first_half(query_term, query_got)
    kv_kept, kv_passed = first_half(kv_term, kv_got)

    def sixth_steps(me, ins, outs, sems):
        return [
            line_exchange(me, lambda z: ins[0].at[z], outs[0], sems[0]),
            plane_second(me, ins[1], outs[1], sems[1]),
            plane_second(me, ins[2], outs[2], sems[2]),
        ]

    out_done, query_got, kv_got = transfer(
        8,
        [out_sum, query_passed, kv_passed],
        [(out_sum.shape, bf16), (query_passed.shape, bf16), (kv_passed.shape, bf16)],
        [LINE_SEMS, PLANE_SEMS, PLANE_SEMS],
        sixth_steps,
    )
    query_sum = second_half(query_kept, query_got)
    kv_sum = second_half(kv_kept, kv_got)

    def last_steps(me, ins, outs, sems):
        return [
            line_exchange(me, lambda z: ins[0].at[z], outs[0], sems[0]),
            line_exchange(me, lambda z: ins[1].at[z], outs[1], sems[1]),
        ]

    query_done, kv_done = transfer(
        9,
        [query_sum, kv_sum],
        [(query_sum.shape, bf16), (kv_sum.shape, bf16)],
        [LINE_SEMS, LINE_SEMS],
        last_steps,
    )

    ffn_grad = jnp.transpose(ffn_done[..., :hidden_block], (1, 2, 0, 3)).reshape(
        3, rows, hidden_half
    )
    ffn_grad = shrink(ffn_grad.astype(f32), 1, groups)
    out_grad = shrink(jnp.sum(out_done.astype(f32), axis=0), 0, groups).T
    query_grad = shrink(jnp.sum(query_done.astype(f32), axis=0), 0, groups)
    kv_sums = jnp.sum(kv_done.astype(f32), axis=0)
    key_value_grad = shrink(kv_sums[:kv_rows], 0, groups)
    small_grads = [shrink(kv_sums[kv_rows + i, :kv_rows], 0, groups) for i in range(4)]
    gate_up_bias_grad = shrink(
        kv_sums[kv_rows + 4 : kv_rows + 6, : hidden_bias.shape[1]], 1, groups
    )
    return (
        output,
        input_grad,
        small_grads[0],
        query_grad,
        key_value_grad,
        out_grad,
        small_grads[1],
        small_grads[2],
        ffn_grad[:2],
        gate_up_bias_grad,
        ffn_grad[2].T,
        small_grads[3],
    )


def solution(mesh):
    in_specs = (
        P("seq", None),
        P("seq"),
        P("seq", None),
        P(("seq", "tensor")),
        P("seq", "tensor"),
        P(("seq", "tensor"), None),
        P("tensor", "seq"),
        P(("seq", "tensor")),
        P(("seq", "tensor")),
        P(None, "seq", "tensor"),
        P(None, ("seq", "tensor")),
        P("tensor", "seq"),
        P(("seq", "tensor")),
    )
    out_specs = (
        P("seq", None),
        P("seq", None),
        P(("seq", "tensor")),
        P("seq", "tensor"),
        P(("seq", "tensor"), None),
        P("tensor", "seq"),
        P(("seq", "tensor")),
        P(("seq", "tensor")),
        P(None, "seq", "tensor"),
        P(None, ("seq", "tensor")),
        P("tensor", "seq"),
        P(("seq", "tensor")),
    )
    return jax.shard_map(body, mesh=mesh, in_specs=in_specs, out_specs=out_specs, check_vma=False)
```

time: 4620 us -> 1170 us (0.25)
  waiting for transfers between devices: 3960 us -> 0 us
  Pallas kernels: 0 us -> 848 us
  blocking collectives: 134 us -> 0 us
  starting transfers between devices: 96 us -> 0 us
  matrix products: 199 us -> 137 us
  local copies, waits for them, and re-layouts: 166 us -> 115 us
    unnamed x16 -> x0, waiting for transfers between devices: 1910 us -> none
    reduce_scatter x4 -> x0, waiting for transfers between devices: 1270 us -> none  [the longest x1 579 us: body(): lax.psum_scatter(down_term, 'seq', scatter_dimension=1, tiled=True)]
    pallas_call x0 -> x10, Pallas kernels: none -> 848 us  [transfer(): pl.pallas_call(kernel, out_shape=[jax.ShapeDtypeStruct(shape, dtype) for...]
    all_gather x5 -> x0, waiting for transfers between devices: 676 us -> none  [the longest x1 385 us: body(): lax.all_gather(gate_up_weight, 'seq', axis=1, tiled=True)]
    transpose x1 -> x0, local copies, waits for them, and re-layouts: 113 us -> none  [body(): jnp.einsum('td,gtf->gdf', normed_two, gate_up_low, preferred_element_type...]
    ppermute x24 -> x0, waiting for transfers between devices: 97.8 us -> none  [from_behind(): return lax.ppermute(block, axis, route)]
    ppermute x24 -> x0, starting transfers between devices: 95.2 us -> none  [from_behind(): return lax.ppermute(block, axis, route)]
    unnamed x2 -> x0, blocking collectives: 94.7 us -> none
  transfers between devices with their start and end apart: 38 -> 0, of which waited for: 26 -> 0; matrix products, arithmetic and copies ran while one was open for 8% -> 0% of each run, Pallas kernels for 0% -> 0%
where the time goes in v1:
time: 1170 us
  Pallas kernels  848 us (72%)
  matrix products  137 us (12%)
  local copies, waits for them, and re-layouts  115 us (10%)
  other arithmetic  62.6 us (5%)
    pallas_call x10, Pallas kernels, transfer(): pl.pallas_call(kernel, out_shape=[jax.ShapeDtypeStruct(shape, dtype) for...  848 us
    dot_general x18, matrix products, dot(): lax.dot_general(a, b, (((ca,), (cb,)), ((), ())), preferred_element_type=...  104 us
    unnamed x160, local copies, waits for them, and re-layouts  28.1 us

profile of v1, /device:TPU:0, one launch (start us, length us, event | category | flops | bytes accessed | tf_op | source)
XLA Modules:
  0.0 1165.6 jit_solution(2657316288389895832)
XLA Ops:
  4.7 76.2 %shard_map.220 = (bf16[16,160,1280]{2,1,0:T(8,128)(2,1)}, bf16[16,96,512]{2,1,0:T(8,128)(2,1)S(1)}, bf16[16,96,512]{2,1,0:T(8,128)(2,1)S(1)}) custom-call(bf16[160,1280]{1,0:T(8,128)(2,1)S(1)} %copy-done.4, bf16[96,512]{1,0:T(8,128)(2,1)S(1)} %concatenate.65.refs_1_), custom_call_target="tpu_custom_call" | custom-call | tf_op jit(solution)/shard_map/pallas_call | solution.py:461
  87.3 9.6 copy.88
  113.1 7.2 concatenate.68
  125.3 8.9 reshape.509.refs_2_
  136.4 236.9 %shard_map.221 = (bf16[16,256,512]{2,1,0:T(8,128)(2,1)}, bf16[16,160,1280]{2,1,0:T(8,128)(2,1)}, bf16[3,16,160,1024]{3,2,1,0:T(8,128)(2,1)}, bf16[4,256,2560]{2,1,0:T(8,128)(2,1)}) custom-call(bf16[256,512]{1,0:T(8,128)(2,1)S(1)} %pad_maximum_fusion.10.refs_0_, bf16[160,1280]{1,0:T(8,128)(2,1)S(1)} %bitcast.318, bf16[3,160,4096]{2,1,0:T(8,128)(2,1)S(1)} %copy-done, ...), custom_call_target="tpu_custom_call" | custom-call | tf_op jit(solution)/shard_map/pallas_call | solution.py:461
  382.9 7.8 fusion.59
  404.8 51.3 %shard_map.223 = bf16[4,256,2560]{2,1,0:T(8,128)(2,1)} custom-call(bf16[256,2560]{1,0:T(8,128)(2,1)S(1)} %multiply_convert_fusion.2.refs_0_), custom_call_target="tpu_custom_call" | custom-call | tf_op jit(solution)/shard_map/pallas_call | solution.py:461
  456.1 11.0 fusion.140
  469.4 7.5 fusion.142
  478.4 12.5 %multiply_convert_fusion = (bf16[1024,1024]{1,0:T(8,128)(2,1)}, f32[1024,1024]{1,0:T(8,128)}) fusion(f32[1024]{0:T(1024)S(1)} %bitcast.381, f32[1024,1024]{1,0:T(8,128)} %fusion.142, f32[1024]{0:T(1024)S(1)} %bitcast.383, bf16[1024,2560]{1,0:T(8,128)(2,1)} %bitcast.337, bf16[2560,1024]{1,0:T(8,128)(2,1)} %bitcast.349), kind=kOutput, calls=%fused_computation.45 | convolution fusion | flops 5381292032 | bytes 20979712 | tf_op jit(solution)/shard_map/dot_general | solution.py:566
  490.9 13.3 %fusion.138 = (bf16[1024]{0:T(1024)(128)(2,1)S(1)}, bf16[1024,1024]{1,0:T(8,128)(2,1)S(1)}, bf16[1024]{0:T(1024)(128)(2,1)S(1)}, bf16[1024,1024]{1,0:T(8,128)(2,1)}) fusion(f32[1024,1024]{1,0:T(8,128)S(1)} %copy-done.54, f32[1024]{0:T(1024)S(1)} %bitcast.384, f32[1024,1024]{1,0:T(8,128)} %get-tuple-element.134, f32[1024]{0:T(1024)S(1)} %bitcast.382, ...), kind=kOutput, calls=%fused_computation.287 | convolution fusion | flops 5398067200 | bytes 23080960 | tf_op jit(solution)/shard_map/dot_general | solution.py:566
  504.3 10.1 fusion.143
  514.4 10.2 add_convert_fusion
  524.6 7.9 convolution_convert_fusion.3
  544.5 6.9 pad_maximum_fusion.refs_1_
  551.5 135.7 %shard_map.224 = (bf16[256,2560]{1,0:T(8,128)(2,1)S(1)}, bf16[2,2,3,4,80,1024]{5,4,3,2,1,0:T(8,128)(2,1)}, bf16[16,1024]{1,0:T(8,128)(2,1)S(1)}) custom-call(bf16[4,256,2560]{2,1,0:T(8,128)(2,1)} %bitcast.336, bf16[3,4,4,160,1024]{4,3,2,1,0:T(8,128)(2,1)} %pad_maximum_fusion.refs_1_, bf16[16,1024]{1,0:T(8,128)(2,1)S(1)} %get-tuple-element.123.refs_2_), custom_call_target="tpu_custom_call" | custom-call | tf_op jit(solution)/shard_map/pallas_call | solution.py:461
  719.5 9.5 dynamic-slice_bitcast_fusion
  742.2 7.4 convolution_convert_fusion.2
  749.6 149.3 %shard_map.225 = (f32[256,512]{1,0:T(8,128)S(1)}, bf16[2,3,4,80,1024]{4,3,2,1,0:T(8,128)(2,1)}, bf16[2,2,4,80,1280]{4,3,2,1,0:T(8,128)(2,1)}, bf16[256,2560]{1,0:T(8,128)(2,1)S(1)}) custom-call(bf16[9,256,512]{2,1,0:T(8,128)(2,1)S(1)} %bitcast.315, bf16[2,3,4,80,1024]{4,3,2,1,0:T(8,128)(2,1)} %pad_maximum_fusion.1.refs_1_, ...), custom_call_target="tpu_custom_call" | custom-call | tf_op jit(solution)/shard_map/pallas_call | solution.py:461
  911.7 21.5 %shard_map.226 = bf16[256,2560]{1,0:T(8,128)(2,1)S(1)} custom-call(bf16[256,2560]{1,0:T(8,128)(2,1)S(1)} %convolution_convert_fusion.6.refs_0_), custom_call_target="tpu_custom_call" | custom-call | tf_op jit(solution)/shard_map/pallas_call | solution.py:461
  957.7 68.9 %shard_map.227 = (bf16[4,3,160,1024]{3,2,1,0:T(8,128)(2,1)}, bf16[2,4,80,1280]{3,2,1,0:T(8,128)(2,1)S(1)}, bf16[2,2,4,80,1280]{4,3,2,1,0:T(8,128)(2,1)}, bf16[2,2,4,48,512]{4,3,2,1,0:T(8,128)(2,1)S(1)}) custom-call(bf16[3,4,160,1024]{3,2,1,0:T(8,128)(2,1)} %pad_maximum_fusion.2.refs_0_, bf16[2,4,80,1280]{3,2,1,0:T(8,128)(2,1)S(1)} %pad_maximum_fusion.4.refs_1_, ...), custom_call_target="tpu_custom_call" | custom-call | tf_op jit(solution)/shard_map/pallas_call | solution.py:461
  1031.7 51.4 %shard_map.228 = (bf16[4,160,1280]{2,1,0:T(8,128)(2,1)S(1)}, bf16[2,4,80,1280]{3,2,1,0:T(8,128)(2,1)S(1)}, bf16[2,4,48,512]{3,2,1,0:T(8,128)(2,1)S(1)}) custom-call(bf16[4,160,1280]{2,1,0:T(8,128)(2,1)S(1)} %pad_maximum_fusion.5.refs_0_, bf16[2,4,80,1280]{3,2,1,0:T(8,128)(2,1)} %pad_maximum_fusion.6.refs_1_, ...), custom_call_target="tpu_custom_call" | custom-call | tf_op jit(solution)/shard_map/pallas_call | solution.py:461
  1084.0 52.5 %shard_map.229 = (bf16[4,160,1280]{2,1,0:T(8,128)(2,1)S(1)}, bf16[4,96,512]{2,1,0:T(8,128)(2,1)S(1)}) custom-call(bf16[4,160,1280]{2,1,0:T(8,128)(2,1)S(1)} %pad_maximum_fusion.7.refs_0_, bf16[4,96,512]{2,1,0:T(8,128)(2,1)S(1)} %pad_maximum_fusion.9.refs_1_), custom_call_target="tpu_custom_call" | custom-call | tf_op jit(solution)/shard_map/pallas_call | solution.py:461
  1150.4 7.4 slice.343
  (311 shorter events, 182.3 us)
Async XLA Ops:
  84.9 23.7 %copy-start.48 = (f32[256]{0:T(256)}, f32[256]{0:T(256)S(1)}, u32[]{:S(2)}) copy-start(f32[256]{0:T(256)S(1)} %get-tuple-element.139) | copy-start | bytes 3076
  136.4 236.9 %copy-start.14 = (pred[256,2304]{0,1:T(8,128)(4,1)S(1)}, pred[256,2304]{0,1:T(8,128)(4,1)}, u32[]{:S(2)}) copy-start(pred[256,2304]{0,1:T(8,128)(4,1)} %fusion.48) | copy-start | bytes 1769476
  136.4 236.9 %copy-start.32 = (f32[256,5,128]{0,2,1:T(8,128)S(1)}, f32[256,5,128]{0,2,1:T(8,128)}, u32[]{:S(2)}) copy-start(f32[256,5,128]{0,2,1:T(8,128)} %slice.359) | copy-start | bytes 1966084
  136.4 236.9 %copy-start.38 = (f32[256,5,64]{0,2,1:T(8,128)S(1)}, f32[256,5,64]{0,2,1:T(8,128)}, u32[]{:S(2)}) copy-start(f32[256,5,64]{0,2,1:T(8,128)} %get-tuple-element.109) | copy-start | bytes 983044
  136.4 236.9 %copy-start.40 = (f32[256,5,64]{0,2,1:T(8,128)S(1)}, f32[256,5,64]{0,2,1:T(8,128)}, u32[]{:S(2)}) copy-start(f32[256,5,64]{0,2,1:T(8,128)} %get-tuple-element.110) | copy-start | bytes 983044
  456.1 13.3 %copy-start.20 = (bf16[4,256,2560]{2,1,0:T(8,128)(2,1)S(1)}, bf16[4,256,2560]{2,1,0:T(8,128)(2,1)}, u32[]{:S(2)}) copy-start(bf16[4,256,2560]{2,1,0:T(8,128)(2,1)} %shard_map.223) | copy-start | bytes 15728644
  478.4 25.9 %slice-start.17 = ((s8[5242880]{0:T(1024)(128)(4,1)}), s8[4194304]{0:T(1024)(128)(4,1)S(1)}, s32[]{:S(2)}) async-start(s8[5242880]{0:T(1024)(128)(4,1)} %bitcast.354), calls=%async_computation.17 | async-start | bytes 8388608
  478.4 36.0 %slice-start.15 = ((s8[5242880]{0:T(1024)(128)(4,1)}), s8[4194304]{0:T(1024)(128)(4,1)S(1)}, s32[]{:S(2)}) async-start(s8[5242880]{0:T(1024)(128)(4,1)} %bitcast.350), calls=%async_computation.15 | async-start | bytes 8388608
  490.9 13.4 %slice-start.18 = ((s8[5242880]{0:T(1024)(128)(4,1)}), s8[1048576]{0:T(1024)(128)(4,1)S(1)}, s32[]{:S(2)}) async-start(s8[5242880]{0:T(1024)(128)(4,1)} %bitcast.354), calls=%async_computation.18 | async-start | bytes 2097152
  490.9 23.5 %slice-start.16 = ((s8[5242880]{0:T(1024)(128)(4,1)}), s8[1048576]{0:T(1024)(128)(4,1)S(1)}, s32[]{:S(2)}) async-start(s8[5242880]{0:T(1024)(128)(4,1)} %bitcast.350), calls=%async_computation.16 | async-start | bytes 2097152
  504.3 20.3 %slice-start.21 = ((s8[5242880]{0:T(1024)(128)(4,1)}), s8[4194304]{0:T(1024)(128)(4,1)S(1)}, s32[]{:S(2)}) async-start(s8[5242880]{0:T(1024)(128)(4,1)} %bitcast.394), calls=%async_computation.21 | async-start | bytes 8388608
  514.4 18.1 %slice-start.11 = ((s8[5242880]{0:T(1024)(128)(4,1)}), s8[1048576]{0:T(1024)(128)(4,1)S(1)}, s32[]{:S(2)}) async-start(s8[5242880]{0:T(1024)(128)(4,1)} %bitcast.339), calls=%async_computation.11 | async-start | bytes 2097152
  544.5 146.0 %slice-start.19 = ((s8[6553600]{0:T(1024)(128)(4,1)}), s8[2359296]{0:T(1024)(128)(4,1)S(1)}, s32[]{:S(2)}) async-start(s8[6553600]{0:T(1024)(128)(4,1)} %bitcast.390), calls=%async_computation.19 | async-start | bytes 4718592
  551.4 135.7 %copy-start.7 = (f32[256,2560]{1,0:T(8,128)S(1)}, f32[256,2560]{1,0:T(8,128)}, u32[]{:S(2)}) copy-start(f32[256,2560]{1,0:T(8,128)} %get-tuple-element.69) | copy-start | bytes 7864324
  551.5 139.1 %slice-start.20 = ((s8[6553600]{0:T(1024)(128)(4,1)}), s8[4194304]{0:T(1024)(128)(4,1)S(1)}, s32[]{:S(2)}) async-start(s8[6553600]{0:T(1024)(128)(4,1)} %bitcast.390), calls=%async_computation.20 | async-start | bytes 8388608
  692.7 13.1 %slice-start = ((s8[11796480]{0:T(1024)(128)(4,1)}), s8[4194304]{0:T(1024)(128)(4,1)S(1)}, s32[]{:S(2)}) async-start(s8[11796480]{0:T(1024)(128)(4,1)} %bitcast.320), calls=%async_computation | async-start | bytes 8388608
  749.6 150.4 %copy-start.45 = (f32[16,2,1,80]{3,2,0,1:T(1,128)S(1)}, f32[16,2,1,80]{3,2,0,1:T(1,128)}, u32[]{:S(2)}) copy-start(f32[16,2,1,80]{3,2,0,1:T(1,128)} %get-tuple-element.96) | copy-start | bytes 30724
  909.7 23.5 %copy-start.9 = (bf16[256,2560]{1,0:T(8,128)(2,1)S(1)}, bf16[256,2560]{1,0:T(8,128)(2,1)}, u32[]{:S(2)}) copy-start(bf16[256,2560]{1,0:T(8,128)(2,1)} %param.13) | copy-start | bytes 3932164
  909.7 23.5 %copy-start.31 = (bf16[16,2,80,512]{3,2,1,0:T(8,128)(2,1)S(1)}, bf16[16,2,80,512]{3,2,1,0:T(8,128)(2,1)}, u32[]{:S(2)}) copy-start(bf16[16,2,80,512]{3,2,1,0:T(8,128)(2,1)} %copy-done.30) | copy-start | bytes 7864324
  909.7 23.5 %copy-start.43 = (f32[2560]{0:T(1024)S(1)}, f32[2560]{0:T(1024)}, u32[]{:S(2)}) copy-start(f32[2560]{0:T(1024)} %copy-done.42) | copy-start | bytes 30724
  909.7 23.5 %copy-start.47 = (f32[256]{0:T(256)S(1)}, f32[256]{0:T(256)}, u32[]{:S(2)}) copy-start(f32[256]{0:T(256)} %copy-done.46) | copy-start | bytes 3076
  957.7 69.0 %copy-start.19 = (bf16[4,160,1280]{2,1,0:T(8,128)(2,1)S(1)}, bf16[4,160,1280]{2,1,0:T(8,128)(2,1)}, u32[]{:S(2)}) copy-start(bf16[4,160,1280]{2,1,0:T(8,128)(2,1)} %get-tuple-element.90) | copy-start | bytes 4915204
  957.7 69.0 %copy-start.28 = (bf16[2,2,4,80,1280]{4,3,2,1,0:T(8,128)(2,1)S(1)}, bf16[2,2,4,80,1280]{4,3,2,1,0:T(8,128)(2,1)}, u32[]{:S(2)}) copy-start(bf16[2,2,4,80,1280]{4,3,2,1,0:T(8,128)(2,1)} %get-tuple-element.47) | copy-start | bytes 9830404
  1031.5 51.6 %copy-start.18 = (bf16[4,160,1280]{2,1,0:T(8,128)(2,1)S(1)}, bf16[4,160,1280]{2,1,0:T(8,128)(2,1)}, u32[]{:S(2)}) copy-start(bf16[4,160,1280]{2,1,0:T(8,128)(2,1)} %get-tuple-element.86) | copy-start | bytes 4915204
  (56 other events, 275.0 us)

commit v2 on v1

--- a/solution.py
+++ b/solution.py
@@ -67,13 +67,14 @@
 
 
 def run(steps):
-    steps = list(steps)
+    steps, ending = list(steps), []
     while steps:
         for step in list(steps):
-            try:
-                next(step)
-            except StopIteration:
+            if next(step, True):
                 steps.remove(step)
+                ending.append(step)
+    for step in ending:
+        next(step, None)
 
 
 GATHER_SEMS = [
@@ -141,6 +142,7 @@
             ).wait_recv()
             corner(z, k).start()
         yield
+    yield True
     for j in range(4):
         z = me.order(j)
         for k in range(2):
@@ -217,6 +219,7 @@
 
         share(z).start()
         yield
+    yield True
     other = pl.ds(pl.multiple_of((1 - me.t) * rows, rows), rows)
     for j in range(1, 4):
         z = me.order(j)
@@ -244,7 +247,7 @@
 def swap(me, src, dst, sems):
     copy = remote(src, dst, sems[0], sems[1], me.other())
     copy.start()
-    yield
+    yield True
     copy.wait()
 
 
@@ -276,48 +279,92 @@
     ]
 
 
+def chain_scratch(rows, columns):
+    return [
+        pltpu.VMEM((LINE, rows, columns), bf16),
+        pltpu.VMEM((LINE, rows, columns), bf16),
+        pltpu.VMEM((2, 3, rows, columns), bf16),
+        pltpu.SemaphoreType.DMA((LINE, 2)),
+        pltpu.SemaphoreType.DMA((LINE,)),
+        pltpu.SemaphoreType.DMA((2, 3)),
+        pltpu.SemaphoreType.DMA((2, 3)),
+        pltpu.SemaphoreType.DMA((3,)),
+    ]
+
+
 def reduce_line(me, src, out, scratch):
-    here, there, landed, total, snd, rcv, end = scratch
+    here, there, landed, snd, rcv, line_snd, line_rcv, end = scratch
     rows = here.shape[1]
     mine = pl.ds(pl.multiple_of(me.t * rows, rows), rows)
     theirs = pl.ds(pl.multiple_of((1 - me.t) * rows, rows), rows)
+    order = (3, 0, 2, 1)
 
     def cross(z):
-        return remote(src.at[z, theirs], there.at[z], snd.at[z, 0], rcv.at[z, 0], me.other())
+        return remote(src.at[z, theirs], there.at[z], snd.at[z, 0], rcv.at[z], me.other())
 
     def local(z):
         return pltpu.make_async_copy(src.at[z, mine], here.at[z], snd.at[z, 1])
 
-    def line(z):
-        return remote(here.at[z], landed.at[me.z], snd.at[z, 2], rcv.at[me.z, 1], me.at(z, me.q))
-
-    for j in (3, 2, 1, 0):
-        z = me.order(j)
+    def send(way, k, source):
+        to = me.z + 1 - 2 * way
+        return remote(
+            source, landed.at[way, k], line_snd.at[way, k], line_rcv.at[way, k], me.at(to, me.q)
+        )
+
+    for z in order:
         cross(z).start()
         local(z).start()
     yield
-    for j in (3, 2, 1, 0):
-        z = me.order(j)
+    for z in order:
         local(z).wait()
         cross(z).wait_recv()
         add_rows(here.at[z], (here.at[z], there.at[z]))
-        if j:
-            line(z).start()
+    for k in range(3):
+        for way in range(2):
+            w = me.z if way == 0 else 3 - me.z
+            block = 3 + w - k if way == 0 else k - w
+
+            @pl.when(w <= k)
+            def _():
+                if k:
+
+                    @pl.when(w < k)
+                    def _():
+                        send(way, k - 1, here.at[0]).wait_send()
+
+                @pl.when(w == 0)
+                def _():
+                    send(way, k, here.at[block]).start()
+
+                if k:
+
+                    @pl.when(w > 0)
+                    def _():
+                        partial = landed.at[way, k - 1]
+                        send(way, k - 1, partial).wait_recv()
+                        add_rows(partial, (partial, here.at[block]))
+                        send(way, k, partial).start()
+
         yield
-    for j in range(1, 4):
-        z = me.order(j)
-        remote(landed.at[z], landed.at[z], snd.at[z, 2], rcv.at[z, 1], me.at(z, me.q)).wait_recv()
-    add_rows(total, [here.at[me.z]] + [landed.at[me.order(j)] for j in range(1, 4)])
-    keep = pltpu.make_async_copy(total, out.at[mine], end.at[0])
-    give = remote(total, out.at[mine], end.at[1], end.at[2], me.other())
+    for way in range(2):
+        w = me.z if way == 0 else 3 - me.z
+
+        @pl.when(w > 0)
+        def _():
+            send(way, 2, landed.at[way, 2]).wait_recv()
+            add_rows(here.at[me.z], (here.at[me.z], landed.at[way, 2]))
+
+        @pl.when(w < 3)
+        def _():
+            send(way, 2, here.at[0]).wait_send()
+
+    keep = pltpu.make_async_copy(here.at[me.z], out.at[mine], end.at[0])
+    give = remote(here.at[me.z], out.at[mine], end.at[1], end.at[2], me.other())
     keep.start()
     give.start()
-    yield
-    for j in range(4):
-        z = me.order(j)
+    yield True
+    for z in range(LINE):
         cross(z).wait_send()
-        if j:
-            line(z).wait_send()
     keep.wait()
     give.wait()
 
@@ -371,7 +418,7 @@
     give = remote(total, out.at[mine], end.at[1], end.at[2], me.other())
     keep.start()
     give.start()
-    yield
+    yield True
     for j in range(slots):
         cross(j).wait_send()
     for k in range(1, slots):
@@ -401,9 +448,84 @@
             copies.append(remote(view, got.at[h, i], snd.at[n], rcv.at[n], me.at(me.z, q)))
     for copy in copies:
         copy.start()
-    yield
+    yield True
     for copy in copies:
         copy.wait()
+
+
+def plane_sums_scratch(shape):
+    parts, line, _, rows, columns = shape
+    block = (parts, 2, 2, line, rows // 2, columns)
+    return [
+        pltpu.VMEM(block, bf16),
+        pltpu.VMEM(block, bf16),
+        pltpu.SemaphoreType.DMA((parts, 4)),
+        pltpu.SemaphoreType.DMA((parts, 4)),
+        pltpu.SemaphoreType.DMA((parts, 4)),
+        pltpu.SemaphoreType.DMA((parts, 4)),
+    ]
+
+
+def plane_sums(me, order, src, kept, passed, scratch):
+    here, there, loc, snd, rcv, end = scratch
+    half = src.shape[3] // 2
+
+    def view(part, place, h):
+        return src.at[part, :, place, pl.ds(h * half, half)]
+
+    def sends(part):
+        for h in range(2):
+            q = (me.xq, me.yq)[h]
+            for i in range(2):
+                n = 2 * h + i
+                yield remote(
+                    view(part, (q, me.dq)[i], h),
+                    there.at[part, h, i],
+                    snd.at[part, n],
+                    rcv.at[part, n],
+                    me.at(me.z, q),
+                )
+
+    def loads(part):
+        for h in range(2):
+            for i in range(2):
+                place = (me.q, (me.yq, me.xq)[h])[i]
+                yield pltpu.make_async_copy(
+                    view(part, place, h), here.at[part, h, i], loc.at[part, 2 * h + i]
+                )
+
+    def stores(part):
+        for h in range(2):
+            for i in range(2):
+                yield pltpu.make_async_copy(
+                    here.at[part, h, i], (kept, passed)[i].at[h, part], end.at[part, 2 * h + i]
+                )
+
+    for part in order:
+        for copy in sends(part):
+            copy.start()
+        for copy in loads(part):
+            copy.start()
+    yield
+    for part in order:
+        yield
+        for copy in loads(part):
+            copy.wait()
+        for copy in sends(part):
+            copy.wait_recv()
+        for h in range(2):
+            for i in range(2):
+                for z in range(here.shape[3]):
+                    block = here.at[part, h, i, z]
+                    add_rows(block, (block, there.at[part, h, i, z]))
+        for copy in stores(part):
+            copy.start()
+    yield True
+    for part in order:
+        for copy in sends(part):
+            copy.wait_send()
+        for copy in stores(part):
+            copy.wait()
 
 
 def plane_second(me, src, got, sems):
@@ -414,7 +536,7 @@
     ]
     for copy in copies:
         copy.start()
-    yield
+    yield True
     for copy in copies:
         copy.wait()
 
@@ -433,7 +555,7 @@
 
     for j in (3, 2, 1):
         send(j).start()
-    yield
+    yield True
     for j in range(1, 4):
         z = me.order(j)
         remote(got.at[z], got.at[z], snd.at[z], rcv.at[z], me.at(z, me.q)).wait_recv()
@@ -626,7 +748,8 @@
 
     def first_steps(me, ins, outs, sems):
         def both():
-            yield from gather_rows(me, ins[1], outs[1], sems[1])
+            for _ in gather_rows(me, ins[1], outs[1], sems[1]):
+                yield
             yield from swap(me, outs[1], outs[2], sems[2])
 
         return [gather_rows(me, ins[0], outs[0], sems[0]), both()]
@@ -795,33 +918,58 @@
         return src.shape[-2] // 2
 
     def second_half(kept, got):
-        return jnp.concatenate([kept[h] + got[h].astype(f32) for h in range(2)], axis=-2).astype(
-            bf16
-        )
+        return jnp.concatenate(
+            [kept[h].astype(f32) + got[h].astype(f32) for h in range(2)], axis=-2
+        ).astype(bf16)
 
     def first_shape(src):
         s = src.shape
         return (2, 2) + s[:-3] + (s[-2] // 2, s[-1])
 
     def third_steps(me, ins, outs, sems):
-        return [
-            plane_first(me, ins[1], outs[1], sems[1]),
-            swap(me, ins[2], outs[2], sems[2]),
-            reduce_line(me, ins[0], outs[0], sems[0]),
-        ]
-
-    normed_two_grad, ffn_got, bias_theirs = transfer(
+        yield from ()
+        one = reduce_line(me, ins[0], outs[0], sems[0])
+        two = reduce_line(me, ins[1], outs[1], sems[1])
+        three = plane_sums(me, (2, 0, 1), ins[2], outs[2], outs[3], sems[2])
+        next(one)
+        next(three)
+        ends = [swap(me, ins[3], outs[4], sems[3])]
+        next(ends[0])
+        next(two)
+        for _ in range(4):
+            next(one)
+        next(three)
+        for _ in range(3):
+            next(two)
+            next(three)
+        next(two)
+        for step in [one, two, three] + ends:
+            next(step, None)
+
+    kept_shape = (2, 3, LINE, rows // 2, hidden_pad)
+    normed_two_grad, mlp_out, ffn_kept, ffn_passed, bias_theirs = transfer(
         4,
-        [normed_two_part.reshape(LINE, tokens, width), ffn_term, hidden_bias_part],
+        [
+            normed_two_part.reshape(LINE, tokens, width),
+            mlp_part.reshape(LINE, tokens, width),
+            ffn_term,
+            hidden_bias_part,
+        ],
         [
             ((tokens, width), bf16),
-            (first_shape(ffn_term), bf16),
+            ((tokens, width), bf16),
+            (kept_shape, bf16),
+            (kept_shape, bf16),
             (hidden_bias_part.shape, bf16),
         ],
-        [reduce_scratch(LINE, tokens // 2, width, bf16), PLANE_SEMS, SWAP_SEMS],
+        [
+            chain_scratch(tokens // 2, width),
+            chain_scratch(tokens // 2, width),
+            plane_sums_scratch(ffn_term.shape),
+            SWAP_SEMS,
+        ],
         third_steps,
     )
-    ffn_kept, ffn_passed = first_half(ffn_term, ffn_got)
     cot_full = cotangent.astype(f32)
     _, norm_two_pull = jax.vjp(normalize, middle, gain_two)
     middle_part, gain_two_grad = norm_two_pull(normed_two_grad.astype(f32))
@@ -853,23 +1001,20 @@
             reduce_window(me, reach, ins[0], outs[0], sems[0]),
             plane_second(me, ins[1], outs[1], sems[1]),
             plane_first(me, ins[2], outs[2], sems[2]),
-            reduce_line(me, ins[3], outs[3], sems[3]),
         ]
 
-    own_grad, ffn_got, out_got, mlp_out = transfer(
+    own_grad, ffn_got, out_got = transfer(
         5,
-        [window_grad, ffn_passed, out_term, mlp_part.reshape(LINE, tokens, width)],
+        [window_grad, ffn_passed, out_term],
         [
             ((tokens, 2 * HD), f32),
             (ffn_passed.shape, bf16),
             (first_shape(out_term), bf16),
-            ((tokens, width), bf16),
         ],
         [
             reduce_scratch(reach + 1, tokens // 2, 2 * HD, f32),
             PLANE_SEMS,
             PLANE_SEMS,
-            reduce_scratch(LINE, tokens // 2, width, bf16),
         ],
         fourth_steps,
         whole=True,

time: 1170 us -> 1050 us (0.90)
  Pallas kernels: 848 us -> 745 us
  other arithmetic: 62.6 us -> 50.2 us
    pallas_call x10, Pallas kernels: 848 us -> 745 us  [transfer(): pl.pallas_call(kernel, out_shape=[jax.ShapeDtypeStruct(shape, dtype) for...]
    unnamed x160 -> x148, local copies, waits for them, and re-layouts: 28.1 us -> 23.4 us
where the time goes in v2:
time: 1050 us; the launch traced here: 1040 us
  Pallas kernels  745 us (71%)
  matrix products  140 us (13%)
  local copies, waits for them, and re-layouts  106 us (10%)
  other arithmetic  50.2 us (5%)
    pallas_call x10, Pallas kernels, transfer(): pl.pallas_call(kernel, out_shape=[jax.ShapeDtypeStruct(shape, dtype) for...  745 us
    dot_general x18, matrix products, dot(): lax.dot_general(a, b, (((ca,), (cb,)), ((), ())), preferred_element_type=...  108 us
    unnamed x148, local copies, waits for them, and re-layouts  23.4 us

profile of v2, /device:TPU:0, one launch (start us, length us, event | category | flops | bytes accessed | tf_op | source)
XLA Modules:
  0.0 1043.1 jit_solution(2151705596544900971)
XLA Ops:
  4.7 76.2 %shard_map.220 = (bf16[16,160,1280]{2,1,0:T(8,128)(2,1)}, bf16[16,96,512]{2,1,0:T(8,128)(2,1)S(1)}, bf16[16,96,512]{2,1,0:T(8,128)(2,1)S(1)}) custom-call(bf16[160,1280]{1,0:T(8,128)(2,1)S(1)} %copy-done.8, bf16[96,512]{1,0:T(8,128)(2,1)S(1)} %concatenate.65.refs_1_), custom_call_target="tpu_custom_call" | custom-call | tf_op jit(solution)/shard_map/pallas_call | solution.py:583
  86.4 9.5 copy.88
  112.2 7.2 concatenate.68
  124.4 8.9 reshape.505.refs_2_
  135.5 236.8 %shard_map.221 = (bf16[16,256,512]{2,1,0:T(8,128)(2,1)}, bf16[16,160,1280]{2,1,0:T(8,128)(2,1)}, bf16[3,16,160,1024]{3,2,1,0:T(8,128)(2,1)}, bf16[4,256,2560]{2,1,0:T(8,128)(2,1)}) custom-call(bf16[256,512]{1,0:T(8,128)(2,1)S(1)} %pad_maximum_fusion.9.refs_0_, bf16[160,1280]{1,0:T(8,128)(2,1)S(1)} %bitcast.294, bf16[3,160,4096]{2,1,0:T(8,128)(2,1)S(1)} %copy-done, ...), custom_call_target="tpu_custom_call" | custom-call | tf_op jit(solution)/shard_map/pallas_call | solution.py:583
  382.0 7.9 fusion.55
  398.2 51.3 %shard_map.223 = bf16[4,256,2560]{2,1,0:T(8,128)(2,1)} custom-call(bf16[256,2560]{1,0:T(8,128)(2,1)S(1)} %multiply_convert_fusion.2.refs_0_), custom_call_target="tpu_custom_call" | custom-call | tf_op jit(solution)/shard_map/pallas_call | solution.py:583
  449.5 11.4 %fusion.136 = (bf16[1,16,160,1024]{3,2,1,0:T(8,128)(2,1)}, bf16[1,16,160,1024]{3,2,1,0:T(8,128)(2,1)S(1)}, bf16[1,16,160,1024]{3,2,1,0:T(8,128)(2,1)}) fusion(bf16[3,16,160,1024]{3,2,1,0:T(8,128)(2,1)} %get-tuple-element.42), kind=kLoop, calls=%fused_computation.276 | loop fusion | bytes 31457280 | tf_op jit(solution)/shard_map/slice | solution.py:873
  463.3 7.1 fusion.138
  471.8 12.5 %multiply_convert_fusion = (bf16[1024,1024]{1,0:T(8,128)(2,1)}, f32[1024,1024]{1,0:T(8,128)}) fusion(f32[1024]{0:T(1024)S(1)} %bitcast.355, f32[1024,1024]{1,0:T(8,128)} %fusion.138, f32[1024]{0:T(1024)S(1)} %bitcast.357, bf16[1024,2560]{1,0:T(8,128)(2,1)} %bitcast.310, bf16[2560,1024]{1,0:T(8,128)(2,1)} %bitcast.323), kind=kOutput, calls=%fused_computation.45 | convolution fusion | flops 5381292032 | bytes 20979712 | tf_op jit(solution)/shard_map/dot_general | solution.py:688
  484.3 12.3 %fusion.134 = (bf16[1024]{0:T(1024)(128)(2,1)S(1)}, bf16[1024,1024]{1,0:T(8,128)(2,1)S(1)}, bf16[1024]{0:T(1024)(128)(2,1)S(1)}, bf16[1024,1024]{1,0:T(8,128)(2,1)S(1)}) fusion(f32[1024,1024]{1,0:T(8,128)S(1)} %copy-done.53, f32[1024]{0:T(1024)S(1)} %bitcast.358, f32[1024,1024]{1,0:T(8,128)} %get-tuple-element.132, f32[1024]{0:T(1024)S(1)} %bitcast.356, ...), kind=kOutput, calls=%fused_computation.275 | convolution fusion | flops 5398067200 | bytes 23080960 | tf_op jit(solution)/shard_map/dot_general | solution.py:688
  496.7 8.2 fusion.139
  504.9 10.0 add_convert_fusion
  514.9 9.3 convolution_convert_fusion.5
  524.2 8.5 convolution_convert_fusion.2
  544.7 6.7 pad_maximum_fusion.refs_2_
  551.5 101.6 %shard_map.224 = (bf16[256,2560]{1,0:T(8,128)(2,1)S(1)}, bf16[256,2560]{1,0:T(8,128)(2,1)S(1)}, bf16[2,3,4,80,1024]{4,3,2,1,0:T(8,128)(2,1)}, bf16[2,3,4,80,1024]{4,3,2,1,0:T(8,128)(2,1)}, bf16[16,1024]{1,0:T(8,128)(2,1)S(1)}) custom-call(bf16[4,256,2560]{2,1,0:T(8,128)(2,1)} %bitcast.317, bf16[4,256,2560]{2,1,0:T(8,128)(2,1)} %bitcast.318, ...), custom_call_target="tpu_custom_call" | custom-call | tf_op jit(solution)/shard_map/pallas_call | solution.py:583
  666.6 6.4 fusion.28
  673.0 6.6 fusion
  699.3 97.3 %shard_map.226 = (f32[256,512]{1,0:T(8,128)S(1)}, bf16[2,3,4,80,1024]{4,3,2,1,0:T(8,128)(2,1)}, bf16[2,2,4,80,1280]{4,3,2,1,0:T(8,128)(2,1)S(1)}) custom-call(bf16[9,256,512]{2,1,0:T(8,128)(2,1)S(1)} %bitcast.291, bf16[2,3,4,80,1024]{4,3,2,1,0:T(8,128)(2,1)} %get-tuple-element.45.refs_1_, bf16[4,4,160,1280]{3,2,1,0:T(8,128)(2,1)} %bitcast.298), custom_call_target="tpu_custom_call" | custom-call | tf_op jit(solution)/shard_map/pallas_call | solution.py:583
  835.0 68.4 %shard_map.227 = (bf16[4,3,160,1024]{3,2,1,0:T(8,128)(2,1)}, bf16[2,4,80,1280]{3,2,1,0:T(8,128)(2,1)S(1)}, bf16[2,2,4,80,1280]{4,3,2,1,0:T(8,128)(2,1)}, bf16[2,2,4,48,512]{4,3,2,1,0:T(8,128)(2,1)S(1)}) custom-call(bf16[3,4,160,1024]{3,2,1,0:T(8,128)(2,1)} %pad_maximum_fusion.1.refs_0_, bf16[2,4,80,1280]{3,2,1,0:T(8,128)(2,1)S(1)} %pad_maximum_fusion.3.refs_1_, ...), custom_call_target="tpu_custom_call" | custom-call | tf_op jit(solution)/shard_map/pallas_call | solution.py:583
  908.4 50.5 %shard_map.228 = (bf16[4,160,1280]{2,1,0:T(8,128)(2,1)S(1)}, bf16[2,4,80,1280]{3,2,1,0:T(8,128)(2,1)S(1)}, bf16[2,4,48,512]{3,2,1,0:T(8,128)(2,1)S(1)}) custom-call(bf16[4,160,1280]{2,1,0:T(8,128)(2,1)S(1)} %pad_maximum_fusion.4.refs_0_, bf16[2,4,80,1280]{3,2,1,0:T(8,128)(2,1)} %pad_maximum_fusion.5.refs_1_, ...), custom_call_target="tpu_custom_call" | custom-call | tf_op jit(solution)/shard_map/pallas_call | solution.py:583
  959.9 54.2 %shard_map.229 = (bf16[4,160,1280]{2,1,0:T(8,128)(2,1)S(1)}, bf16[4,96,512]{2,1,0:T(8,128)(2,1)S(1)}) custom-call(bf16[4,160,1280]{2,1,0:T(8,128)(2,1)S(1)} %pad_maximum_fusion.6.refs_0_, bf16[4,96,512]{2,1,0:T(8,128)(2,1)S(1)} %pad_maximum_fusion.8.refs_1_), custom_call_target="tpu_custom_call" | custom-call | tf_op jit(solution)/shard_map/pallas_call | solution.py:583
  1027.9 7.4 slice.319
  (293 shorter events, 164.3 us)
Async XLA Ops:
  84.8 22.9 %copy-start.47 = (f32[256]{0:T(256)}, f32[256]{0:T(256)S(1)}, u32[]{:S(2)}) copy-start(f32[256]{0:T(256)S(1)} %get-tuple-element.137) | copy-start | bytes 3076
  135.5 236.9 %copy-start.31 = (f32[256,5,128]{0,2,1:T(8,128)S(1)}, f32[256,5,128]{0,2,1:T(8,128)}, u32[]{:S(2)}) copy-start(f32[256,5,128]{0,2,1:T(8,128)} %slice.335) | copy-start | bytes 1966084
  135.5 236.9 %copy-start.37 = (f32[256,5,64]{0,2,1:T(8,128)S(1)}, f32[256,5,64]{0,2,1:T(8,128)}, u32[]{:S(2)}) copy-start(f32[256,5,64]{0,2,1:T(8,128)} %get-tuple-element.107) | copy-start | bytes 983044
  135.5 236.9 %copy-start.39 = (f32[256,5,64]{0,2,1:T(8,128)S(1)}, f32[256,5,64]{0,2,1:T(8,128)}, u32[]{:S(2)}) copy-start(f32[256,5,64]{0,2,1:T(8,128)} %get-tuple-element.108) | copy-start | bytes 983044
  397.8 51.7 %copy-start.10 = (f32[256,2560]{1,0:T(8,128)}, f32[256,2560]{1,0:T(8,128)S(1)}, u32[]{:S(2)}) copy-start(f32[256,2560]{1,0:T(8,128)S(1)} %get-tuple-element.71) | copy-start | bytes 7864324
  449.5 13.8 %copy-start.21 = (bf16[4,256,2560]{2,1,0:T(8,128)(2,1)S(1)}, bf16[4,256,2560]{2,1,0:T(8,128)(2,1)}, u32[]{:S(2)}) copy-start(bf16[4,256,2560]{2,1,0:T(8,128)(2,1)} %shard_map.223) | copy-start | bytes 15728644
  463.3 21.0 %slice-start.11 = ((s8[5242880]{0:T(1024)(128)(4,1)}), s8[1048576]{0:T(1024)(128)(4,1)S(1)}, s32[]{:S(2)}) async-start(s8[5242880]{0:T(1024)(128)(4,1)} %bitcast.319), calls=%async_computation.11 | async-start | bytes 2097152
  471.8 12.5 %slice-start.12 = ((s8[5242880]{0:T(1024)(128)(4,1)}), s8[4194304]{0:T(1024)(128)(4,1)S(1)}, s32[]{:S(2)}) async-start(s8[5242880]{0:T(1024)(128)(4,1)} %bitcast.319), calls=%async_computation.12 | async-start | bytes 8388608
  471.8 12.5 %copy-start.53 = (f32[1024,1024]{1,0:T(8,128)S(1)}, f32[1024,1024]{1,0:T(8,128)}, u32[]{:S(2)}) copy-start(f32[1024,1024]{1,0:T(8,128)} %fusion.138) | copy-start | bytes 12582916
  471.8 24.8 %slice-start.15 = ((s8[5242880]{0:T(1024)(128)(4,1)}), s8[4194304]{0:T(1024)(128)(4,1)S(1)}, s32[]{:S(2)}) async-start(s8[5242880]{0:T(1024)(128)(4,1)} %bitcast.328), calls=%async_computation.15 | async-start | bytes 8388608
  471.8 33.1 %slice-start.13 = ((s8[5242880]{0:T(1024)(128)(4,1)}), s8[4194304]{0:T(1024)(128)(4,1)S(1)}, s32[]{:S(2)}) async-start(s8[5242880]{0:T(1024)(128)(4,1)} %bitcast.324), calls=%async_computation.13 | async-start | bytes 8388608
  484.3 12.4 %slice-start.16 = ((s8[5242880]{0:T(1024)(128)(4,1)}), s8[1048576]{0:T(1024)(128)(4,1)S(1)}, s32[]{:S(2)}) async-start(s8[5242880]{0:T(1024)(128)(4,1)} %bitcast.328), calls=%async_computation.16 | async-start | bytes 2097152
  484.3 20.6 %slice-start.14 = ((s8[5242880]{0:T(1024)(128)(4,1)}), s8[1048576]{0:T(1024)(128)(4,1)S(1)}, s32[]{:S(2)}) async-start(s8[5242880]{0:T(1024)(128)(4,1)} %bitcast.324), calls=%async_computation.14 | async-start | bytes 2097152
  514.9 17.8 %slice-start.9 = ((s8[5242880]{0:T(1024)(128)(4,1)}), s8[1048576]{0:T(1024)(128)(4,1)S(1)}, s32[]{:S(2)}) async-start(s8[5242880]{0:T(1024)(128)(4,1)} %bitcast.312), calls=%async_computation.9 | async-start | bytes 2097152
  551.5 102.7 %copy-start.11 = (f32[256,2560]{1,0:T(8,128)S(1)}, f32[256,2560]{1,0:T(8,128)}, u32[]{:S(2)}) copy-start(f32[256,2560]{1,0:T(8,128)} %copy-done.10) | copy-start | bytes 7864324
  666.5 13.1 %slice-start = ((s8[11796480]{0:T(1024)(128)(4,1)}), s8[4194304]{0:T(1024)(128)(4,1)S(1)}, s32[]{:S(2)}) async-start(s8[11796480]{0:T(1024)(128)(4,1)} %bitcast.296), calls=%async_computation | async-start | bytes 8388608
  666.6 13.1 %slice-start.1 = ((s8[11796480]{0:T(1024)(128)(4,1)}), s8[4194304]{0:T(1024)(128)(4,1)S(1)}, s32[]{:S(2)}) async-start(s8[11796480]{0:T(1024)(128)(4,1)} %bitcast.296), calls=%async_computation.1 | async-start | bytes 8388608
  699.3 98.1 %slice-start.4 = ((s8[5898240]{0:T(1024)(128)(4,1)}), s8[4194304]{0:T(1024)(128)(4,1)S(1)}, s32[]{:S(2)}) async-start(s8[5898240]{0:T(1024)(128)(4,1)} %bitcast.302), calls=%async_computation.4 | async-start | bytes 8388608
  699.3 97.4 %copy-start.48 = (f32[256]{0:T(256)S(1)}, f32[256]{0:T(256)}, u32[]{:S(2)}) copy-start(f32[256]{0:T(256)} %copy-done.47) | copy-start | bytes 3076
  699.3 97.4 %copy-start.52 = (f32[64]{0:T(128)S(1)}, f32[64]{0:T(128)}, u32[]{:S(2)}) copy-start(f32[64]{0:T(128)} %copy-done.51) | copy-start | bytes 772
  699.3 98.1 %slice-start.5 = ((s8[5898240]{0:T(1024)(128)(4,1)}), s8[1703936]{0:T(1024)(128)(4,1)S(1)}, s32[]{:S(2)}) async-start(s8[5898240]{0:T(1024)(128)(4,1)} %bitcast.302), calls=%async_computation.5 | async-start | bytes 3407872
  835.0 68.4 %copy-start.5 = (bf16[2,2,4,80,1280]{4,3,2,1,0:T(8,128)(2,1)S(1)}, bf16[2,2,4,80,1280]{4,3,2,1,0:T(8,128)(2,1)}, u32[]{:S(2)}) copy-start(bf16[2,2,4,80,1280]{4,3,2,1,0:T(8,128)(2,1)} %copy-done.3) | copy-start | bytes 9830404
  835.0 68.4 %copy-start.20 = (bf16[4,160,1280]{2,1,0:T(8,128)(2,1)S(1)}, bf16[4,160,1280]{2,1,0:T(8,128)(2,1)}, u32[]{:S(2)}) copy-start(bf16[4,160,1280]{2,1,0:T(8,128)(2,1)} %get-tuple-element.87) | copy-start | bytes 4915204
  908.3 50.7 %copy-start.19 = (bf16[4,160,1280]{2,1,0:T(8,128)(2,1)S(1)}, bf16[4,160,1280]{2,1,0:T(8,128)(2,1)}, u32[]{:S(2)}) copy-start(bf16[4,160,1280]{2,1,0:T(8,128)(2,1)} %get-tuple-element.83) | copy-start | bytes 4915204
  (50 other events, 217.5 us)

commit v3 on v2

--- a/solution.py
+++ b/solution.py
@@ -19,6 +19,7 @@
 f32 = jnp.float32
 MESH = pl.DeviceIdType.MESH
 ANY = pl.BlockSpec(memory_space=pl.ANY)
+VMEM = pl.BlockSpec(memory_space=pltpu.VMEM)
 
 
 class Place:
@@ -84,7 +85,7 @@
 ]
 
 
-def gather(me, own, slot, part, sems, pieces=None):
+def gather(me, own, slot, part, sems):
     snd, rcv, loc = sems
     local = pltpu.make_async_copy(own, slot(me.z, me.q), loc)
     local.start()
@@ -92,46 +93,59 @@
     def line(z, k, src, to):
         return remote(src, slot(z, me.q), snd.at[z, k], rcv.at[z, 0], me.at(to, me.q))
 
+    @pl.when(me.z < 3)
+    def _():
+        line(me.z, 0, own, me.z + 1).start()
+
+    @pl.when(me.z > 0)
+    def _():
+        line(me.z, 1, own, me.z - 1).start()
+
+    def arrive(j):
+        z = me.order(j)
+        line(z, 0, slot(z, me.q), me.z).wait_recv()
+
+        @pl.when(me.inner == 1)
+        def _():
+            step = 3 - 2 * me.z if j == 1 else 2 * me.z - 3
+            line(z, 0, slot(z, me.q), me.z + step).start()
+
+    yield from in_plane(me, own, slot, part, snd, rcv, arrive)
+    local.wait()
+
+    @pl.when(me.z < 3)
+    def _():
+        line(me.z, 0, own, me.z + 1).wait_send()
+
+    @pl.when(me.z > 0)
+    def _():
+        line(me.z, 1, own, me.z - 1).wait_send()
+
+    @pl.when(me.inner == 1)
+    def _():
+        for j in range(1, 4):
+            z = me.order(j)
+            line(z, 0, slot(z, me.q), me.z).wait_send()
+
+
+def in_plane(me, own, slot, part, snd, rcv, arrive):
     def across(z, k, src):
         q = (me.xq, me.yq)[k]
         return remote(src, slot(z, me.q), snd.at[z, 2 + k], rcv.at[z, 1 + k], me.at(me.z, q))
 
     def corner(z, k):
         src = part(z, (me.xq, me.yq)[k], k)
+        if src is None:
+            return None
         return remote(src, src, snd.at[z, 4 + k], rcv.at[z, 3 + k], me.at(me.z, (me.yq, me.xq)[k]))
 
-    if pieces is None:
-
-        @pl.when(me.z < 3)
-        def _():
-            line(me.z, 0, own, me.z + 1).start()
-
-        @pl.when(me.z > 0)
-        def _():
-            line(me.z, 1, own, me.z - 1).start()
-
-    else:
-        for j in range(1, 4):
-            z = me.order(j)
-            remote(
-                pieces(z), slot(me.z, me.q), snd.at[z, 0], rcv.at[me.z, 0], me.at(z, me.q)
-            ).start()
     for k in range(2):
         across(me.z, k, own).start()
     yield
     for j in range(1, 5):
         if j < 4:
+            arrive(j)
             z = me.order(j)
-            remote(
-                slot(z, me.q), slot(z, me.q), snd.at[z, 0], rcv.at[z, 0], me.at(me.z, me.q)
-            ).wait_recv()
-            if pieces is None:
-
-                @pl.when(me.inner == 1)
-                def _():
-                    step = 3 - 2 * me.z if j == 1 else 2 * me.z - 3
-                    line(z, 0, slot(z, me.q), me.z + step).start()
-
             for k in range(2):
                 across(z, k, slot(z, me.q)).start()
         z = me.order(j - 1)
@@ -140,40 +154,76 @@
             remote(
                 slot(z, q), slot(z, q), snd.at[z, 2 + k], rcv.at[z, 1 + k], me.at(me.z, q)
             ).wait_recv()
-            corner(z, k).start()
+            copy = corner(z, k)
+            if copy is not None:
+                copy.start()
         yield
     yield True
     for j in range(4):
         z = me.order(j)
         for k in range(2):
             src = part(z, me.dq, k)
-            remote(src, src, snd.at[z, 4 + k], rcv.at[z, 3 + k], me.at(me.z, me.xq)).wait_recv()
-    local.wait()
+            if src is not None:
+                remote(src, src, snd.at[z, 4 + k], rcv.at[z, 3 + k], me.at(me.z, me.xq)).wait_recv()
     for j in range(4):
         z = me.order(j)
         for k in range(2):
             across(z, k, slot(z, me.q)).wait_send()
-            corner(z, k).wait_send()
-    if pieces is None:
-
-        @pl.when(me.z < 3)
-        def _():
-            line(me.z, 0, own, me.z + 1).wait_send()
-
-        @pl.when(me.z > 0)
-        def _():
-            line(me.z, 1, own, me.z - 1).wait_send()
-
-        @pl.when(me.inner == 1)
-        def _():
-            for j in range(1, 4):
-                z = me.order(j)
-                line(z, 0, slot(z, me.q), me.z).wait_send()
-
-    else:
-        for j in range(1, 4):
-            z = me.order(j)
-            remote(pieces(z), pieces(z), snd.at[z, 0], rcv.at[z, 0], me.at(z, me.q)).wait_send()
+            copy = corner(z, k)
+            if copy is not None:
+                copy.wait_send()
+
+
+PIECE_SEMS = [
+    pltpu.SemaphoreType.DMA((4, 6)),
+    pltpu.SemaphoreType.DMA((4, 5)),
+    pltpu.SemaphoreType.DMA((4, 2)),
+    pltpu.SemaphoreType.DMA((4, 2)),
+]
+
+
+def gather_pieces(me, sources, dst, sems):
+    snd, rcv, piece_snd, piece_rcv = sems
+    half = dst.shape[2] // 2
+
+    def slot(z, q):
+        return dst.at[:, 4 * z + q]
+
+    def part(z, q, h):
+        return dst.at[:, 4 * z + q, pl.ds(h * half, half)]
+
+    def local(n):
+        parts, piece = sources[n]
+        return pltpu.make_async_copy(piece(me.z), dst.at[parts, me.r], piece_snd.at[me.z, n])
+
+    def send(z, n):
+        parts, piece = sources[n]
+        return remote(
+            piece(z), dst.at[parts, me.r], piece_snd.at[z, n], piece_rcv.at[me.z, n], me.at(z, me.q)
+        )
+
+    for n in range(len(sources)):
+        local(n).start()
+    for j in range(1, 3):
+        for n in range(len(sources)):
+            send(me.order(j), n).start()
+    yield
+    for n in range(len(sources)):
+        send(me.order(3), n).start()
+    yield
+
+    def arrive(j):
+        z = me.order(j)
+        for n in range(len(sources)):
+            view = dst.at[sources[n][0], 4 * z + me.q]
+            remote(view, view, piece_snd.at[z, n], piece_rcv.at[z, n], me.at(z, me.q)).wait_recv()
+
+    for n in range(len(sources)):
+        local(n).wait()
+    yield from in_plane(me, slot(me.z, me.q), slot, part, snd, rcv, arrive)
+    for j in range(1, 4):
+        for n in range(len(sources)):
+            send(me.order(j), n).wait_send()
 
 
 SPREAD_SEMS = [
@@ -564,7 +614,7 @@
     local.wait()
 
 
-def transfer(number, inputs, outputs, scratch, steps, whole=False):
+def transfer(number, inputs, outputs, scratch, steps, whole=False, near=()):
     flat = [item for group in scratch for item in group]
     sizes = [len(group) for group in scratch]
 
@@ -583,41 +633,25 @@
     return pl.pallas_call(
         kernel,
         out_shape=[jax.ShapeDtypeStruct(shape, dtype) for shape, dtype in outputs],
-        in_specs=[ANY] * len(inputs),
+        in_specs=[VMEM if i in near else ANY for i in range(len(inputs))],
         out_specs=[ANY] * len(outputs),
         scratch_shapes=flat,
         compiler_params=pltpu.CompilerParams(
-            collective_id=number, has_side_effects=True, vmem_limit_bytes=48 * 2**20
+            collective_id=number, has_side_effects=True, vmem_limit_bytes=56 * 2**20
         ),
     )(*inputs)
 
 
 def gather_rows(me, src, dst, sems):
-    half = src.shape[0] // 2
-    return gather(
-        me,
-        src,
-        lambda z, q: dst.at[4 * z + q],
-        lambda z, q, h: dst.at[4 * z + q, pl.ds(h * half, half)],
-        sems,
-    )
-
-
-def gather_pieces(me, src, dst, sems):
-    half = src.shape[1] // 2
-    width = dst.shape[-1]
-
-    def piece(z):
-        return src.at[:, :, pl.ds(pl.multiple_of(z * width, width), width)]
-
-    return gather(
-        me,
-        piece(me.z),
-        lambda z, q: dst.at[:, 4 * z + q],
-        lambda z, q, h: dst.at[:, 4 * z + q, pl.ds(h * half, half)],
-        sems,
-        piece,
-    )
+    rows = src.shape[0]
+    cut = -(-rows // 32) * 16
+
+    def part(z, q, h):
+        if cut == rows and h:
+            return None
+        return dst.at[4 * z + q, pl.ds(h * cut, (rows - cut) if h else cut)]
+
+    return gather(me, src, lambda z, q: dst.at[4 * z + q], part, sems)
 
 
 def group_lists(groups):
@@ -638,22 +672,16 @@
     )
 
 
-def merge(blocks, axis, groups):
-    shape = blocks.shape
-    rows = shape[axis + 1]
-    if groups > 1:
-        blocks = blocks.reshape(shape[: axis + 1] + (groups, rows // groups) + shape[axis + 2 :])
-        blocks = jnp.moveaxis(blocks, axis + 1, axis)
-    return blocks.reshape(shape[:axis] + (shape[axis] * rows,) + shape[axis + 2 :])
-
-
-def split(full, axis, places, groups):
-    shape = full.shape
-    rows = shape[axis] // (places * groups)
-    blocks = full.reshape(shape[:axis] + (groups, places, rows) + shape[axis + 1 :])
-    if groups > 1:
-        blocks = jnp.moveaxis(blocks, axis, axis + 1)
-    return blocks.reshape(shape[:axis] + (places, groups * rows) + shape[axis + 1 :])
+def to_places(x, groups):
+    if groups == 1:
+        return x
+    return x.reshape(x.shape[0], groups, RING, -1).swapaxes(1, 2).reshape(x.shape)
+
+
+def from_places(x, groups):
+    if groups == 1:
+        return x
+    return x.reshape(x.shape[0], RING, groups, -1).swapaxes(1, 2).reshape(x.shape)
 
 
 def normalize(stream, scale_vec):
@@ -710,20 +738,24 @@
     q = r % 4
     groups = lax.axis_size("seq") // RING
     tokens, width = inputs.shape
+    inputs = to_places(inputs, groups)
+    cotangent = to_places(cotangent, groups)
     heads = query_weight.shape[1] // HD
     hidden_half = gate_up_weight.shape[2]
-    hidden_block = hidden_half // LINE
-    hidden_pad = -(-hidden_block // LANES) * LANES
+    block = -(-hidden_half // (LINE * LANES)) * LANES
+    block_start = jnp.minimum(z * block, hidden_half - block)
+    block_skip = z * block - block_start
     reach = (W + tokens - 2) // tokens
+    span = (reach + 1) * tokens
+    first_block = jnp.maximum(r - reach, 0)
     scale_factor = HD ** (-0.5)
     assert tokens * RING == SEQ_LEN and lax.axis_size("tensor") == 2
 
     kv_own = grow(key_value_weight, 0, groups)
-    kv_rows = kv_own.shape[0]
+    kv_rows, columns = kv_own.shape
     vectors = [grow(v, 0, groups) for v in (attn_gain, out_bias, mlp_gain, down_bias)]
     hidden_bias = grow(gate_up_bias, 1, groups)
     marks = jnp.stack([segment_ids // 256, segment_ids % 256]).astype(bf16)
-    columns = kv_own.shape[1]
 
     def pad_to(x, n):
         return jnp.pad(x, ((0, 0), (0, n - x.shape[1])))
@@ -736,56 +768,68 @@
             jnp.zeros((8, columns), bf16),
         ]
     )
-    kv_block = jnp.concatenate([kv_own, small])
     query_own = grow(query_weight, 0, groups)
     out_own = grow(out_weight.T, 0, groups)
-    ffn_own = grow(jnp.concatenate([gate_up_weight, down_weight.T[None]]), 1, groups)
-    ffn_own = jnp.pad(
-        ffn_own.reshape(3, -1, LINE, hidden_block),
-        ((0, 0), (0, 0), (0, 0), (0, hidden_pad - hidden_block)),
-    ).reshape(3, -1, LINE * hidden_pad)
+    gate_up_own = grow(gate_up_weight, 1, groups)
+    down_own = grow(down_weight.T, 0, groups)
     rows = query_own.shape[0]
 
     def first_steps(me, ins, outs, sems):
-        def both():
-            for _ in gather_rows(me, ins[1], outs[1], sems[1]):
+        def both(n):
+            mine = outs[n].at[:, me.t]
+            for _ in gather_rows(me, ins[n], mine, sems[n]):
                 yield
-            yield from swap(me, outs[1], outs[2], sems[2])
-
-        return [gather_rows(me, ins[0], outs[0], sems[0]), both()]
-
-    query_full, kv_mine, kv_theirs = transfer(
+            copy = remote(mine, mine, sems[4][0].at[n], sems[4][1].at[n], me.other())
+            copy.start()
+            yield True
+            copy.wait()
+
+        return [
+            both(2),
+            both(1),
+            gather_rows(me, ins[0], outs[0], sems[0]),
+            spread(me, ins[3], outs[3], sems[3]),
+        ]
+
+    query_full, kv_full, smalls, cot_all = transfer(
         0,
-        [query_own, kv_block],
-        [((RING,) + query_own.shape, bf16)] + [((RING,) + kv_block.shape, bf16)] * 2,
-        [GATHER_SEMS, GATHER_SEMS, SWAP_SEMS],
+        [query_own, kv_own, small, cotangent],
+        [
+            ((RING,) + query_own.shape, bf16),
+            ((RING, 2) + kv_own.shape, bf16),
+            ((RING, 2) + small.shape, bf16),
+            ((LINE,) + cotangent.shape, bf16),
+        ],
+        [
+            GATHER_SEMS,
+            GATHER_SEMS,
+            GATHER_SEMS,
+            SPREAD_SEMS,
+            [pltpu.SemaphoreType.DMA((3,)), pltpu.SemaphoreType.DMA((3,))],
+        ],
         first_steps,
     )
-    query_full = merge(query_full, 0, groups)
-    kv_both = jnp.where(
-        t == 0, jnp.stack([kv_mine, kv_theirs], 1), jnp.stack([kv_theirs, kv_mine], 1)
-    )
-    kv_full = merge(
-        kv_both[:, :, :kv_rows]
-        .reshape(RING, 2, groups, kv_rows // groups, columns)
-        .swapaxes(1, 2)
-        .reshape(RING, 2 * kv_rows, columns),
-        0,
-        groups,
-    )
-
-    def vector(row, count):
-        piece = kv_both[:, :, kv_rows + row, :count].reshape(RING, 2, groups, count // groups)
-        return jnp.transpose(piece, (2, 0, 1, 3)).reshape(-1).astype(f32)
-
-    gain_one, bias_out, gain_two, bias_down = (vector(i, kv_rows) for i in range(4))
-    bias_gate_up = jnp.stack([vector(4 + i, hidden_bias.shape[1]) for i in range(2)])
-    bias_local = lax.dynamic_slice_in_dim(
-        bias_gate_up, t * hidden_half + z * hidden_block, hidden_block, 1
-    )
-    bias_local = pad_to(bias_local, hidden_pad)
-    all_marks = kv_both[:, 0, kv_rows + 6 : kv_rows + 8, :tokens].astype(f32)
+    query_full = query_full.reshape(width, heads * HD)
+    if groups > 1:
+        kv_full = kv_full.reshape(RING, 2, groups, kv_rows // groups, columns).swapaxes(1, 2)
+    kv_full = kv_full.reshape(width, columns)
+    cot_all = cot_all.reshape(LINE * tokens, width)
+
+    def vector(row, count, order):
+        piece = smalls[:, :, row, :count].reshape(RING, 2, groups, count // groups)
+        return jnp.transpose(piece, order).reshape(-1).astype(f32)
+
+    gain_one, bias_out, gain_two, bias_down = (
+        vector(i, kv_rows, (0, 2, 1, 3)) for i in range(4)
+    )
+    bias_gate_up = jnp.stack(
+        [vector(4 + i, hidden_bias.shape[1], (2, 0, 1, 3)) for i in range(2)]
+    )
+    bias_local = lax.dynamic_slice_in_dim(bias_gate_up, t * hidden_half + block_start, block, 1)
+    all_marks = smalls[:, 0, 6:8, :tokens].astype(f32)
     all_marks = (all_marks[:, 0] * 256.0 + all_marks[:, 1]).reshape(-1)
+    window_marks = lax.dynamic_slice_in_dim(all_marks, first_block * tokens, span, 0)
+    own_marks = lax.dynamic_slice_in_dim(all_marks, r * tokens, tokens, 0)
 
     stream = inputs.astype(f32)
     places = r * tokens + jnp.arange(tokens, dtype=jnp.int32)
@@ -797,55 +841,177 @@
     values_own = key_value[:, HD:].astype(bf16)
     own_block = jnp.concatenate([keys_own, values_own], axis=1)
 
-    def second_steps(me, ins, outs, sems):
-        return [
-            gather_rows(me, ins[0], outs[0], sems[0]),
-            gather_rows(me, ins[1], outs[1], sems[1]),
-            gather_pieces(me, ins[2], outs[2], sems[2]),
-            spread(me, ins[3], outs[3], sems[3]),
-        ]
-
-    kv_all, out_full, ffn_full, cot_all = transfer(
+    def second_steps(me, ins, outs, groups_in):
+        own_kv, own_out, own_gate_up, own_down, q_in, x_in, vec, marks_row, marks_column = ins
+        kv_all, out_all, ffn_all, mixed_out, log_out, middle_out, normed_out = outs
+        kv_sems, out_sems, ffn_sems, spread_sems, swap_sems, scratch = groups_in
+        qs, win, weight, mask, mixed, part, theirs, x, middle, normed_two, logs, loads = scratch
+
+        def load(n, src, dst):
+            return pltpu.make_async_copy(src, dst, loads.at[n])
+
+        def columns_of(source, lead):
+            def piece(place):
+                start = jnp.minimum(place * block, hidden_half - block)
+                at = pl.ds(pl.multiple_of(start, LANES), block)
+                return source.at[:, :, at] if lead else source.at[:, at]
+
+            return piece
+
+        keys = gather_rows(me, own_kv, kv_all, kv_sems)
+        outw = gather_rows(me, own_out, out_all, out_sems)
+        ffn = gather_pieces(
+            me,
+            [(pl.ds(0, 2), columns_of(own_gate_up, True)), (2, columns_of(own_down, False))],
+            ffn_all,
+            ffn_sems,
+        )
+        next(keys)
+        load(0, q_in, qs).start()
+        load(1, x_in, x).start()
+        next(outw)
+        start = jnp.maximum(me.r - reach, 0)
+        row_places = me.r * tokens + lax.broadcasted_iota(jnp.int32, (tokens, 1), 0)
+
+        @pl.loop(0, reach + 1)
+        def _(i):
+            at = pl.ds(pl.multiple_of(i * tokens, tokens), tokens)
+            key_places = (start + i) * tokens + lax.broadcasted_iota(jnp.int32, (1, tokens), 1)
+            gap = row_places - key_places
+            seen = (gap >= 0) & (gap < W) & (marks_column[...] == marks_row[:, at])
+            mask[:, at] = jnp.where(seen, 0.0, -1e30)
+
+        next(keys)
+        next(keys)
+        next(ffn)
+        for _ in range(3):
+            next(keys)
+        next(outw)
+        next(keys, None)
+        window = load(2, kv_all.at[pl.ds(start, reach + 1)], win)
+        window.start()
+        load(0, q_in, qs).wait()
+        window.wait()
+
+        @pl.loop(0, heads)
+        def _(h):
+            at = pl.ds(pl.multiple_of(h * HD, HD), HD)
+            both = win[...].reshape(span, 2 * HD)
+            scores = dot(qs[:, at], both[:, :HD], 1, 1) + mask[...]
+            top = jnp.max(scores, axis=1, keepdims=True)
+            exponent = jnp.exp(scores - top)
+            total = jnp.sum(exponent, axis=1, keepdims=True)
+            blend = dot(exponent.astype(bf16), both[:, HD:])
+            mixed[:, at] = (blend / total).astype(bf16)
+            logs[h] = top + jnp.log(total)
+            for i in range(1, heads):
+
+                @pl.when(h == i)
+                def _():
+                    next(outw if i < 4 else ffn)
+
+        next(ffn)
+        for _ in outw:
+            pass
+        load(3, mixed, mixed_out).start()
+        load(4, logs, log_out).start()
+        weights = load(2, out_all, weight)
+        weights.start()
+        weights.wait()
+
+        @pl.loop(0, LINE)
+        def _(i):
+            at = pl.ds(pl.multiple_of(i * 4 * rows, LANES), 4 * rows)
+            piece = weight[pl.ds(4 * i, 4)].reshape(4 * rows, heads * HD)
+            part[:, at] = dot(mixed[...], piece, 1, 1).astype(bf16)
+
+        swapped = remote(part, theirs, swap_sems[0], swap_sems[1], me.other())
+        swapped.start()
+        load(1, x_in, x).wait()
+        swapped.wait()
+
+        @pl.loop(0, tokens // 16)
+        def _(i):
+            at = pl.ds(pl.multiple_of(i * 16, 16), 16)
+            total = x[at].astype(f32) + (part[at].astype(f32) + theirs[at].astype(f32)) + vec[0:1]
+            middle[at] = total
+            scale = lax.rsqrt(jnp.mean(total * total, axis=1, keepdims=True) + epsilon)
+            normed_two[at] = (total * scale * vec[1:2]).astype(bf16)
+
+        out = spread(me, normed_two, normed_out, spread_sems)
+        next(out)
+        load(0, middle, middle_out).start()
+        next(ffn)
+        next(out)
+        next(ffn)
+        next(out)
+        next(out)
+        next(out)
+        for step in (ffn, out):
+            for _ in step:
+                pass
+        load(3, mixed, mixed_out).wait()
+        load(4, logs, log_out).wait()
+        load(0, middle, middle_out).wait()
+        return []
+
+    kv_all, out_full, ffn_full, mixed_low, log_total, middle, normed_all = transfer(
         1,
-        [own_block, out_own, ffn_own, cotangent],
+        [
+            own_block,
+            out_own,
+            gate_up_own,
+            down_own,
+            queries,
+            inputs,
+            jnp.stack([bias_out, gain_two]),
+            window_marks[None],
+            own_marks[:, None],
+        ],
         [
             ((RING,) + own_block.shape, bf16),
             ((RING,) + out_own.shape, bf16),
-            ((3, RING, rows, hidden_pad), bf16),
-            ((LINE,) + cotangent.shape, bf16),
+            ((3, RING, rows, block), bf16),
+            (queries.shape, bf16),
+            ((heads, tokens, 1), f32),
+            (inputs.shape, f32),
+            ((LINE,) + inputs.shape, bf16),
         ],
-        [GATHER_SEMS, GATHER_SEMS, GATHER_SEMS, SPREAD_SEMS],
+        [
+            GATHER_SEMS,
+            GATHER_SEMS,
+            PIECE_SEMS,
+            SPREAD_SEMS,
+            SWAP_SEMS,
+            [
+                pltpu.VMEM(queries.shape, bf16),
+                pltpu.VMEM((reach + 1, tokens, 2 * HD), bf16),
+                pltpu.VMEM((RING,) + out_own.shape, bf16),
+                pltpu.VMEM((tokens, span), f32),
+                pltpu.VMEM(queries.shape, bf16),
+                pltpu.VMEM(inputs.shape, bf16),
+                pltpu.VMEM(inputs.shape, bf16),
+                pltpu.VMEM(inputs.shape, bf16),
+                pltpu.VMEM(inputs.shape, f32),
+                pltpu.VMEM(inputs.shape, bf16),
+                pltpu.VMEM((heads, tokens, 1), f32),
+                pltpu.SemaphoreType.DMA((5,)),
+            ],
+        ],
         second_steps,
-    )
-    out_full = merge(out_full, 0, groups)
-    ffn_full = merge(ffn_full, 1, groups)
-    cot_all = cot_all.reshape(LINE * tokens, width)
-
-    first_block = jnp.maximum(r - reach, 0)
-    span = (reach + 1) * tokens
-    window = lax.dynamic_slice_in_dim(
-        kv_all.reshape(RING * tokens, 2 * HD), first_block * tokens, span, 0
-    )
-    window_marks = lax.dynamic_slice_in_dim(all_marks, first_block * tokens, span, 0)
-    own_marks = lax.dynamic_slice_in_dim(all_marks, r * tokens, tokens, 0)
+        near=(6, 7, 8),
+    )
+    out_full = out_full.reshape(width, heads * HD)
+    ffn_full = ffn_full.reshape(3, width, block)
     key_places = first_block * tokens + jnp.arange(span, dtype=jnp.int32)
     key_gap = places[:, None] - key_places[None, :]
     visible = (key_gap >= 0) & (key_gap < W) & (own_marks[:, None] == window_marks[None, :])
+    window = lax.dynamic_slice_in_dim(
+        kv_all.reshape(RING * tokens, 2 * HD), first_block * tokens, span, 0
+    )
     key_win = window[:, :HD]
     value_win = window[:, HD:]
     query_heads = queries.reshape(tokens, heads, HD)
-    scores = jnp.einsum("qhd,kd->hqk", query_heads, key_win, preferred_element_type=f32)
-    scores = jnp.where(visible[None], scores, -1e30)
-    row_top = jnp.max(scores, axis=-1, keepdims=True)
-    exponent = jnp.exp(scores - row_top)
-    row_total = jnp.sum(exponent, axis=-1, keepdims=True)
-    log_total = row_top + jnp.log(row_total)
-    probs_low = (exponent / row_total).astype(bf16)
-    mixed_low = (
-        jnp.einsum("hqk,kd->qhd", probs_low, value_win, preferred_element_type=f32)
-        .reshape(tokens, heads * HD)
-        .astype(bf16)
-    )
 
     def both_cores(number, part):
         (theirs,) = transfer(
@@ -857,29 +1023,19 @@
         )
         return part.astype(f32) + theirs.astype(f32)
 
-    branch = both_cores(2, dot(mixed_low, out_full, 1, 1).astype(bf16))
-    middle = stream + branch + bias_out
-    normed_two = normalize(middle, gain_two).astype(bf16)
-
-    (normed_all,) = transfer(
-        3,
-        [normed_two],
-        [((LINE,) + normed_two.shape, bf16)],
-        [SPREAD_SEMS],
-        lambda me, ins, outs, sems: [spread(me, ins[0], outs[0], sems[0])],
-    )
     normed_all = normed_all.reshape(LINE * tokens, width)
+    ours = (jnp.arange(block) >= block_skip)[None, :]
     gate_pre = dot(normed_all, ffn_full[0]) + bias_local[0]
     up_pre = dot(normed_all, ffn_full[1]) + bias_local[1]
-    hidden = (jax.nn.gelu(gate_pre, approximate=True) * up_pre).astype(bf16)
+    hidden = jnp.where(ours, jax.nn.gelu(gate_pre, approximate=True) * up_pre, 0.0).astype(bf16)
     mlp_part = dot(hidden, ffn_full[2], 1, 1).astype(bf16)
     hidden_grad = dot(cot_all, ffn_full[2])
     _, unit_pull = jax.vjp(
         lambda gate_in, up_in: jax.nn.gelu(gate_in, approximate=True) * up_in, gate_pre, up_pre
     )
     gate_grad, up_grad = unit_pull(hidden_grad)
-    gate_low = gate_grad.astype(bf16)
-    up_low = up_grad.astype(bf16)
+    gate_low = jnp.where(ours, gate_grad, 0.0).astype(bf16)
+    up_low = jnp.where(ours, up_grad, 0.0).astype(bf16)
     ffn_term = jnp.stack(
         [
             dot(normed_all, gate_low, 0, 0).astype(bf16),
@@ -887,7 +1043,7 @@
             dot(cot_all, hidden, 0, 0).astype(bf16),
         ]
     )
-    ffn_term = split(ffn_term, 1, RING, groups).reshape(3, LINE, 4, rows, hidden_pad)
+    ffn_term = ffn_term.reshape(3, LINE, 4, rows, block)
     normed_two_part = (dot(gate_low, ffn_full[0], 1, 1) + dot(up_low, ffn_full[1], 1, 1)).astype(
         bf16
     )
@@ -946,7 +1102,7 @@
         for step in [one, two, three] + ends:
             next(step, None)
 
-    kept_shape = (2, 3, LINE, rows // 2, hidden_pad)
+    kept_shape = (2, 3, LINE, rows // 2, block)
     normed_two_grad, mlp_out, ffn_kept, ffn_passed, bias_theirs = transfer(
         4,
         [
@@ -976,7 +1132,7 @@
     middle_grad = cot_full + middle_part
     middle_low = middle_grad.astype(bf16)
     out_term = dot(middle_low, mixed_low, 0, 0).astype(bf16)
-    out_term = split(out_term, 0, RING, groups).reshape(LINE, 4, rows, heads * HD)
+    out_term = out_term.reshape(LINE, 4, rows, heads * HD)
     mixed_grad = dot(middle_low, out_full).astype(bf16).reshape(tokens, heads, HD)
 
     scores_again = jnp.einsum("qhd,kd->hqk", query_heads, key_win, preferred_element_type=f32)
@@ -1032,16 +1188,24 @@
     stream_part, gain_one_grad = norm_one_pull(normed_grad)
     input_grad = middle_grad + stream_part
     query_term = dot(normed, query_lin_grad, 0, 0).astype(bf16)
-    query_term = split(query_term, 0, RING, groups).reshape(LINE, 4, rows, heads * HD)
-
-    def take_core(full):
+    query_term = query_term.reshape(LINE, 4, rows, heads * HD)
+
+    def take_core(full, axis):
+        blocks = lax.dynamic_index_in_dim(full, t, axis, keepdims=False)
+        return jnp.moveaxis(blocks, 1, 0).reshape(RING, full.shape[0], -1)
+
+    def core_features(full):
+        return take_core(full.reshape(full.shape[0], RING, groups, 2, -1), 3)
+
+    def core_hidden(full):
         blocks = full.reshape(full.shape[0], groups, RING, 2, -1)
-        mine = lax.dynamic_index_in_dim(blocks, t, 3, keepdims=False)
-        return jnp.transpose(mine, (2, 0, 1, 3)).reshape(RING, full.shape[0], -1)
+        return take_core(jnp.swapaxes(blocks, 1, 2), 3)
 
     kv_term = dot(normed, kv_grad_low, 0, 0)
-    kv_term = jnp.moveaxis(take_core(kv_term.T), 1, 2)
-    vector_terms = take_core(
+    kv_term = lax.dynamic_index_in_dim(
+        kv_term.reshape(RING, groups, 2, -1, columns), t, 2, keepdims=False
+    ).reshape(RING, kv_rows, columns)
+    vector_terms = core_features(
         jnp.stack(
             [gain_one_grad, jnp.sum(middle_grad, axis=0), gain_two_grad, jnp.sum(cot_full, axis=0)]
         )
@@ -1050,14 +1214,11 @@
         t == 0,
         jnp.stack([hidden_bias_part, bias_theirs]),
         jnp.stack([bias_theirs, hidden_bias_part]),
-    )[:, :2, :hidden_block].astype(f32)
-    bias_terms = lax.dynamic_update_slice_in_dim(
-        jnp.zeros((2, 2, LINE, hidden_block), f32),
-        jnp.swapaxes(bias_pair, 0, 1)[:, :, None],
-        z,
-        2,
-    ).reshape(2, -1)
-    bias_terms = take_core(bias_terms)
+    )[:, :2].astype(f32)
+    bias_terms = jnp.zeros((2, 2, hidden_half), f32)
+    start = jnp.minimum(z * block, hidden_half - block)
+    bias_terms = lax.dynamic_update_slice_in_dim(bias_terms, bias_pair, start, 2)
+    bias_terms = core_hidden(jnp.swapaxes(bias_terms, 0, 1).reshape(2, -1))
 
     def widen(x):
         return jnp.pad(x, ((0, 0), (0, 0), (0, columns - x.shape[2])))
@@ -1080,7 +1241,7 @@
         7,
         [ffn_sum, out_passed, query_term, kv_term],
         [
-            ((LINE, 3, rows, hidden_pad), bf16),
+            ((LINE, 3, rows, block), bf16),
             (out_passed.shape, bf16),
             (first_shape(query_term), bf16),
             (first_shape(kv_term), bf16),
@@ -1123,8 +1284,9 @@
         last_steps,
     )
 
-    ffn_grad = jnp.transpose(ffn_done[..., :hidden_block], (1, 2, 0, 3)).reshape(
-        3, rows, hidden_half
+    last_skip = LINE * block - hidden_half
+    ffn_grad = jnp.concatenate(
+        [ffn_done[i] for i in range(LINE - 1)] + [ffn_done[LINE - 1, :, :, last_skip:]], axis=2
     )
     ffn_grad = shrink(ffn_grad.astype(f32), 1, groups)
     out_grad = shrink(jnp.sum(out_done.astype(f32), axis=0), 0, groups).T
@@ -1136,8 +1298,8 @@
         kv_sums[kv_rows + 4 : kv_rows + 6, : hidden_bias.shape[1]], 1, groups
     )
     return (
-        output,
-        input_grad,
+        from_places(output, groups),
+        from_places(input_grad, groups),
         small_grads[0],
         query_grad,
         key_value_grad,

time: 1050 us -> 974 us (0.928)
  local copies, waits for them, and re-layouts: 106 us -> 57.1 us
  Pallas kernels: 745 us -> 707 us
  other arithmetic: 50.2 us -> 61.1 us
    pallas_call x10 -> x8, Pallas kernels: 745 us -> 707 us  [transfer(): pl.pallas_call(kernel, out_shape=[jax.ShapeDtypeStruct(shape, dtype) for...]
    unnamed x148 -> x122, local copies, waits for them, and re-layouts: 23.4 us -> 9.18 us
    concatenate x3 -> x1, local copies, waits for them, and re-layouts: 11.8 us -> 0.08 us  [body(): jnp.concatenate([pad_to(jnp.stack(vectors), columns), pad_to(hidden_bias,...]
    slice x3 -> x1, local copies, waits for them, and re-layouts: 13.6 us -> 2.57 us  [body(): ffn_grad[:2]]
    dot_general x18 -> x17, matrix products: 108 us -> 110 us  [dot(): lax.dot_general(a, b, (((ca,), (cb,)), ((), ())), preferred_element_type=...]
where the time goes in v3:
time: 974 us; the launch traced here: 970 us
  Pallas kernels  707 us (73%)
  matrix products  143 us (15%)
  other arithmetic  61.1 us (6%)
  local copies, waits for them, and re-layouts  57.1 us (6%)
    pallas_call x8, Pallas kernels, transfer(): pl.pallas_call(kernel, out_shape=[jax.ShapeDtypeStruct(shape, dtype) for...  707 us
    dot_general x17, matrix products, dot(): lax.dot_general(a, b, (((ca,), (cb,)), ((), ())), preferred_element_type=...  110 us

profile of v3, /device:TPU:0, one launch (start us, length us, event | category | flops | bytes accessed | tf_op | source)
XLA Modules:
  0.0 969.7 jit_solution(9044209609909646755)
XLA Ops:
  3.6 91.8 %shard_map.220 = (bf16[16,160,1280]{2,1,0:T(8,128)(2,1)}, bf16[16,2,80,512]{3,2,1,0:T(8,128)(2,1)}, bf16[16,2,16,512]{3,2,1,0:T(8,128)(2,1)}, bf16[4,256,2560]{2,1,0:T(8,128)(2,1)}) custom-call(bf16[160,1280]{1,0:T(8,128)(2,1)} %refs_0_.1, bf16[80,512]{1,0:T(8,128)(2,1)} %refs_1_.1, bf16[16,512]{1,0:T(8,128)(2,1)} %fusion.96.refs_2_, bf16[256,2560]{1,0:T(8,128)(2,1)} %refs_3_.1), custom_call_target="tpu_custom_call" | custom-call | tf_op jit(solution)/shard_map/pallas_call | solution.py:633
  102.1 10.0 %copy.67 = bf16[1280,2560]{1,0:T(8,128)(2,1)} copy(bf16[1280,2560]{0,1:T(8,128)(2,1)} %bitcast.266) | data formatting | bytes 13107200 | tf_op jit(solution)/shard_map/dot_general | solution.py:716
  112.1 4.9 fusion.51
  124.3 236.5 %shard_map.221 = (bf16[16,256,512]{2,1,0:T(8,128)(2,1)}, bf16[16,160,1280]{2,1,0:T(8,128)(2,1)}, bf16[3,16,160,1024]{3,2,1,0:T(8,128)(2,1)}, bf16[256,1280]{1,0:...) custom-call(bf16[256,512]{1,0:T(8,128)(2,1)} %pad_maximum_fusion.9.refs_0_, ...), custom_call_target="tpu_custom_call" | custom-call | tf_op jit(solution)/shard_map/pallas_call | solution.py:633
  360.8 11.0 %fusion.130 = (bf16[1,16,160,1024]{3,2,1,0:T(8,128)(2,1)}, bf16[1,16,160,1024]{3,2,1,0:T(8,128)(2,1)S(1)}, bf16[1,16,160,1024]{3,2,1,0:T(8,128)(2,1)}) fusion(bf16[3,16,160,1024]{3,2,1,0:T(8,128)(2,1)} %get-tuple-element.45), kind=kLoop, calls=%fused_computation.273 | loop fusion | bytes 31457280 | tf_op jit(solution)/shard_map/slice | solution.py:1029
  374.1 7.1 fusion.132
  382.8 12.6 %select_convert_fusion = (bf16[1024,1024]{1,0:T(8,128)(2,1)}, f32[1024,1024]{1,0:T(8,128)}) fusion(f32[1024]{0:T(1024)S(1)} %bitcast.309, pred[1024]{0:T(1024)(128)(4,1)S(1)} %iota_compare_fusion.5, f32[1024,1024]{1,0:T(8,128)} %fusion.132, f32[1024]{0:T(1024)S(1)} %bitcast.311, bf16[1024,2560]{1,0:T(8,128)(2,1)} %bitcast.320, bf16[2560,1024]{1,0:T(8,128)(2,1)} %bitcast.278), kind=kOutput, calls=%fused_computation.35 | convolution fusion | flops 5382340608 | bytes 20980736 | tf_op jit(solution)/shard_map/dot_general | solution.py:716
  395.4 12.7 %fusion.129 = (bf16[1024]{0:T(1024)(128)(2,1)S(1)}, bf16[1024,1024]{1,0:T(8,128)(2,1)S(1)}, bf16[1024]{0:T(1024)(128)(2,1)S(1)}, bf16[1024,1024]{1,0:T(8,128)(2,1)S(1)}) fusion(f32[1024,1024]{1,0:T(8,128)S(1)} %copy-done.44, f32[1024]{0:T(1024)S(1)} %bitcast.312, pred[1024]{0:T(1024)(128)(4,1)S(1)} %iota_compare_fusion.5, ...), kind=kOutput, calls=%fused_computation.272 | convolution fusion | flops 5400164352 | bytes 23081984 | tf_op jit(solution)/shard_map/dot_general | solution.py:716
  408.2 8.3 fusion.133
  416.5 10.1 %add_convert_fusion = bf16[1024,2560]{1,0:T(8,128)(2,1)} fusion(f32[1024,2560]{1,0:T(8,128)} %fusion.133, bf16[1024,1024]{1,0:T(8,128)(2,1)S(1)} %get-tuple-element.84, bf16[2560,1024]{1,0:T(8,128)(2,1)S(1)} %bitcast.281), kind=kOutput, calls=%fused_computation.11 | convolution fusion | flops 5373952000 | bytes 23068672 | tf_op jit(solution)/shard_map/dot_general | solution.py:716
  426.6 9.1 convolution_convert_fusion.5
  435.8 8.7 convolution_convert_fusion.2
  444.5 6.0 convolution_convert_fusion.3
  450.5 6.0 convolution_convert_fusion.4
  456.5 6.8 pad_maximum_fusion.refs_2_
  463.9 104.0 %shard_map.222 = (bf16[256,2560]{1,0:T(8,128)(2,1)}, bf16[256,2560]{1,0:T(8,128)(2,1)}, bf16[2,3,4,80,1024]{4,3,2,1,0:T(8,128)(2,1)}, bf16[2,3,4,80,1024]{4,3,2,1,0:T(8,128)(2,1)}, bf16[16,1024]{1,0:T(8,128)(2,1)}) custom-call(bf16[4,256,2560]{2,1,0:T(8,128)(2,1)} %bitcast.272, bf16[4,256,2560]{2,1,0:T(8,128)(2,1)} %bitcast.273, ...), custom_call_target="tpu_custom_call" | custom-call | tf_op jit(solution)/shard_map/pallas_call | solution.py:633
  581.7 7.6 fusion.54
  592.0 7.3 fusion.23
  599.4 8.1 fusion
  627.5 96.9 %shard_map.224 = (f32[256,512]{1,0:T(8,128)}, bf16[2,3,4,80,1024]{4,3,2,1,0:T(8,128)(2,1)}, bf16[2,2,4,80,1280]{4,3,2,1,0:T(8,128)(2,1)}) custom-call(bf16[9,256,512]{2,1,0:T(8,128)(2,1)} %bitcast.264, bf16[2,3,4,80,1024]{4,3,2,1,0:T(8,128)(2,1)} %get-tuple-element.52.refs_1_, bf16[4,4,160,1280]{3,2,1,0:T(8,128)(2,1)} %bitcast.260), custom_call_target="tpu_custom_call" | custom-call | tf_op jit(solution)/shard_map/pallas_call | solution.py:633
  727.1 4.9 convolution_bitcast_fusion.1
  771.6 68.3 %shard_map.225 = (bf16[4,3,160,1024]{3,2,1,0:T(8,128)(2,1)}, bf16[2,4,80,1280]{3,2,1,0:T(8,128)(2,1)}, bf16[2,2,4,80,1280]{4,3,2,1,0:T(8,128)(2,1)}, bf16[2,2,4,48,512]{4,3,2,1,0:T(8,128)(2,1)}) custom-call(bf16[3,4,160,1024]{3,2,1,0:T(8,128)(2,1)} %pad_maximum_fusion.1.refs_0_, bf16[2,4,80,1280]{3,2,1,0:T(8,128)(2,1)} %pad_maximum_fusion.3.refs_1_, ...), custom_call_target="tpu_custom_call" | custom-call | tf_op jit(solution)/shard_map/pallas_call | solution.py:633
  848.6 50.6 %shard_map.226 = (bf16[4,160,1280]{2,1,0:T(8,128)(2,1)}, bf16[2,4,80,1280]{3,2,1,0:T(8,128)(2,1)}, bf16[2,4,48,512]{3,2,1,0:T(8,128)(2,1)}) custom-call(bf16[4,160,1280]{2,1,0:T(8,128)(2,1)} %pad_maximum_fusion.4.refs_0_, bf16[2,4,80,1280]{3,2,1,0:T(8,128)(2,1)} %pad_maximum_fusion.5.refs_1_, bf16[2,4,48,512]{3,2,1,0:T(8,128)(2,1)} %pad_maximum_fusion.7.refs_2_), custom_call_target="tpu_custom_call" | custom-call | tf_op jit(solution)/shard_map/pallas_call | solution.py:633
  903.4 54.1 %shard_map.227 = (bf16[4,160,1280]{2,1,0:T(8,128)(2,1)}, bf16[4,96,512]{2,1,0:T(8,128)(2,1)}) custom-call(bf16[4,160,1280]{2,1,0:T(8,128)(2,1)} %pad_maximum_fusion.6.refs_0_, bf16[4,96,512]{2,1,0:T(8,128)(2,1)} %pad_maximum_fusion.8.refs_1_), custom_call_target="tpu_custom_call" | custom-call | tf_op jit(solution)/shard_map/pallas_call | solution.py:633
  (250 shorter events, 124.2 us)
Async XLA Ops:
  0.6 96.3 %copy-start.2 = (bf16[256,2560]{1,0:T(8,128)(2,1)S(1)}, bf16[256,2560]{1,0:T(8,128)(2,1)}, u32[]{:S(2)}) copy-start(bf16[256,2560]{1,0:T(8,128)(2,1)} %refs_5_.1) | copy-start | bytes 3932164
  97.0 15.2 %copy-start.31 = (f32[2560]{0:T(1024)}, f32[2560]{0:T(1024)S(1)}, u32[]{:S(2)}) copy-start(f32[2560]{0:T(1024)S(1)} %reshape.525) | copy-start | bytes 30724
  97.3 14.8 %copy-start.36 = (f32[256]{0:T(256)}, f32[256]{0:T(256)S(1)}, u32[]{:S(2)}) copy-start(f32[256]{0:T(256)S(1)} %fusion.114) | copy-start | bytes 3076
  100.6 16.4 %copy-start.34 = (f32[256]{0:T(256)}, f32[256]{0:T(256)S(1)}, u32[]{:S(2)}) copy-start(f32[256]{0:T(256)S(1)} %get-tuple-element.145) | copy-start | bytes 3076
  100.6 16.4 %copy-start.40 = (f32[64]{0:T(128)}, f32[64]{0:T(128)S(1)}, u32[]{:S(2)}) copy-start(f32[64]{0:T(128)S(1)} %multiply_power_fusion) | copy-start | bytes 772
  118.8 462.9 %copy-start.9 = (bf16[256,5,256]{0,2,1:T(8,128)(2,1)}, bf16[256,5,256]{0,2,1:T(8,128)(2,1)S(1)}, u32[]{:S(2)}) copy-start(bf16[256,5,256]{0,2,1:T(8,128)(2,1)S(1)} %fusion.49) | copy-start | bytes 1966084
  360.8 13.3 %copy-start.43 = (bf16[4,256,2560]{2,1,0:T(8,128)(2,1)S(1)}, bf16[4,256,2560]{2,1,0:T(8,128)(2,1)}, u32[]{:S(2)}) copy-start(bf16[4,256,2560]{2,1,0:T(8,128)(2,1)} %get-tuple-element.46) | copy-start | bytes 15728644
  374.1 21.2 %slice-start.5 = ((s8[5242880]{0:T(1024)(128)(4,1)}), s8[1048576]{0:T(1024)(128)(4,1)S(1)}, s32[]{:S(2)}) async-start(s8[5242880]{0:T(1024)(128)(4,1)} %bitcast.274), calls=%async_computation.5 | async-start | bytes 2097152
  382.8 12.6 %slice-start.6 = ((s8[5242880]{0:T(1024)(128)(4,1)}), s8[4194304]{0:T(1024)(128)(4,1)S(1)}, s32[]{:S(2)}) async-start(s8[5242880]{0:T(1024)(128)(4,1)} %bitcast.274), calls=%async_computation.6 | async-start | bytes 8388608
  382.8 12.6 %copy-start.44 = (f32[1024,1024]{1,0:T(8,128)S(1)}, f32[1024,1024]{1,0:T(8,128)}, u32[]{:S(2)}) copy-start(f32[1024,1024]{1,0:T(8,128)} %fusion.132) | copy-start | bytes 12582916
  382.8 25.4 %slice-start.9 = ((s8[5242880]{0:T(1024)(128)(4,1)}), s8[4194304]{0:T(1024)(128)(4,1)S(1)}, s32[]{:S(2)}) async-start(s8[5242880]{0:T(1024)(128)(4,1)} %bitcast.283), calls=%async_computation.9 | async-start | bytes 8388608
  382.8 33.7 %slice-start.7 = ((s8[5242880]{0:T(1024)(128)(4,1)}), s8[4194304]{0:T(1024)(128)(4,1)S(1)}, s32[]{:S(2)}) async-start(s8[5242880]{0:T(1024)(128)(4,1)} %bitcast.279), calls=%async_computation.7 | async-start | bytes 8388608
  395.4 12.8 %slice-start.10 = ((s8[5242880]{0:T(1024)(128)(4,1)}), s8[1048576]{0:T(1024)(128)(4,1)S(1)}, s32[]{:S(2)}) async-start(s8[5242880]{0:T(1024)(128)(4,1)} %bitcast.283), calls=%async_computation.10 | async-start | bytes 2097152
  395.4 21.1 %slice-start.8 = ((s8[5242880]{0:T(1024)(128)(4,1)}), s8[1048576]{0:T(1024)(128)(4,1)S(1)}, s32[]{:S(2)}) async-start(s8[5242880]{0:T(1024)(128)(4,1)} %bitcast.279), calls=%async_computation.8 | async-start | bytes 2097152
  426.6 9.1 copy-start.45
  426.6 17.8 %slice-start.11 = ((s8[5242880]{0:T(1024)(128)(4,1)}), s8[4194304]{0:T(1024)(128)(4,1)S(1)}, s32[]{:S(2)}) async-start(s8[5242880]{0:T(1024)(128)(4,1)} %bitcast.322), calls=%async_computation.11 | async-start | bytes 8388608
  435.8 8.7 slice-start.12
  463.9 104.1 %copy-start.5 = (f32[256,2560]{1,0:T(8,128)S(1)}, f32[256,2560]{1,0:T(8,128)}, u32[]{:S(2)}) copy-start(f32[256,2560]{1,0:T(8,128)} %get-tuple-element.43) | copy-start | bytes 7864324
  581.6 9.6 copy-start.21
  627.5 98.9 %copy-start.35 = (f32[256]{0:T(256)S(1)}, f32[256]{0:T(256)}, u32[]{:S(2)}) copy-start(f32[256]{0:T(256)} %copy-done.34) | copy-start | bytes 3076
  627.5 98.9 %copy-start.41 = (f32[64]{0:T(128)S(1)}, f32[64]{0:T(128)}, u32[]{:S(2)}) copy-start(f32[64]{0:T(128)} %copy-done.40) | copy-start | bytes 772
  771.6 68.3 %copy-start.11 = (bf16[4,160,1280]{2,1,0:T(8,128)(2,1)S(1)}, bf16[4,160,1280]{2,1,0:T(8,128)(2,1)}, u32[]{:S(2)}) copy-start(bf16[4,160,1280]{2,1,0:T(8,128)(2,1)} %get-tuple-element.100) | copy-start | bytes 4915204
  847.7 51.5 %copy-start.20 = (bf16[2,2,4,80,1280]{4,3,2,1,0:T(8,128)(2,1)S(1)}, bf16[2,2,4,80,1280]{4,3,2,1,0:T(8,128)(2,1)}, u32[]{:S(2)}) copy-start(bf16[2,2,4,80,1280]{4,3,2,1,0:T(8,128)(2,1)} %get-tuple-element.59) | copy-start | bytes 9830404
  903.4 59.2 %copy-start.22 = (bf16[4,160,1280]{2,1,0:T(8,128)(2,1)S(1)}, bf16[4,160,1280]{2,1,0:T(8,128)(2,1)}, u32[]{:S(2)}) copy-start(bf16[4,160,1280]{2,1,0:T(8,128)(2,1)} %get-tuple-element.66) | copy-start | bytes 4915204
  (35 other events, 156.2 us)

commit v4 on v3

--- a/solution.py
+++ b/solution.py
@@ -501,6 +501,202 @@
     yield True
     for copy in copies:
         copy.wait()
+
+
+def add_blocks(out, more):
+    blocks, rows, _ = out.shape
+    steps = rows // 16
+
+    @pl.loop(0, blocks * steps)
+    def _(i):
+        n = lax.div(i, steps)
+        at = pl.ds(pl.multiple_of(lax.rem(i, steps) * 16, 16), 16)
+        out[n, at] = (out[n, at].astype(f32) + more[n, at].astype(f32)).astype(out.dtype)
+
+
+def scatter_buffers(rows, columns):
+    half = (2, LINE, rows // 2, columns)
+    return [((2,) + half, bf16)] + [(half, bf16)] * 3 + [((LINE, rows, columns), bf16)]
+
+
+SCATTER_SEMS = [
+    pltpu.SemaphoreType.DMA((6,)),
+    pltpu.SemaphoreType.DMA((6,)),
+    pltpu.SemaphoreType.DMA((8,)),
+    pltpu.SemaphoreType.DMA((4,)),
+    pltpu.SemaphoreType.DMA((4,)),
+]
+
+
+def scatter(me, src, done, buffers, here, there, sems):
+    got, kept, passed, got_two, total = buffers
+    snd, rcv, loc, line_snd, line_rcv = sems
+    half = src.shape[2] // 2
+    first, second = [], []
+    for h in range(2):
+        q = (me.xq, me.yq)[h]
+        rows = pl.ds(h * half, half)
+        for i in range(2):
+            n = 2 * h + i
+            view = src.at[:, (q, me.dq)[i], rows]
+            first.append(remote(view, got.at[h, i], snd.at[n], rcv.at[n], me.at(me.z, q)))
+        q = (me.yq, me.xq)[h]
+        second.append(
+            remote(passed.at[h], got_two.at[h], snd.at[4 + h], rcv.at[4 + h], me.at(me.z, q))
+        )
+    for copy in first:
+        copy.start()
+    yield
+    for copy in first:
+        copy.wait_recv()
+    loads, stores = [], []
+    for h in range(2):
+        for i in range(2):
+            n = 2 * h + i
+            view = src.at[:, (me.q, (me.yq, me.xq)[h])[i], pl.ds(h * half, half)]
+            loads.append(pltpu.make_async_copy(view, here.at[h, i], loc.at[n]))
+            loads.append(pltpu.make_async_copy(got.at[h, i], there.at[h, i], loc.at[4 + n]))
+            stores.append(
+                pltpu.make_async_copy(here.at[h, i], (kept, passed)[i].at[h], loc.at[n])
+            )
+    for copy in loads:
+        copy.start()
+    for copy in loads:
+        copy.wait()
+    for h in range(2):
+        for i in range(2):
+            add_blocks(here.at[h, i], there.at[h, i])
+    for copy in stores:
+        copy.start()
+    for copy in stores:
+        copy.wait()
+    for copy in second:
+        copy.start()
+    yield
+    for copy in second:
+        copy.wait_recv()
+    loads, stores = [], []
+    for h in range(2):
+        loads.append(pltpu.make_async_copy(kept.at[h], here.at[h, 0], loc.at[h]))
+        loads.append(pltpu.make_async_copy(got_two.at[h], there.at[h, 0], loc.at[4 + h]))
+        stores.append(
+            pltpu.make_async_copy(here.at[h, 0], total.at[:, pl.ds(h * half, half)], loc.at[h])
+        )
+    for copy in loads:
+        copy.start()
+    for copy in loads:
+        copy.wait()
+    for h in range(2):
+        add_blocks(here.at[h, 0], there.at[h, 0])
+    for copy in stores:
+        copy.start()
+    for copy in stores:
+        copy.wait()
+
+    def send(j):
+        z = me.order(j)
+        return remote(total.at[z], done.at[me.z], line_snd.at[z], line_rcv.at[me.z], me.at(z, me.q))
+
+    local = pltpu.make_async_copy(total.at[me.z], done.at[me.z], loc.at[7])
+    local.start()
+    for j in (3, 2, 1):
+        send(j).start()
+    yield True
+    for j in range(1, 4):
+        z = me.order(j)
+        remote(done.at[z], done.at[z], line_snd.at[z], line_rcv.at[z], me.at(z, me.q)).wait_recv()
+    local.wait()
+    for copy in first + second:
+        copy.wait_send()
+    for j in range(1, 4):
+        send(j).wait_send()
+
+
+FFN_SEMS = [
+    pltpu.SemaphoreType.DMA((3, 2)),
+    pltpu.SemaphoreType.DMA((3, 2)),
+    pltpu.SemaphoreType.DMA((3, 4)),
+    pltpu.SemaphoreType.DMA((3, 4)),
+    pltpu.SemaphoreType.DMA((3, 4)),
+]
+
+
+def ffn_scatter(me, order, kept, passed, got, total, done, here, there, sems):
+    snd, rcv, loc, line_snd, line_rcv = sems
+    half, columns = kept.shape[3:]
+
+    def cross(part):
+        return [
+            remote(
+                passed.at[h, part],
+                got.at[h, part],
+                snd.at[part, h],
+                rcv.at[part, h],
+                me.at(me.z, (me.yq, me.xq)[h]),
+            )
+            for h in range(2)
+        ]
+
+    def send(part, j):
+        z = me.order(j)
+        return remote(
+            total.at[part, z],
+            done.at[part, me.z],
+            line_snd.at[part, z],
+            line_rcv.at[part, me.z],
+            me.at(z, me.q),
+        )
+
+    def local(part):
+        return pltpu.make_async_copy(
+            total.at[part, me.z], done.at[part, me.z], line_snd.at[part, me.z]
+        )
+
+    for part in order:
+        for copy in cross(part):
+            copy.start()
+    yield
+    at = pl.ds(0, columns)
+    for part in order:
+        for copy in cross(part):
+            copy.wait_recv()
+        loads, stores = [], []
+        for h in range(2):
+            a, b = here.at[h, 0, :, :, at], there.at[h, 0, :, :, at]
+            loads.append(pltpu.make_async_copy(kept.at[h, part], a, loc.at[part, h]))
+            loads.append(pltpu.make_async_copy(got.at[h, part], b, loc.at[part, 2 + h]))
+            stores.append(
+                pltpu.make_async_copy(
+                    a, total.at[part, :, pl.ds(h * half, half)], loc.at[part, h]
+                )
+            )
+        for copy in loads:
+            copy.start()
+        for copy in loads:
+            copy.wait()
+        for h in range(2):
+            add_blocks(here.at[h, 0, :, :, at], there.at[h, 0, :, :, at])
+        for copy in stores:
+            copy.start()
+        for copy in stores:
+            copy.wait()
+        local(part).start()
+        for j in (3, 2, 1):
+            send(part, j).start()
+        yield
+    yield True
+    for part in order:
+        for j in range(1, 4):
+            z = me.order(j)
+            view = done.at[part, z]
+            remote(
+                view, view, line_snd.at[part, z], line_rcv.at[part, z], me.at(z, me.q)
+            ).wait_recv()
+        local(part).wait()
+        for copy in cross(part):
+            copy.wait_send()
+        for j in range(1, 4):
+            send(part, j).wait_send()
 
 
 def plane_sums_scratch(shape):
@@ -1052,36 +1248,6 @@
     )
     hidden_bias_part = jnp.pad(hidden_bias_part, ((0, 14), (0, 0))).astype(bf16)
 
-    def first_half(src, got):
-        lead = src.ndim - 3
-        half = rows_of(src)
-        xq, yq = q + 1 - 2 * (q % 2), q + 2 - 4 * (q // 2)
-
-        def own(place, h):
-            piece = lax.dynamic_index_in_dim(src, place, lead, keepdims=False)
-            return lax.slice_in_dim(piece, h * half, (h + 1) * half, axis=lead).astype(f32)
-
-        kept = [own(q, h) + got[h, 0].astype(f32) for h in range(2)]
-        passed = jnp.stack(
-            [
-                (own(yq, 0) + got[0, 1].astype(f32)).astype(bf16),
-                (own(xq, 1) + got[1, 1].astype(f32)).astype(bf16),
-            ]
-        )
-        return kept, passed
-
-    def rows_of(src):
-        return src.shape[-2] // 2
-
-    def second_half(kept, got):
-        return jnp.concatenate(
-            [kept[h].astype(f32) + got[h].astype(f32) for h in range(2)], axis=-2
-        ).astype(bf16)
-
-    def first_shape(src):
-        s = src.shape
-        return (2, 2) + s[:-3] + (s[-2] // 2, s[-1])
-
     def third_steps(me, ins, outs, sems):
         yield from ()
         one = reduce_line(me, ins[0], outs[0], sems[0])
@@ -1131,84 +1297,19 @@
     middle_part, gain_two_grad = norm_two_pull(normed_two_grad.astype(f32))
     middle_grad = cot_full + middle_part
     middle_low = middle_grad.astype(bf16)
-    out_term = dot(middle_low, mixed_low, 0, 0).astype(bf16)
-    out_term = out_term.reshape(LINE, 4, rows, heads * HD)
-    mixed_grad = dot(middle_low, out_full).astype(bf16).reshape(tokens, heads, HD)
-
-    scores_again = jnp.einsum("qhd,kd->hqk", query_heads, key_win, preferred_element_type=f32)
-    probs_again = jnp.where(visible[None], jnp.exp(scores_again - log_total), 0.0)
-    probs_again_low = probs_again.astype(bf16)
-    prob_grad = jnp.einsum("qhd,kd->hqk", mixed_grad, value_win, preferred_element_type=f32)
-    value_grad = jnp.einsum("hqk,qhd->kd", probs_again_low, mixed_grad, preferred_element_type=f32)
-    row_inner = jnp.sum(probs_again * prob_grad, axis=-1, keepdims=True)
-    score_grad = (probs_again * (prob_grad - row_inner)).astype(bf16)
-    query_grad_raw = jnp.einsum(
-        "hqk,kd->qhd", score_grad, key_win, preferred_element_type=f32
-    ).reshape(tokens, heads * HD)
-    key_grad_raw = jnp.einsum("hqk,qhd->kd", score_grad, query_heads, preferred_element_type=f32)
-    window_grad = (
-        jnp.concatenate([key_grad_raw, value_grad], axis=1)
-        .reshape(reach + 1, tokens, 2 * HD)
-        .astype(bf16)
-    )
-
-    def fourth_steps(me, ins, outs, sems):
-        return [
-            reduce_window(me, reach, ins[0], outs[0], sems[0]),
-            plane_second(me, ins[1], outs[1], sems[1]),
-            plane_first(me, ins[2], outs[2], sems[2]),
-        ]
-
-    own_grad, ffn_got, out_got = transfer(
-        5,
-        [window_grad, ffn_passed, out_term],
-        [
-            ((tokens, 2 * HD), f32),
-            (ffn_passed.shape, bf16),
-            (first_shape(out_term), bf16),
-        ],
-        [
-            reduce_scratch(reach + 1, tokens // 2, 2 * HD, f32),
-            PLANE_SEMS,
-            PLANE_SEMS,
-        ],
-        fourth_steps,
-        whole=True,
-    )
-    output = (middle + mlp_out.astype(f32) + bias_down).astype(bf16)
-    ffn_sum = second_half(ffn_kept, ffn_got)
-    out_kept, out_passed = first_half(out_term, out_got)
-    key_lin_grad = rotate(own_grad[:, :HD], places, 1, -1.0)
-    kv_grad_low = jnp.concatenate([key_lin_grad, own_grad[:, HD:]], axis=1).astype(bf16)
-    query_lin_grad = (rotate(query_grad_raw, places, heads, -1.0) * scale_factor).astype(bf16)
-    normed_grad = both_cores(6, dot(query_lin_grad, query_full, 1, 1).astype(bf16)) + dot(
-        kv_grad_low, kv_full, 1, 1
-    )
-    _, norm_one_pull = jax.vjp(normalize, stream, gain_one)
-    stream_part, gain_one_grad = norm_one_pull(normed_grad)
-    input_grad = middle_grad + stream_part
-    query_term = dot(normed, query_lin_grad, 0, 0).astype(bf16)
-    query_term = query_term.reshape(LINE, 4, rows, heads * HD)
-
-    def take_core(full, axis):
-        blocks = lax.dynamic_index_in_dim(full, t, axis, keepdims=False)
+
+    def core_features(full):
+        blocks = full.reshape(full.shape[0], RING, groups, 2, -1)
+        blocks = lax.dynamic_index_in_dim(blocks, t, 3, keepdims=False)
         return jnp.moveaxis(blocks, 1, 0).reshape(RING, full.shape[0], -1)
-
-    def core_features(full):
-        return take_core(full.reshape(full.shape[0], RING, groups, 2, -1), 3)
 
     def core_hidden(full):
         blocks = full.reshape(full.shape[0], groups, RING, 2, -1)
-        return take_core(jnp.swapaxes(blocks, 1, 2), 3)
-
-    kv_term = dot(normed, kv_grad_low, 0, 0)
-    kv_term = lax.dynamic_index_in_dim(
-        kv_term.reshape(RING, groups, 2, -1, columns), t, 2, keepdims=False
-    ).reshape(RING, kv_rows, columns)
+        blocks = lax.dynamic_index_in_dim(blocks, t, 3, keepdims=False)
+        return jnp.transpose(blocks, (2, 0, 1, 3)).reshape(RING, full.shape[0], -1)
+
     vector_terms = core_features(
-        jnp.stack(
-            [gain_one_grad, jnp.sum(middle_grad, axis=0), gain_two_grad, jnp.sum(cot_full, axis=0)]
-        )
+        jnp.stack([jnp.sum(middle_grad, axis=0), gain_two_grad, jnp.sum(cot_full, axis=0)])
     )
     bias_pair = jnp.where(
         t == 0,
@@ -1216,87 +1317,346 @@
         jnp.stack([bias_theirs, hidden_bias_part]),
     )[:, :2].astype(f32)
     bias_terms = jnp.zeros((2, 2, hidden_half), f32)
-    start = jnp.minimum(z * block, hidden_half - block)
-    bias_terms = lax.dynamic_update_slice_in_dim(bias_terms, bias_pair, start, 2)
+    bias_terms = lax.dynamic_update_slice_in_dim(bias_terms, bias_pair, block_start, 2)
     bias_terms = core_hidden(jnp.swapaxes(bias_terms, 0, 1).reshape(2, -1))
 
     def widen(x):
-        return jnp.pad(x, ((0, 0), (0, 0), (0, columns - x.shape[2])))
-
-    kv_term = jnp.concatenate(
-        [kv_term, widen(vector_terms), widen(bias_terms), jnp.zeros((RING, 10, columns), f32)],
-        axis=1,
+        return jnp.pad(x, ((0, 0), (0, 0), (0, HD - x.shape[2])))
+
+    small_terms = jnp.concatenate(
+        [widen(vector_terms), widen(bias_terms), jnp.zeros((RING, 27, HD), f32)], axis=1
     ).astype(bf16)
-    kv_term = kv_term.reshape(LINE, 4, kv_rows + 16, columns)
-
-    def fifth_steps(me, ins, outs, sems):
-        return [
-            line_exchange(me, lambda z: ins[0].at[:, z], outs[0], sems[0]),
-            plane_second(me, ins[1], outs[1], sems[1]),
-            plane_first(me, ins[2], outs[2], sems[2]),
-            plane_first(me, ins[3], outs[3], sems[3]),
+
+    frequency = 10000.0 ** (-jnp.arange(HD // 4, dtype=f32) / (HD // 4))
+    angles = places.astype(f32)[:, None] * frequency[None, :]
+    turn_cos = jnp.concatenate([jnp.cos(angles), jnp.cos(angles)], axis=1)
+    turn_sin = jnp.concatenate([-jnp.sin(angles), jnp.sin(angles)], axis=1)
+    chunk = 3 if (reach + 1) % 3 == 0 else 1
+    pieces = (reach + 1) // chunk
+    kv_size = rows + small_terms.shape[1]
+    vector_rows = -(-width // (LANES * 32)) * 32
+
+    def fourth_steps(me, ins, outs, groups_in):
+        (
+            low_in, out_in, mixed_in, q_in, kv_in, logs_in, normed_in, query_in, kvw_in,
+            kept_in, passed_in, small_in, grad_in, x_in,
+            marks_row, marks_column, cos2, sin2, gain,
+        ) = ins
+        ffn_done, out_done, query_done, kv_done, input_out, gain_all = outs[:6]
+        out_term, query_term, kv_term, ffn_got, ffn_total = outs[6:11]
+        out_buffers, query_buffers, kv_buffers = outs[11:16], outs[16:21], outs[21:26]
+        (
+            ffn_sems, out_sems, query_sems, kv_sems, window_scratch, swap_sems, last_sems,
+            vector_sems, scratch,
+        ) = groups_in
+        (
+            low, weight, mixed, qs, win, normed_v, logs, mixed_grad, q_grad, window_sum, mask,
+            kv_total, kv_low, kvw, stage, kv_stage, here, there, kv_here, kv_there, part, theirs,
+            gain_sum, gain_rows, gain_low, loads,
+        ) = scratch
+
+        def load(n, src, dst):
+            return pltpu.make_async_copy(src, dst, loads.at[n])
+
+        def turn(v, direction):
+            first = v[:, : HD // 2]
+            turned = first * cos2[...] + direction * (pltpu.roll(first, HD // 4, 1) * sin2[...])
+            return jnp.concatenate([turned, v[:, HD // 2 :]], axis=1)
+
+        part_rows = 4 * rows
+
+        def part_columns(i):
+            return pl.ds(pl.multiple_of(i * part_rows, LANES), part_rows)
+
+        ffn = ffn_scatter(
+            me, (2, 0, 1), kept_in, passed_in, ffn_got, ffn_total, ffn_done, here, there, ffn_sems
+        )
+        outw = scatter(me, out_term, out_done, out_buffers, here, there, out_sems)
+        query = scatter(me, query_term, query_done, query_buffers, here, there, query_sems)
+        kvw_steps = scatter(
+            me, kv_term, kv_done.at[me.t], kv_buffers, kv_here, kv_there, kv_sems
+        )
+        next(ffn)
+        start = jnp.maximum(me.r - reach, 0)
+        first_loads = [
+            load(0, low_in, low),
+            load(1, mixed_in, mixed),
+            load(2, out_in, weight),
+            load(3, q_in, qs),
+            load(4, kv_in.at[pl.ds(start, reach + 1)], win),
+            load(5, logs_in, logs),
+            load(6, normed_in, normed_v),
+            load(7, kvw_in, kvw),
         ]
-
-    ffn_done, out_got, query_got, kv_got = transfer(
-        7,
-        [ffn_sum, out_passed, query_term, kv_term],
+        for copy in first_loads:
+            copy.start()
+        first_loads[0].wait()
+        first_loads[1].wait()
+
+        def weight_term(left, right, term):
+            @pl.loop(0, LINE)
+            def _(i):
+                value = dot(left[:, part_columns(i)], right[...], 0, 0).astype(bf16)
+                stage[...] = value.reshape(stage.shape)
+                copy = load(8, stage, term.at[i])
+                copy.start()
+                copy.wait()
+
+        weight_term(low, mixed, out_term)
+        next(outw)
+        first_loads[2].wait()
+
+        @pl.loop(0, heads)
+        def _(h):
+            at = pl.ds(pl.multiple_of(h * HD, HD), HD)
+            mixed_grad[:, at] = dot(low[...], weight[:, at]).astype(bf16)
+
+        load(2, query_in, weight).start()
+        load(0, x_in, low).start()
+        row_places = me.r * tokens + lax.broadcasted_iota(jnp.int32, (tokens, 1), 0)
+
+        @pl.loop(0, reach + 1)
+        def _(i):
+            at = pl.ds(pl.multiple_of(i * tokens, tokens), tokens)
+            key_places = (start + i) * tokens + lax.broadcasted_iota(jnp.int32, (1, tokens), 1)
+            gap = row_places - key_places
+            seen = (gap >= 0) & (gap < W) & (marks_column[...] == marks_row[:, at])
+            mask[:, at] = jnp.where(seen, 0.0, -1e30)
+            window_sum[i] = jnp.zeros((tokens, 2 * HD), f32)
+
+        for copy in first_loads[3:]:
+            copy.wait()
+
+        @pl.loop(0, heads)
+        def _(h):
+            at = pl.ds(pl.multiple_of(h * HD, HD), HD)
+            q_head = qs[:, at]
+            grad = mixed_grad[:, at]
+            inner = jnp.sum(grad.astype(f32) * mixed[:, at].astype(f32), axis=1, keepdims=True)
+            log = logs[h]
+            q_sum = jnp.zeros((tokens, HD), f32)
+            for c in range(pieces):
+                blocks = pl.ds(c * chunk, chunk)
+                both = win[blocks].reshape(chunk * tokens, 2 * HD)
+                k, v = both[:, :HD], both[:, HD:]
+                span_at = pl.ds(c * chunk * tokens, chunk * tokens)
+                probs = jnp.exp(dot(q_head, k, 1, 1) + mask[:, span_at] - log)
+                value_sum = dot(probs.astype(bf16), grad, 0, 0)
+                score_grad = (probs * (dot(grad, v, 1, 1) - inner)).astype(bf16)
+                q_sum += dot(score_grad, k)
+                key_sum = dot(score_grad, q_head, 0, 0)
+                window_sum[blocks, :, :HD] += key_sum.reshape(chunk, tokens, HD)
+                window_sum[blocks, :, HD:] += value_sum.reshape(chunk, tokens, HD)
+            q_grad[:, at] = (turn(q_sum, -1.0) * scale_factor).astype(bf16)
+            for i in (2, 4):
+
+                @pl.when(h == i)
+                def _():
+                    next(ffn)
+
+        @pl.loop(0, reach + 1)
+        def _(i):
+            win[i] = window_sum[i].astype(bf16)
+
+        window_steps = reduce_window(me, reach, win, kv_total, window_scratch)
+        next(window_steps)
+        load(5, grad_in, mask).start()
+        weight_term(normed_v, q_grad, query_term)
+        next(query)
+        load(2, query_in, weight).wait()
+
+        @pl.loop(0, LINE)
+        def _(i):
+            piece = weight[pl.ds(pl.multiple_of(i * part_rows, LANES), part_rows)]
+            part[:, part_columns(i)] = dot(q_grad[...], piece, 1, 1).astype(bf16)
+
+        swapped = remote(part, theirs, swap_sems[0], swap_sems[1], me.other())
+        swapped.start()
+        next(window_steps)
+        next(outw)
+        next(ffn)
+        next(window_steps)
+        next(window_steps, None)
+
+        kv_low[:, :HD] = turn(kv_total[:, :HD], -1.0).astype(bf16)
+        kv_low[:, HD:] = kv_total[:, HD:].astype(bf16)
+        ours_at = pl.ds(pl.multiple_of(me.t * HD, HD), HD)
+        small_copy = load(0, x_in, low)
+        small_copy.wait()
+
+        @pl.loop(0, LINE)
+        def _(i):
+            value = dot(normed_v[:, part_columns(i)], kv_low[:, ours_at], 0, 0).astype(bf16)
+            kv_stage[:, pl.ds(0, rows)] = value.reshape(4, rows, HD)
+            copy = load(9, small_in.at[pl.ds(4 * i, 4)], kv_stage.at[:, pl.ds(rows, kv_size - rows)])
+            copy.start()
+            copy.wait()
+            copy = load(9, kv_stage, kv_term.at[i])
+            copy.start()
+            copy.wait()
+
+        next(kvw_steps)
+        next(outw)
+        next(query)
+
+        swapped.wait()
+
+        @pl.loop(0, width // (2 * HD))
+        def _(i):
+            at = pl.ds(pl.multiple_of(i * 2 * HD, 2 * HD), 2 * HD)
+            more = dot(kv_low[...], kvw[at], 1, 1)
+            window_sum[i] = part[:, at].astype(f32) + theirs[:, at].astype(f32) + more
+
+        gain_sum[...] = jnp.zeros(gain_sum.shape, f32)
+        load(5, grad_in, mask).wait()
+
+        @pl.loop(0, tokens // 16)
+        def _(i):
+            at = pl.ds(pl.multiple_of(i * 16, 16), 16)
+            grad = jnp.concatenate([window_sum[n, at] for n in range(width // (2 * HD))], axis=1)
+            stream_rows = low[at].astype(f32)
+            scale = lax.rsqrt(
+                jnp.mean(stream_rows * stream_rows, axis=1, keepdims=True) + epsilon
+            )
+            unit = stream_rows * scale
+            gain_sum[...] += grad * unit
+            scaled = grad * gain[...]
+            inner = jnp.mean(scaled * unit, axis=1, keepdims=True)
+            mask[at] = mask[at] + scale * (scaled - unit * inner)
+
+        load(5, mask, input_out).start()
+        gain_rows[...] = jnp.zeros(gain_rows.shape, f32)
+        gain_total = jnp.sum(gain_sum[...], axis=0, keepdims=True)
+        for i in range(width // LANES):
+            gain_rows[pl.ds(i, 1)] = gain_total[:, i * LANES : (i + 1) * LANES]
+        gain_low[...] = gain_rows[...].astype(bf16)
+
+        def gain_send(k):
+            to = (me.base + lax.rem(me.r + k, RING), me.t)
+            return remote(
+                gain_low, gain_all.at[me.r], vector_sems[0].at[k], vector_sems[1].at[me.r], to
+            )
+
+        keep_gain = load(9, gain_low, gain_all.at[me.r])
+        keep_gain.start()
+
+        @pl.loop(1, RING)
+        def _(k):
+            gain_send(k).start()
+
+        next(kvw_steps)
+        next(query)
+        next(kvw_steps)
+        for step in (ffn, outw, query, kvw_steps):
+            for _ in step:
+                pass
+        mine = kv_done.at[me.t]
+        last = remote(mine, mine, last_sems[0], last_sems[1], me.other())
+        last.start()
+
+        @pl.loop(1, RING)
+        def _(k):
+            gain_send(k).wait_send()
+            source = lax.rem(me.r + k, RING)
+            landed = gain_all.at[source]
+            remote(
+                landed, landed, vector_sems[0].at[k], vector_sems[1].at[source], me.at(me.z, me.q)
+            ).wait_recv()
+
+        keep_gain.wait()
+        load(5, mask, input_out).wait()
+        last.wait()
+        return []
+
+    term_shape = (LINE, 4, rows, heads * HD)
+    ffn_shape = (3, LINE, rows, block)
+    half = (2, 2, LINE, rows // 2, heads * HD)
+    kv_half = (2, 2, LINE, kv_size // 2, HD)
+    ffn_done, out_done, query_done, kv_done, input_grad, gain_all = transfer(
+        5,
         [
-            ((LINE, 3, rows, block), bf16),
-            (out_passed.shape, bf16),
-            (first_shape(query_term), bf16),
-            (first_shape(kv_term), bf16),
+            middle_low, out_full, mixed_low, queries, kv_all, log_total, normed, query_full, kv_full,
+            ffn_kept, ffn_passed, small_terms, middle_grad, inputs,
+            window_marks[None], own_marks[:, None], turn_cos, turn_sin, gain_one[None],
         ],
-        [LINE_SEMS, PLANE_SEMS, PLANE_SEMS, PLANE_SEMS],
-        fifth_steps,
-    )
-    out_sum = second_half(out_kept, out_got)
-    query_kept, query_passed = first_half(query_term, query_got)
-    kv_kept, kv_passed = first_half(kv_term, kv_got)
-
-    def sixth_steps(me, ins, outs, sems):
-        return [
-            line_exchange(me, lambda z: ins[0].at[z], outs[0], sems[0]),
-            plane_second(me, ins[1], outs[1], sems[1]),
-            plane_second(me, ins[2], outs[2], sems[2]),
+        [
+            (ffn_shape, bf16),
+            ((LINE, rows, heads * HD), bf16),
+            ((LINE, rows, heads * HD), bf16),
+            ((2, LINE, kv_size, HD), bf16),
+            (inputs.shape, f32),
+            ((RING, vector_rows, LANES), bf16),
+            (term_shape, bf16),
+            (term_shape, bf16),
+            ((LINE, 4, kv_size, HD), bf16),
+            (kept_shape, bf16),
+            (ffn_shape, bf16),
         ]
-
-    out_done, query_got, kv_got = transfer(
-        8,
-        [out_sum, query_passed, kv_passed],
-        [(out_sum.shape, bf16), (query_passed.shape, bf16), (kv_passed.shape, bf16)],
-        [LINE_SEMS, PLANE_SEMS, PLANE_SEMS],
-        sixth_steps,
-    )
-    query_sum = second_half(query_kept, query_got)
-    kv_sum = second_half(kv_kept, kv_got)
-
-    def last_steps(me, ins, outs, sems):
-        return [
-            line_exchange(me, lambda z: ins[0].at[z], outs[0], sems[0]),
-            line_exchange(me, lambda z: ins[1].at[z], outs[1], sems[1]),
-        ]
-
-    query_done, kv_done = transfer(
-        9,
-        [query_sum, kv_sum],
-        [(query_sum.shape, bf16), (kv_sum.shape, bf16)],
-        [LINE_SEMS, LINE_SEMS],
-        last_steps,
-    )
+        + scatter_buffers(rows, heads * HD) * 2
+        + scatter_buffers(kv_size, HD),
+        [
+            FFN_SEMS,
+            SCATTER_SEMS,
+            SCATTER_SEMS,
+            SCATTER_SEMS,
+            reduce_scratch(reach + 1, tokens // 2, 2 * HD, f32),
+            SWAP_SEMS,
+            SWAP_SEMS,
+            [pltpu.SemaphoreType.DMA((RING,)), pltpu.SemaphoreType.DMA((RING,))],
+            [
+                pltpu.VMEM(inputs.shape, bf16),
+                pltpu.VMEM(out_full.shape, bf16),
+                pltpu.VMEM(queries.shape, bf16),
+                pltpu.VMEM(queries.shape, bf16),
+                pltpu.VMEM((reach + 1, tokens, 2 * HD), bf16),
+                pltpu.VMEM(inputs.shape, bf16),
+                pltpu.VMEM((heads, tokens, 1), f32),
+                pltpu.VMEM(queries.shape, bf16),
+                pltpu.VMEM(queries.shape, bf16),
+                pltpu.VMEM((reach + 1, tokens, 2 * HD), f32),
+                pltpu.VMEM(inputs.shape, f32),
+                pltpu.VMEM((tokens, 2 * HD), f32),
+                pltpu.VMEM((tokens, 2 * HD), bf16),
+                pltpu.VMEM(kv_full.shape, bf16),
+                pltpu.VMEM((4, rows, heads * HD), bf16),
+                pltpu.VMEM((4, kv_size, HD), bf16),
+                pltpu.VMEM(half, bf16),
+                pltpu.VMEM(half, bf16),
+                pltpu.VMEM(kv_half, bf16),
+                pltpu.VMEM(kv_half, bf16),
+                pltpu.VMEM(inputs.shape, bf16),
+                pltpu.VMEM(inputs.shape, bf16),
+                pltpu.VMEM((16, width), f32),
+                pltpu.VMEM((vector_rows, LANES), f32),
+                pltpu.VMEM((vector_rows, LANES), bf16),
+                pltpu.SemaphoreType.DMA((10,)),
+            ],
+        ],
+        fourth_steps,
+        whole=True,
+        near=(14, 15, 16, 17, 18),
+    )[:6]
+    output = (middle + mlp_out.astype(f32) + bias_down).astype(bf16)
 
     last_skip = LINE * block - hidden_half
     ffn_grad = jnp.concatenate(
-        [ffn_done[i] for i in range(LINE - 1)] + [ffn_done[LINE - 1, :, :, last_skip:]], axis=2
+        [ffn_done[:, i] for i in range(LINE - 1)] + [ffn_done[:, LINE - 1, :, last_skip:]], axis=2
     )
     ffn_grad = shrink(ffn_grad.astype(f32), 1, groups)
     out_grad = shrink(jnp.sum(out_done.astype(f32), axis=0), 0, groups).T
     query_grad = shrink(jnp.sum(query_done.astype(f32), axis=0), 0, groups)
-    kv_sums = jnp.sum(kv_done.astype(f32), axis=0)
-    key_value_grad = shrink(kv_sums[:kv_rows], 0, groups)
-    small_grads = [shrink(kv_sums[kv_rows + i, :kv_rows], 0, groups) for i in range(4)]
-    gate_up_bias_grad = shrink(
-        kv_sums[kv_rows + 4 : kv_rows + 6, : hidden_bias.shape[1]], 1, groups
-    )
+    kv_sums = jnp.sum(kv_done.astype(f32), axis=1)
+    small_sums = lax.dynamic_index_in_dim(kv_sums[:, rows:], t, 0, keepdims=False)
+    kv_grad = jnp.concatenate([kv_sums[0, :rows], kv_sums[1, :rows]], axis=1)
+    kv_grad = lax.dynamic_index_in_dim(kv_grad.reshape(groups, 2, -1, columns), t, 1, keepdims=False)
+    key_value_grad = shrink(kv_grad.reshape(kv_rows, columns), 0, groups)
+    gain_sum = jnp.sum(gain_all[:, : width // LANES].astype(f32), axis=0).reshape(
+        RING, groups, 2, kv_rows // groups
+    )
+    gain_sum = lax.dynamic_index_in_dim(gain_sum, r, 0, keepdims=False)
+    gain_sum = lax.dynamic_index_in_dim(gain_sum, t, 1, keepdims=False).reshape(kv_rows)
+    small_grads = [shrink(v, 0, groups) for v in [gain_sum] + [small_sums[i, :kv_rows] for i in range(3)]]
+    gate_up_bias_grad = shrink(small_sums[3:5, : hidden_bias.shape[1]], 1, groups)
     return (
         from_places(output, groups),
         from_places(input_grad, groups),

time: 974 us -> 832 us (0.85)
  matrix products: 143 us -> 88.8 us
  Pallas kernels: 707 us -> 665 us
  local copies, waits for them, and re-layouts: 57.1 us -> 30.5 us
  other arithmetic: 61.1 us -> 36.7 us
    pallas_call x8 -> x4, Pallas kernels: 707 us -> 665 us  [transfer(): pl.pallas_call(kernel, out_shape=[jax.ShapeDtypeStruct(shape, dtype) for...]
    dot_general x5 -> x0, matrix products: 32.4 us -> none  [the longest x1 8.1 us: body(): jnp.einsum('qhd,kd->hqk', mixed_grad, value_win, preferred_element_type=f32)]
    dot_general x17 -> x11, matrix products: 110 us -> 88.8 us  [dot(): lax.dot_general(a, b, (((ca,), (cb,)), ((), ())), preferred_element_type=...]
    another operation x13 -> x2, other arithmetic: 11.1 us -> 1.27 us
where the time goes in v4:
time: 832 us; the launch traced here: 823 us
  Pallas kernels  665 us (80%)
  matrix products  88.8 us (11%)
  other arithmetic  36.7 us (4%)
  local copies, waits for them, and re-layouts  30.5 us (4%)
    pallas_call x4, Pallas kernels, transfer(): pl.pallas_call(kernel, out_shape=[jax.ShapeDtypeStruct(shape, dtype) for...  665 us
    dot_general x11, matrix products, dot(): lax.dot_general(a, b, (((ca,), (cb,)), ((), ())), preferred_element_type=...  88.8 us

profile of v4, /device:TPU:0, one launch (start us, length us, event | category | flops | bytes accessed | tf_op | source)
XLA Modules:
  0.0 822.9 jit_solution(11243968411391270781)
XLA Ops:
  0.9 1.8 fusion.11
  7.1 91.9 %shard_map.220 = (bf16[16,160,1280]{2,1,0:T(8,128)(2,1)}, bf16[16,2,80,512]{3,2,1,0:T(8,128)(2,1)}, bf16[16,2,16,512]{3,2,1,0:T(8,128)(2,1)}, bf16[4,256,2560]{2,1,0:T(8,128)(2,1)}) custom-call(bf16[160,1280]{1,0:T(8,128)(2,1)} %refs_0_.1, bf16[80,512]{1,0:T(8,128)(2,1)} %refs_1_.1, bf16[16,512]{1,0:T(8,128)(2,1)} %fusion.44.refs_2_, bf16[256,2560]{1,0:T(8,128)(2,1)} %refs_3_.1), custom_call_target="tpu_custom_call" | custom-call | tf_op jit(solution)/shard_map/pallas_call | solution.py:829
  107.3 3.0 fusion.73
  111.9 9.7 %copy.46 = bf16[1280,2560]{1,0:T(8,128)(2,1)} copy(bf16[1280,2560]{0,1:T(8,128)(2,1)} %bitcast.103) | data formatting | bytes 13107200 | tf_op jit(solution)/shard_map/dot_general | solution.py:912
  121.6 4.8 fusion.16
  127.8 236.5 %shard_map.221 = (bf16[16,256,512]{2,1,0:T(8,128)(2,1)}, bf16[16,160,1280]{2,1,0:T(8,128)(2,1)}, bf16[3,16,160,1024]{3,2,1,0:T(8,128)(2,1)}, bf16[256,1280]{1,0:...) custom-call(bf16[256,512]{1,0:T(8,128)(2,1)} %pad_maximum_fusion.1.refs_0_, ...), custom_call_target="tpu_custom_call" | custom-call | tf_op jit(solution)/shard_map/pallas_call | solution.py:829
  364.3 6.7 fusion.70
  371.3 8.0 fusion.74
  379.4 8.6 %select_convert_fusion = (bf16[1024,1024]{1,0:T(8,128)(2,1)}, f32[1024,1024]{1,0:T(8,128)}) fusion(f32[1024]{0:T(1024)S(1)} %bitcast.133, pred[1024]{0:T(1024)(128)(4,1)S(1)} %iota_compare_fusion.8, f32[1024,1024]{1,0:T(8,128)S(1)} %fusion.74, f32[1024]{0:T(1024)S(1)} %bitcast.135, bf16[1024,2560]{1,0:T(8,128)(2,1)S(1)} %bitcast.147, ...), kind=kOutput, calls=%fused_computation.16 | convolution fusion | flops 5382340608 | bytes 20980736 | tf_op jit(solution)/shard_map/dot_general | solution.py:912
  387.9 13.6 %fusion.69 = (bf16[1024]{0:T(1024)(128)(2,1)S(1)}, bf16[1024,1024]{1,0:T(8,128)(2,1)S(1)}, bf16[1024]{0:T(1024)(128)(2,1)S(1)}, bf16[1024,1024]{1,0:T(8,128)(2,1)}) fusion(f32[1024,1024]{1,0:T(8,128)S(1)} %fusion.74, f32[1024]{0:T(1024)S(1)} %bitcast.136, pred[1024]{0:T(1024)(128)(4,1)S(1)} %iota_compare_fusion.8, f32[1024,1024]{1,0:T(8,128)} %get-tuple-element.100, ...), kind=kOutput, calls=%fused_computation.161 | convolution fusion | flops 5400164352 | bytes 23081984 | tf_op jit(solution)/shard_map/dot_general | solution.py:912
  401.6 9.2 %convolution_convert_fusion.3 = bf16[1024,2560]{1,0:T(8,128)(2,1)} fusion(bf16[1024,1024]{1,0:T(8,128)(2,1)} %get-tuple-element.99, bf16[2560,1024]{1,0:T(8,128)(2,1)S(1)} %bitcast.114), kind=kOutput, calls=%fused_computation.7 | convolution fusion | flops 5371330560 | bytes 12582912 | tf_op jit(solution)/shard_map/dot_general | solution.py:912
  410.7 8.5 %convolution_convert_fusion = bf16[2560,1024]{1,0:T(8,128)(2,1)S(1)} fusion(bf16[1024,2560]{1,0:T(8,128)(2,1)} %bitcast.142, bf16[1024,1024]{1,0:T(8,128)(2,1)S(1)} %copy-done.11), kind=kOutput, calls=%fused_computation.4 | convolution fusion | flops 5371330560 | bytes 12582912 | tf_op jit(solution)/shard_map/dot_general | solution.py:912
  419.9 6.0 convolution_convert_fusion.1
  425.9 8.8 %convolution_convert_fusion.2 = bf16[2560,1024]{1,0:T(8,128)(2,1)S(1)} fusion(bf16[1024,2560]{1,0:T(8,128)(2,1)} %bitcast.144, bf16[1024,1024]{1,0:T(8,128)(2,1)S(1)} %copy-done.10), kind=kOutput, calls=%fused_computation.6 | convolution fusion | flops 5371330560 | bytes 12582912 | tf_op jit(solution)/shard_map/dot_general | solution.py:912
  434.8 6.7 pad_maximum_fusion.refs_2_
  441.5 8.2 %fusion.75 = f32[1024,2560]{1,0:T(8,128)} fusion(bf16[1024,1024]{1,0:T(8,128)(2,1)S(1)} %copy-done.10, bf16[2560,1024]{1,0:T(8,128)(2,1)S(1)} %bitcast.112), kind=kOutput, calls=%fused_computation.167 | convolution fusion | flops 5368709120 | bytes 17825792 | tf_op jit(solution)/shard_map/dot_general | solution.py:912
  449.7 10.0 %add_convert_fusion = bf16[1024,2560]{1,0:T(8,128)(2,1)} fusion(f32[1024,2560]{1,0:T(8,128)} %fusion.75, bf16[1024,1024]{1,0:T(8,128)(2,1)S(1)} %get-tuple-element.70, bf16[2560,1024]{1,0:T(8,128)(2,1)S(1)} %bitcast.110), kind=kOutput, calls=%fused_computation.1 | convolution fusion | flops 5373952000 | bytes 23068672 | tf_op jit(solution)/shard_map/dot_general | solution.py:912
  459.7 103.9 %shard_map.222 = (bf16[256,2560]{1,0:T(8,128)(2,1)}, bf16[256,2560]{1,0:T(8,128)(2,1)}, bf16[2,3,4,80,1024]{4,3,2,1,0:T(8,128)(2,1)}, bf16[2,3,4,80,1024]{4,3,2,1,0:T(8,128)(2,1)}, bf16[16,1024]{1,0:T(8,128)(2,1)}) custom-call(bf16[4,256,2560]{2,1,0:T(8,128)(2,1)} %bitcast.108, bf16[4,256,2560]{2,1,0:T(8,128)(2,1)} %bitcast.107, ...), custom_call_target="tpu_custom_call" | custom-call | tf_op jit(solution)/shard_map/pallas_call | solution.py:829
  565.2 2.4 fusion.14
  567.6 4.2 fusion.66
  574.5 233.0 %shard_map.223 = (bf16[3,4,160,1024]{3,2,1,0:T(8,128)(2,1)}, bf16[4,160,1280]{2,1,0:T(8,128)(2,1)}, bf16[4,160,1280]{2,1,0:T(8,128)(2,1)}, bf16[2,4,192,256]{3,2...) custom-call(bf16[256,2560]{1,0:T(8,128)(2,1)} %convert_element_type., ...), custom_call_target="tpu_custom_call" | custom-call | tf_op jit(solution)/shard_map/pallas_call | solution.py:829
  816.2 1.6 convert_bitcast_fusion
  818.4 2.6 slice.175
  821.2 1.5 copy.70
  (121 shorter events, 30.2 us)
Async XLA Ops:
  0.6 106.3 %copy-start.3 = (bf16[256,2560]{1,0:T(8,128)(2,1)S(1)}, bf16[256,2560]{1,0:T(8,128)(2,1)}, u32[]{:S(2)}) copy-start(bf16[256,2560]{1,0:T(8,128)(2,1)} %refs_13_.1) | copy-start | bytes 3932164
  107.3 14.2 %copy-start.4 = (bf16[256,2560]{1,0:T(8,128)(2,1)}, bf16[256,2560]{1,0:T(8,128)(2,1)S(1)}, u32[]{:S(2)}) copy-start(bf16[256,2560]{1,0:T(8,128)(2,1)S(1)} %fusion.13.refs_6_) | copy-start | bytes 3932164
  364.3 6.7 copy-start.1
  371.0 8.3 %slice-start = ((s8[5242880]{0:T(1024)(128)(4,1)}), s8[4194304]{0:T(1024)(128)(4,1)S(1)}, s32[]{:S(2)}) async-start(s8[5242880]{0:T(1024)(128)(4,1)} %bitcast.145), calls=%async_computation | async-start | bytes 8388608
  371.3 8.0 slice-start.1
  401.6 9.2 %copy-start.11 = (bf16[1024,1024]{1,0:T(8,128)(2,1)S(1)}, bf16[1024,1024]{1,0:T(8,128)(2,1)}, u32[]{:S(2)}) copy-start(bf16[1024,1024]{1,0:T(8,128)(2,1)} %get-tuple-element.99) | copy-start | bytes 6291460
  401.6 18.3 %slice-start.2 = ((s8[5242880]{0:T(1024)(128)(4,1)}), s8[1048576]{0:T(1024)(128)(4,1)S(1)}, s32[]{:S(2)}) async-start(s8[5242880]{0:T(1024)(128)(4,1)} %bitcast.148), calls=%async_computation.2 | async-start | bytes 2097152
  410.7 9.2 %slice-start.3 = ((s8[5242880]{0:T(1024)(128)(4,1)}), s8[4194304]{0:T(1024)(128)(4,1)S(1)}, s32[]{:S(2)}) async-start(s8[5242880]{0:T(1024)(128)(4,1)} %bitcast.148), calls=%async_computation.3 | async-start | bytes 8388608
  419.9 6.0 copy-start.10
  565.1 2.5 copy-start.2
  565.1 2.5 copy-start.5
  571.8 2.8 copy-start
  807.5 6.2 copy-start.9
  807.5 7.3 copy-start.8
  809.2 6.7 copy-start.6
  818.3 2.9 copy-start.7

commit v5 on v4

--- a/solution.py
+++ b/solution.py
@@ -329,12 +329,12 @@
     ]
 
 
-def chain_scratch(rows, columns):
+def line_sum_scratch(rows, columns):
     return [
-        pltpu.VMEM((LINE, rows, columns), bf16),
+        pltpu.VMEM((LINE, 2 * rows, columns), bf16),
         pltpu.VMEM((LINE, rows, columns), bf16),
         pltpu.VMEM((2, 3, rows, columns), bf16),
-        pltpu.SemaphoreType.DMA((LINE, 2)),
+        pltpu.SemaphoreType.DMA((LINE,)),
         pltpu.SemaphoreType.DMA((LINE,)),
         pltpu.SemaphoreType.DMA((2, 3)),
         pltpu.SemaphoreType.DMA((2, 3)),
@@ -342,36 +342,43 @@
     ]
 
 
-def reduce_line(me, src, out, scratch):
-    here, there, landed, snd, rcv, line_snd, line_rcv, end = scratch
-    rows = here.shape[1]
-    mine = pl.ds(pl.multiple_of(me.t * rows, rows), rows)
-    theirs = pl.ds(pl.multiple_of((1 - me.t) * rows, rows), rows)
-    order = (3, 0, 2, 1)
-
-    def cross(z):
-        return remote(src.at[z, theirs], there.at[z], snd.at[z, 0], rcv.at[z], me.other())
-
-    def local(z):
-        return pltpu.make_async_copy(src.at[z, mine], here.at[z], snd.at[z, 1])
-
-    def send(way, k, source):
-        to = me.z + 1 - 2 * way
-        return remote(
-            source, landed.at[way, k], line_snd.at[way, k], line_rcv.at[way, k], me.at(to, me.q)
-        )
-
-    for z in order:
-        cross(z).start()
-        local(z).start()
-    yield
-    for z in order:
-        local(z).wait()
-        cross(z).wait_recv()
-        add_rows(here.at[z], (here.at[z], there.at[z]))
-    for k in range(3):
+class LineSum:
+    def __init__(self, me, out, scratch):
+        self.me = me
+        self.src, self.there, self.landed, *self.sems = scratch
+        rows = self.there.shape[1]
+        self.mine = pl.ds(pl.multiple_of(me.t * rows, rows), rows)
+        self.theirs = pl.ds(pl.multiple_of((1 - me.t) * rows, rows), rows)
+        self.out = out
+
+    def here(self, z):
+        return self.src.at[z, self.mine]
+
+    def cross(self, z):
+        snd, rcv = self.sems[:2]
+        source = self.src.at[z, self.theirs]
+        return remote(source, self.there.at[z], snd.at[z], rcv.at[z], self.me.other())
+
+    def send(self, way, k, source):
+        me = self.me
+        snd, rcv = self.sems[2:4]
+        to = me.at(me.z + 1 - 2 * way, me.q)
+        return remote(source, self.landed.at[way, k], snd.at[way, k], rcv.at[way, k], to)
+
+    def ends(self):
+        me = self.me
+        end = self.sems[4]
+        done = self.here(me.z)
+        keep = pltpu.make_async_copy(done, self.out.at[self.mine], end.at[0])
+        return keep, remote(done, self.out.at[self.mine], end.at[1], end.at[2], me.other())
+
+    def fold(self, z):
+        self.cross(z).wait_recv()
+        add_rows(self.here(z), (self.here(z), self.there.at[z]))
+
+    def step(self, k):
         for way in range(2):
-            w = me.z if way == 0 else 3 - me.z
+            w = self.me.z if way == 0 else 3 - self.me.z
             block = 3 + w - k if way == 0 else k - w
 
             @pl.when(w <= k)
@@ -380,43 +387,44 @@
 
                     @pl.when(w < k)
                     def _():
-                        send(way, k - 1, here.at[0]).wait_send()
+                        self.send(way, k - 1, self.here(0)).wait_send()
 
                 @pl.when(w == 0)
                 def _():
-                    send(way, k, here.at[block]).start()
+                    self.send(way, k, self.here(block)).start()
 
                 if k:
 
                     @pl.when(w > 0)
                     def _():
-                        partial = landed.at[way, k - 1]
-                        send(way, k - 1, partial).wait_recv()
-                        add_rows(partial, (partial, here.at[block]))
-                        send(way, k, partial).start()
-
-        yield
-    for way in range(2):
-        w = me.z if way == 0 else 3 - me.z
-
-        @pl.when(w > 0)
-        def _():
-            send(way, 2, landed.at[way, 2]).wait_recv()
-            add_rows(here.at[me.z], (here.at[me.z], landed.at[way, 2]))
-
-        @pl.when(w < 3)
-        def _():
-            send(way, 2, here.at[0]).wait_send()
-
-    keep = pltpu.make_async_copy(here.at[me.z], out.at[mine], end.at[0])
-    give = remote(here.at[me.z], out.at[mine], end.at[1], end.at[2], me.other())
-    keep.start()
-    give.start()
-    yield True
-    for z in range(LINE):
-        cross(z).wait_send()
-    keep.wait()
-    give.wait()
+                        partial = self.landed.at[way, k - 1]
+                        self.send(way, k - 1, partial).wait_recv()
+                        add_rows(partial, (partial, self.here(block)))
+                        self.send(way, k, partial).start()
+
+    def finish(self):
+        for way in range(2):
+            w = self.me.z if way == 0 else 3 - self.me.z
+
+            @pl.when(w > 0)
+            def _():
+                last = self.landed.at[way, 2]
+                self.send(way, 2, last).wait_recv()
+                here = self.here(self.me.z)
+                add_rows(here, (here, last))
+
+            @pl.when(w < 3)
+            def _():
+                self.send(way, 2, self.here(0)).wait_send()
+
+        for copy in self.ends():
+            copy.start()
+
+    def close(self):
+        for z in range(LINE):
+            self.cross(z).wait_send()
+        for copy in self.ends():
+            copy.wait()
 
 
 def reduce_window(me, reach, src, out, scratch):
@@ -484,25 +492,6 @@
 PLANE_SEMS = [pltpu.SemaphoreType.DMA((4,)), pltpu.SemaphoreType.DMA((4,))]
 
 
-def plane_first(me, src, got, sems):
-    snd, rcv = sems
-    rows = src.shape[-2] // 2
-    copies = []
-    lead = (slice(None),) * (len(src.shape) - 3)
-    for h in range(2):
-        q = (me.xq, me.yq)[h]
-        for i in range(2):
-            place = (q, me.dq)[i]
-            n = 2 * h + i
-            view = src.at[lead + (place, pl.ds(h * rows, rows))]
-            copies.append(remote(view, got.at[h, i], snd.at[n], rcv.at[n], me.at(me.z, q)))
-    for copy in copies:
-        copy.start()
-    yield True
-    for copy in copies:
-        copy.wait()
-
-
 def add_blocks(out, more):
     blocks, rows, _ = out.shape
     steps = rows // 16
@@ -532,7 +521,12 @@
     got, kept, passed, got_two, total = buffers
     snd, rcv, loc, line_snd, line_rcv = sems
     half = src.shape[2] // 2
+    across = pl.ds(0, src.shape[3])
     first, second = [], []
+
+    def held(ref, h, i):
+        return ref.at[h, i, :, :, across]
+
     for h in range(2):
         q = (me.xq, me.yq)[h]
         rows = pl.ds(h * half, half)
@@ -544,6 +538,7 @@
         second.append(
             remote(passed.at[h], got_two.at[h], snd.at[4 + h], rcv.at[4 + h], me.at(me.z, q))
         )
+    yield
     for copy in first:
         copy.start()
     yield
@@ -554,10 +549,10 @@
         for i in range(2):
             n = 2 * h + i
             view = src.at[:, (me.q, (me.yq, me.xq)[h])[i], pl.ds(h * half, half)]
-            loads.append(pltpu.make_async_copy(view, here.at[h, i], loc.at[n]))
-            loads.append(pltpu.make_async_copy(got.at[h, i], there.at[h, i], loc.at[4 + n]))
+            loads.append(pltpu.make_async_copy(view, held(here, h, i), loc.at[n]))
+            loads.append(pltpu.make_async_copy(got.at[h, i], held(there, h, i), loc.at[4 + n]))
             stores.append(
-                pltpu.make_async_copy(here.at[h, i], (kept, passed)[i].at[h], loc.at[n])
+                pltpu.make_async_copy(held(here, h, i), (kept, passed)[i].at[h], loc.at[n])
             )
     for copy in loads:
         copy.start()
@@ -565,7 +560,7 @@
         copy.wait()
     for h in range(2):
         for i in range(2):
-            add_blocks(here.at[h, i], there.at[h, i])
+            add_blocks(held(here, h, i), held(there, h, i))
     for copy in stores:
         copy.start()
     for copy in stores:
@@ -577,17 +572,17 @@
         copy.wait_recv()
     loads, stores = [], []
     for h in range(2):
-        loads.append(pltpu.make_async_copy(kept.at[h], here.at[h, 0], loc.at[h]))
-        loads.append(pltpu.make_async_copy(got_two.at[h], there.at[h, 0], loc.at[4 + h]))
+        loads.append(pltpu.make_async_copy(kept.at[h], held(here, h, 0), loc.at[h]))
+        loads.append(pltpu.make_async_copy(got_two.at[h], held(there, h, 0), loc.at[4 + h]))
         stores.append(
-            pltpu.make_async_copy(here.at[h, 0], total.at[:, pl.ds(h * half, half)], loc.at[h])
+            pltpu.make_async_copy(held(here, h, 0), total.at[:, pl.ds(h * half, half)], loc.at[h])
         )
     for copy in loads:
         copy.start()
     for copy in loads:
         copy.wait()
     for h in range(2):
-        add_blocks(here.at[h, 0], there.at[h, 0])
+        add_blocks(held(here, h, 0), held(there, h, 0))
     for copy in stores:
         copy.start()
     for copy in stores:
@@ -597,214 +592,153 @@
         z = me.order(j)
         return remote(total.at[z], done.at[me.z], line_snd.at[z], line_rcv.at[me.z], me.at(z, me.q))
 
-    local = pltpu.make_async_copy(total.at[me.z], done.at[me.z], loc.at[7])
-    local.start()
+    def local():
+        return pltpu.make_async_copy(total.at[me.z], done.at[me.z], loc.at[7])
+
+    local().start()
     for j in (3, 2, 1):
         send(j).start()
     yield True
     for j in range(1, 4):
         z = me.order(j)
         remote(done.at[z], done.at[z], line_snd.at[z], line_rcv.at[z], me.at(z, me.q)).wait_recv()
-    local.wait()
+    local().wait()
     for copy in first + second:
         copy.wait_send()
     for j in range(1, 4):
         send(j).wait_send()
 
 
-FFN_SEMS = [
-    pltpu.SemaphoreType.DMA((3, 2)),
-    pltpu.SemaphoreType.DMA((3, 2)),
-    pltpu.SemaphoreType.DMA((3, 4)),
-    pltpu.SemaphoreType.DMA((3, 4)),
-    pltpu.SemaphoreType.DMA((3, 4)),
+PLANE_SUM_SEMS = [
+    pltpu.SemaphoreType.DMA((3, 6)),
+    pltpu.SemaphoreType.DMA((3, 6)),
+    pltpu.SemaphoreType.DMA((4,)),
 ]
 
 
-def ffn_scatter(me, order, kept, passed, got, total, done, here, there, sems):
-    snd, rcv, loc, line_snd, line_rcv = sems
-    half, columns = kept.shape[3:]
-
-    def cross(part):
+class PlaneSum:
+    def __init__(self, me, src, buffers, total, here, there, sems):
+        self.me, self.src, self.total = me, src, total
+        self.got, self.kept, self.passed, self.got_two = buffers
+        self.here, self.there = here, there
+        self.snd, self.rcv, self.loc = sems
+        self.half = src.shape[3] // 2
+
+    def view(self, part, place, h):
+        return self.src.at[part, :, place, pl.ds(h * self.half, self.half)]
+
+    def sends(self, part):
+        me = self.me
+        copies = []
+        for h in range(2):
+            q = (me.xq, me.yq)[h]
+            for i in range(2):
+                n = 2 * h + i
+                copies.append(
+                    remote(
+                        self.view(part, (q, me.dq)[i], h),
+                        self.got.at[part, h, i],
+                        self.snd.at[part, n],
+                        self.rcv.at[part, n],
+                        me.at(me.z, q),
+                    )
+                )
+        return copies
+
+    def start(self, part):
+        for copy in self.sends(part):
+            copy.start()
+
+    def fold(self, part):
+        me = self.me
+        for copy in self.sends(part):
+            copy.wait_recv()
+        for h in range(2):
+            places = (me.q, (me.yq, me.xq)[h])
+            loads, stores = [], []
+            for i in range(2):
+                a, b = self.here.at[i], self.there.at[i]
+                loads.append(pltpu.make_async_copy(self.view(part, places[i], h), a, self.loc.at[i]))
+                loads.append(
+                    pltpu.make_async_copy(self.got.at[part, h, i], b, self.loc.at[2 + i])
+                )
+                stores.append(
+                    pltpu.make_async_copy(
+                        a, (self.kept, self.passed)[i].at[h, part], self.loc.at[i]
+                    )
+                )
+            for copy in loads:
+                copy.start()
+            for copy in loads:
+                copy.wait()
+            for i in range(2):
+                add_blocks(self.here.at[i], self.there.at[i])
+            for copy in stores:
+                copy.start()
+            for copy in stores:
+                copy.wait()
+
+    def second(self, part):
+        me = self.me
         return [
             remote(
-                passed.at[h, part],
-                got.at[h, part],
-                snd.at[part, h],
-                rcv.at[part, h],
+                self.passed.at[h, part],
+                self.got_two.at[h, part],
+                self.snd.at[part, 4 + h],
+                self.rcv.at[part, 4 + h],
                 me.at(me.z, (me.yq, me.xq)[h]),
             )
             for h in range(2)
         ]
 
-    def send(part, j):
-        z = me.order(j)
-        return remote(
-            total.at[part, z],
-            done.at[part, me.z],
-            line_snd.at[part, z],
-            line_rcv.at[part, me.z],
-            me.at(z, me.q),
-        )
-
-    def local(part):
-        return pltpu.make_async_copy(
-            total.at[part, me.z], done.at[part, me.z], line_snd.at[part, me.z]
-        )
-
-    for part in order:
-        for copy in cross(part):
+    def pass_on(self, part):
+        for copy in self.second(part):
             copy.start()
-    yield
-    at = pl.ds(0, columns)
-    for part in order:
-        for copy in cross(part):
+
+    def fold_again(self, part):
+        for copy in self.second(part):
             copy.wait_recv()
         loads, stores = [], []
         for h in range(2):
-            a, b = here.at[h, 0, :, :, at], there.at[h, 0, :, :, at]
-            loads.append(pltpu.make_async_copy(kept.at[h, part], a, loc.at[part, h]))
-            loads.append(pltpu.make_async_copy(got.at[h, part], b, loc.at[part, 2 + h]))
-            stores.append(
-                pltpu.make_async_copy(
-                    a, total.at[part, :, pl.ds(h * half, half)], loc.at[part, h]
-                )
-            )
+            a, b = self.here.at[h], self.there.at[h]
+            target = self.total.at[part, :, pl.ds(h * self.half, self.half)]
+            loads.append(pltpu.make_async_copy(self.kept.at[h, part], a, self.loc.at[h]))
+            loads.append(pltpu.make_async_copy(self.got_two.at[h, part], b, self.loc.at[2 + h]))
+            stores.append(pltpu.make_async_copy(a, target, self.loc.at[h]))
         for copy in loads:
             copy.start()
         for copy in loads:
             copy.wait()
         for h in range(2):
-            add_blocks(here.at[h, 0, :, :, at], there.at[h, 0, :, :, at])
+            add_blocks(self.here.at[h], self.there.at[h])
         for copy in stores:
             copy.start()
         for copy in stores:
             copy.wait()
-        local(part).start()
-        for j in (3, 2, 1):
-            send(part, j).start()
-        yield
-    yield True
-    for part in order:
-        for j in range(1, 4):
-            z = me.order(j)
-            view = done.at[part, z]
-            remote(
-                view, view, line_snd.at[part, z], line_rcv.at[part, z], me.at(z, me.q)
-            ).wait_recv()
-        local(part).wait()
-        for copy in cross(part):
+
+    def close(self, part):
+        for copy in self.sends(part) + self.second(part):
             copy.wait_send()
-        for j in range(1, 4):
-            send(part, j).wait_send()
-
-
-def plane_sums_scratch(shape):
-    parts, line, _, rows, columns = shape
-    block = (parts, 2, 2, line, rows // 2, columns)
-    return [
-        pltpu.VMEM(block, bf16),
-        pltpu.VMEM(block, bf16),
-        pltpu.SemaphoreType.DMA((parts, 4)),
-        pltpu.SemaphoreType.DMA((parts, 4)),
-        pltpu.SemaphoreType.DMA((parts, 4)),
-        pltpu.SemaphoreType.DMA((parts, 4)),
-    ]
-
-
-def plane_sums(me, order, src, kept, passed, scratch):
-    here, there, loc, snd, rcv, end = scratch
-    half = src.shape[3] // 2
-
-    def view(part, place, h):
-        return src.at[part, :, place, pl.ds(h * half, half)]
-
-    def sends(part):
-        for h in range(2):
-            q = (me.xq, me.yq)[h]
-            for i in range(2):
-                n = 2 * h + i
-                yield remote(
-                    view(part, (q, me.dq)[i], h),
-                    there.at[part, h, i],
-                    snd.at[part, n],
-                    rcv.at[part, n],
-                    me.at(me.z, q),
-                )
-
-    def loads(part):
-        for h in range(2):
-            for i in range(2):
-                place = (me.q, (me.yq, me.xq)[h])[i]
-                yield pltpu.make_async_copy(
-                    view(part, place, h), here.at[part, h, i], loc.at[part, 2 * h + i]
-                )
-
-    def stores(part):
-        for h in range(2):
-            for i in range(2):
-                yield pltpu.make_async_copy(
-                    here.at[part, h, i], (kept, passed)[i].at[h, part], end.at[part, 2 * h + i]
-                )
-
-    for part in order:
-        for copy in sends(part):
-            copy.start()
-        for copy in loads(part):
-            copy.start()
-    yield
-    for part in order:
-        yield
-        for copy in loads(part):
-            copy.wait()
-        for copy in sends(part):
-            copy.wait_recv()
-        for h in range(2):
-            for i in range(2):
-                for z in range(here.shape[3]):
-                    block = here.at[part, h, i, z]
-                    add_rows(block, (block, there.at[part, h, i, z]))
-        for copy in stores(part):
-            copy.start()
-    yield True
-    for part in order:
-        for copy in sends(part):
-            copy.wait_send()
-        for copy in stores(part):
-            copy.wait()
-
-
-def plane_second(me, src, got, sems):
-    snd, rcv = sems
-    copies = [
-        remote(src.at[h], got.at[h], snd.at[h], rcv.at[h], me.at(me.z, (me.yq, me.xq)[h]))
-        for h in range(2)
-    ]
-    for copy in copies:
-        copy.start()
-    yield True
-    for copy in copies:
-        copy.wait()
 
 
 LINE_SEMS = [pltpu.SemaphoreType.DMA((4,)), pltpu.SemaphoreType.DMA((4,)), pltpu.SemaphoreType.DMA]
 
 
-def line_exchange(me, piece, got, sems):
+def line_exchange(me, src, done, sems):
     snd, rcv, loc = sems
-    local = pltpu.make_async_copy(piece(me.z), got.at[me.z], loc)
+    local = pltpu.make_async_copy(src.at[me.z], done.at[me.z], loc)
     local.start()
 
     def send(j):
         z = me.order(j)
-        return remote(piece(z), got.at[me.z], snd.at[z], rcv.at[me.z], me.at(z, me.q))
+        return remote(src.at[z], done.at[me.z], snd.at[z], rcv.at[me.z], me.at(z, me.q))
 
     for j in (3, 2, 1):
         send(j).start()
     yield True
     for j in range(1, 4):
         z = me.order(j)
-        remote(got.at[z], got.at[z], snd.at[z], rcv.at[z], me.at(z, me.q)).wait_recv()
+        remote(done.at[z], done.at[z], snd.at[z], rcv.at[z], me.at(z, me.q)).wait_recv()
     for j in range(1, 4):
         send(j).wait_send()
     local.wait()
@@ -833,7 +767,7 @@
         out_specs=[ANY] * len(outputs),
         scratch_shapes=flat,
         compiler_params=pltpu.CompilerParams(
-            collective_id=number, has_side_effects=True, vmem_limit_bytes=56 * 2**20
+            collective_id=number, has_side_effects=True, vmem_limit_bytes=62 * 2**20
         ),
     )(*inputs)
 
@@ -1009,7 +943,6 @@
     if groups > 1:
         kv_full = kv_full.reshape(RING, 2, groups, kv_rows // groups, columns).swapaxes(1, 2)
     kv_full = kv_full.reshape(width, columns)
-    cot_all = cot_all.reshape(LINE * tokens, width)
 
     def vector(row, count, order):
         piece = smalls[:, :, row, :count].reshape(RING, 2, groups, count // groups)
@@ -1219,79 +1152,239 @@
         )
         return part.astype(f32) + theirs.astype(f32)
 
-    normed_all = normed_all.reshape(LINE * tokens, width)
-    ours = (jnp.arange(block) >= block_skip)[None, :]
-    gate_pre = dot(normed_all, ffn_full[0]) + bias_local[0]
-    up_pre = dot(normed_all, ffn_full[1]) + bias_local[1]
-    hidden = jnp.where(ours, jax.nn.gelu(gate_pre, approximate=True) * up_pre, 0.0).astype(bf16)
-    mlp_part = dot(hidden, ffn_full[2], 1, 1).astype(bf16)
-    hidden_grad = dot(cot_all, ffn_full[2])
-    _, unit_pull = jax.vjp(
-        lambda gate_in, up_in: jax.nn.gelu(gate_in, approximate=True) * up_in, gate_pre, up_pre
-    )
-    gate_grad, up_grad = unit_pull(hidden_grad)
-    gate_low = jnp.where(ours, gate_grad, 0.0).astype(bf16)
-    up_low = jnp.where(ours, up_grad, 0.0).astype(bf16)
-    ffn_term = jnp.stack(
-        [
-            dot(normed_all, gate_low, 0, 0).astype(bf16),
-            dot(normed_all, up_low, 0, 0).astype(bf16),
-            dot(cot_all, hidden, 0, 0).astype(bf16),
-        ]
-    )
-    ffn_term = ffn_term.reshape(3, LINE, 4, rows, block)
-    normed_two_part = (dot(gate_low, ffn_full[0], 1, 1) + dot(up_low, ffn_full[1], 1, 1)).astype(
-        bf16
-    )
-    hidden_bias_part = jnp.stack(
-        [jnp.sum(gate_low.astype(f32), axis=0), jnp.sum(up_low.astype(f32), axis=0)]
-    )
-    hidden_bias_part = jnp.pad(hidden_bias_part, ((0, 14), (0, 0))).astype(bf16)
-
-    def third_steps(me, ins, outs, sems):
-        yield from ()
-        one = reduce_line(me, ins[0], outs[0], sems[0])
-        two = reduce_line(me, ins[1], outs[1], sems[1])
-        three = plane_sums(me, (2, 0, 1), ins[2], outs[2], outs[3], sems[2])
-        next(one)
-        next(three)
-        ends = [swap(me, ins[3], outs[4], sems[3])]
-        next(ends[0])
-        next(two)
-        for _ in range(4):
-            next(one)
-        next(three)
-        for _ in range(3):
-            next(two)
-            next(three)
-        next(two)
-        for step in [one, two, three] + ends:
-            next(step, None)
-
-    kept_shape = (2, 3, LINE, rows // 2, block)
-    normed_two_grad, mlp_out, ffn_kept, ffn_passed, bias_theirs = transfer(
+    ours = (jnp.arange(block) >= block_skip).astype(f32)[None, :]
+    part_rows = 4 * rows
+    pace = block // 2
+
+    def third_steps(me, ins, outs, groups_in):
+        normed_in, cot_in, weights_in, bias, valid = ins
+        normed_grad_out, mlp_out, total, bias_own, bias_theirs, term, *buffers = outs
+        one_scratch, two_scratch, plane_sems, swap_sems, scratch = groups_in
+        (
+            weights, normed_v, cot_v, chunks, hidden, gate_low, up_low, bias_sum, bias_low,
+            stage, here, there, loads,
+        ) = scratch
+        one = LineSum(me, normed_grad_out, one_scratch)
+        two = LineSum(me, mlp_out, two_scratch)
+        plane = PlaneSum(me, term, buffers, total, here, there, plane_sems)
+
+        def load(n, src, dst):
+            return pltpu.make_async_copy(src, dst, loads.at[n])
+
+        def part_columns(i):
+            return pl.ds(pl.multiple_of(i * part_rows, LANES), part_rows)
+
+        def rows_of(i):
+            return pl.ds(pl.multiple_of(i * tokens, tokens), tokens)
+
+        for n in range(3):
+            load(n, weights_in.at[n], weights.at[n]).start()
+        load(3, normed_in.at[0], normed_v).start()
+        load(4, cot_in.at[0], cot_v).start()
+        bias_sum[...] = jnp.zeros(bias_sum.shape, f32)
+        for n in range(3):
+            load(n, weights_in.at[n], weights.at[n]).wait()
+
+        def both_ways(place):
+            load(3, normed_in.at[place], normed_v).wait()
+            load(4, cot_in.at[place], cot_v).wait()
+            at = rows_of(place)
+
+            @pl.loop(0, 2)
+            def _(n):
+                part = pl.ds(pl.multiple_of(n * pace, LANES), pace)
+                gate = dot(normed_v[...], weights[0, :, part]) + bias[0:1, part]
+                up = dot(normed_v[...], weights[1, :, part]) + bias[1:2, part]
+                grad = dot(cot_v[...], weights[2, :, part]) * valid[:, part]
+                square = gate * gate
+                slope = 0.7978845608028654 * (1.0 + 3.0 * 0.044715 * square)
+                turn = jnp.tanh(0.7978845608028654 * gate * (1.0 + 0.044715 * square))
+                side = 0.5 * (1.0 + turn)
+                unit = gate * side
+                hidden[at, part] = (unit * up * valid[:, part]).astype(bf16)
+                gate_grad = grad * up * (side + 0.5 * gate * (1.0 - turn * turn) * slope)
+                gate_low[at, part] = gate_grad.astype(bf16)
+                up_low[at, part] = (grad * unit).astype(bf16)
+                for i, low in enumerate((gate_low, up_low)):
+                    bias_sum[i : i + 1, part] += jnp.sum(
+                        low[at, part].astype(f32), axis=0, keepdims=True
+                    )
+
+            @pl.when(place < LINE - 1)
+            def _():
+                load(3, normed_in.at[place + 1], normed_v).start()
+                load(4, cot_in.at[place + 1], cot_v).start()
+
+        pl.loop(0, LINE)(both_ways)
+
+        def back(place):
+            at = rows_of(place)
+
+            @pl.loop(0, LINE)
+            def _(i):
+                lines = part_columns(i)
+                value = dot(gate_low[at], weights[0, lines], 1, 1)
+                value += dot(up_low[at], weights[1, lines], 1, 1)
+                one.src[place, :, lines] = value.astype(bf16)
+
+            one.cross(place).start()
+
+        bias_low[...] = bias_sum[...].astype(bf16)
+        bias_swap = remote(bias_low, bias_theirs, swap_sems[0], swap_sems[1], me.other())
+        bias_swap.start()
+        bias_keep = load(0, bias_low, bias_own)
+        bias_keep.start()
+
+        def chunk(source, i, slot):
+            return load(3 + slot, source.at[:, :, part_columns(i)], chunks.at[slot])
+
+        def stored(n, target):
+            return load(1 + n, stage.at[n], target)
+
+        def weight_term(slot, factor, n, target):
+            left = chunks[slot].reshape(LINE * tokens, part_rows)
+            stage[n] = dot(left, factor[...], 0, 0).astype(bf16).reshape(stage.shape[1:])
+            stored(n, target).start()
+
+        def outputs_of(place):
+            @pl.loop(0, LINE)
+            def _(i):
+                lines = part_columns(i)
+                value = dot(hidden[rows_of(place)], weights[2, lines], 1, 1)
+                two.src[place, :, lines] = value.astype(bf16)
+
+            two.cross(place).start()
+
+        def down_terms(i):
+            slot = lax.rem(i, 2)
+            chunk(cot_in, i, slot).wait()
+
+            @pl.when(i < LINE - 1)
+            def _():
+                chunk(cot_in, i + 1, 1 - slot).start()
+
+            @pl.when(i > 1)
+            def _():
+                stored(slot, term.at[2, i]).wait()
+
+            weight_term(slot, hidden, slot, term.at[2, i])
+
+        def gate_up_terms(i):
+            slot = lax.rem(i, 2)
+            chunk(normed_in, i, slot).wait()
+
+            @pl.when(i < LINE - 1)
+            def _():
+                chunk(normed_in, i + 1, 1 - slot).start()
+
+            for n, factor in enumerate((gate_low, up_low)):
+
+                @pl.when(i > 0)
+                def _():
+                    stored(n, term.at[n, i]).wait()
+
+                weight_term(slot, factor, n, term.at[n, i])
+
+        chunk(cot_in, 0, 0).start()
+
+        @pl.loop(0, 2)
+        def _(i):
+            outputs_of(3 - 3 * i)
+
+        two.fold(3)
+        two.fold(0)
+        two.step(0)
+        pl.loop(0, LINE)(down_terms)
+        chunk(normed_in, 0, 0).start()
+        for n in range(2):
+            stored(n, term.at[2, 0]).wait()
+        plane.start(2)
+
+        @pl.loop(0, 2)
+        def _(i):
+            outputs_of(2 - i)
+
+        two.fold(2)
+        two.fold(1)
+        two.step(1)
+        pl.loop(0, LINE)(gate_up_terms)
+        for n in range(2):
+            stored(n, term.at[n, 0]).wait()
+        plane.start(0)
+        two.step(2)
+
+        @pl.loop(0, 2)
+        def _(i):
+            back(3 - 3 * i)
+
+        one.fold(3)
+        one.fold(0)
+        one.step(0)
+
+        @pl.loop(0, 2)
+        def _(i):
+            back(2 - i)
+
+        one.fold(2)
+        one.fold(1)
+        two.finish()
+        one.step(1)
+        plane.fold(2)
+        plane.pass_on(2)
+        one.step(2)
+        plane.fold(0)
+        plane.pass_on(0)
+        plane.fold_again(2)
+        one.finish()
+        plane.fold_again(0)
+        one.close()
+        two.close()
+        for part in (0, 2):
+            plane.close(part)
+        bias_swap.wait()
+        bias_keep.wait()
+        return []
+
+    half_shape = (2, 3, LINE, rows // 2, block)
+    normed_two_grad, mlp_out, ffn_total, hidden_bias_part, bias_theirs, ffn_term = transfer(
         4,
-        [
-            normed_two_part.reshape(LINE, tokens, width),
-            mlp_part.reshape(LINE, tokens, width),
-            ffn_term,
-            hidden_bias_part,
-        ],
+        [normed_all, cot_all, ffn_full, bias_local, ours],
         [
             ((tokens, width), bf16),
             ((tokens, width), bf16),
-            (kept_shape, bf16),
-            (kept_shape, bf16),
-            (hidden_bias_part.shape, bf16),
+            ((3, LINE, rows, block), bf16),
+            ((16, block), bf16),
+            ((16, block), bf16),
+            ((3, LINE, 4, rows, block), bf16),
+            ((3, 2, 2, LINE, rows // 2, block), bf16),
+            (half_shape, bf16),
+            (half_shape, bf16),
+            (half_shape, bf16),
         ],
         [
-            chain_scratch(tokens // 2, width),
-            chain_scratch(tokens // 2, width),
-            plane_sums_scratch(ffn_term.shape),
+            line_sum_scratch(tokens // 2, width),
+            line_sum_scratch(tokens // 2, width),
+            PLANE_SUM_SEMS,
             SWAP_SEMS,
+            [
+                pltpu.VMEM((3, width, block), bf16),
+                pltpu.VMEM((tokens, width), bf16),
+                pltpu.VMEM((tokens, width), bf16),
+                pltpu.VMEM((2, LINE, tokens, part_rows), bf16),
+                pltpu.VMEM((LINE * tokens, block), bf16),
+                pltpu.VMEM((LINE * tokens, block), bf16),
+                pltpu.VMEM((LINE * tokens, block), bf16),
+                pltpu.VMEM((16, block), f32),
+                pltpu.VMEM((16, block), bf16),
+                pltpu.VMEM((2, 4, rows, block), bf16),
+                pltpu.VMEM((2, LINE, rows // 2, block), bf16),
+                pltpu.VMEM((2, LINE, rows // 2, block), bf16),
+                pltpu.SemaphoreType.DMA((5,)),
+            ],
         ],
         third_steps,
-    )
+        near=(3, 4),
+    )[:6]
     cot_full = cotangent.astype(f32)
     _, norm_two_pull = jax.vjp(normalize, middle, gain_two)
     middle_part, gain_two_grad = norm_two_pull(normed_two_grad.astype(f32))
@@ -1339,14 +1432,15 @@
     def fourth_steps(me, ins, outs, groups_in):
         (
             low_in, out_in, mixed_in, q_in, kv_in, logs_in, normed_in, query_in, kvw_in,
-            kept_in, passed_in, small_in, grad_in, x_in,
+            ffn_in, total_in, small_in, grad_in, x_in,
             marks_row, marks_column, cos2, sin2, gain,
         ) = ins
         ffn_done, out_done, query_done, kv_done, input_out, gain_all = outs[:6]
-        out_term, query_term, kv_term, ffn_got, ffn_total = outs[6:11]
-        out_buffers, query_buffers, kv_buffers = outs[11:16], outs[16:21], outs[21:26]
+        out_term, query_term, kv_term = outs[6:9]
+        out_buffers, kv_buffers, ffn_buffers = outs[9:14], outs[14:19], outs[19:24]
+        query_buffers = (outs[24:29], outs[29:34])
         (
-            ffn_sems, out_sems, query_sems, kv_sems, window_scratch, swap_sems, last_sems,
+            line_sems, line_sems_two, ffn_sems, out_sems, query_sems, more_sems, kv_sems, window_scratch, swap_sems, last_sems,
             vector_sems, scratch,
         ) = groups_in
         (
@@ -1368,15 +1462,21 @@
         def part_columns(i):
             return pl.ds(pl.multiple_of(i * part_rows, LANES), part_rows)
 
-        ffn = ffn_scatter(
-            me, (2, 0, 1), kept_in, passed_in, ffn_got, ffn_total, ffn_done, here, there, ffn_sems
+        lines = [
+            line_exchange(me, total_in.at[2], ffn_done.at[2], line_sems),
+            line_exchange(me, total_in.at[0], ffn_done.at[0], line_sems_two),
+        ]
+        ffn = scatter(me, ffn_in.at[1], ffn_done.at[1], ffn_buffers, here, there, ffn_sems)
+        outw = scatter(me, out_term, out_done, out_buffers, here, there, out_sems)
+        query, more = (
+            scatter(me, query_term.at[n], query_done.at[n], query_buffers[n], here, there, sems)
+            for n, sems in enumerate((query_sems, more_sems))
         )
-        outw = scatter(me, out_term, out_done, out_buffers, here, there, out_sems)
-        query = scatter(me, query_term, query_done, query_buffers, here, there, query_sems)
         kvw_steps = scatter(
             me, kv_term, kv_done.at[me.t], kv_buffers, kv_here, kv_there, kv_sems
         )
-        next(ffn)
+        for step in [ffn, outw, query, more, kvw_steps] + lines + [ffn]:
+            next(step)
         start = jnp.maximum(me.r - reach, 0)
         first_loads = [
             load(0, low_in, low),
@@ -1393,17 +1493,23 @@
         first_loads[0].wait()
         first_loads[1].wait()
 
-        def weight_term(left, right, term):
+        def weight_term(left, right, targets):
+            width_of = heads * HD // len(targets)
+
             @pl.loop(0, LINE)
             def _(i):
                 value = dot(left[:, part_columns(i)], right[...], 0, 0).astype(bf16)
                 stage[...] = value.reshape(stage.shape)
-                copy = load(8, stage, term.at[i])
-                copy.start()
-                copy.wait()
-
-        weight_term(low, mixed, out_term)
-        next(outw)
+                copies = [
+                    load(8 + n, stage.at[:, :, pl.ds(n * width_of, width_of)], term.at[i])
+                    for n, term in enumerate(targets)
+                ]
+                for copy in copies:
+                    copy.start()
+                for copy in copies:
+                    copy.wait()
+
+        weight_term(low, mixed, [out_term])
         first_loads[2].wait()
 
         @pl.loop(0, heads)
@@ -1448,11 +1554,11 @@
                 window_sum[blocks, :, :HD] += key_sum.reshape(chunk, tokens, HD)
                 window_sum[blocks, :, HD:] += value_sum.reshape(chunk, tokens, HD)
             q_grad[:, at] = (turn(q_sum, -1.0) * scale_factor).astype(bf16)
-            for i in (2, 4):
-
-                @pl.when(h == i)
-                def _():
-                    next(ffn)
+
+            @pl.when(h == heads - 1)
+            def _():
+                next(outw)
+
 
         @pl.loop(0, reach + 1)
         def _(i):
@@ -1461,8 +1567,8 @@
         window_steps = reduce_window(me, reach, win, kv_total, window_scratch)
         next(window_steps)
         load(5, grad_in, mask).start()
-        weight_term(normed_v, q_grad, query_term)
-        next(query)
+        next(window_steps)
+        weight_term(normed_v, q_grad, [query_term.at[0], query_term.at[1]])
         load(2, query_in, weight).wait()
 
         @pl.loop(0, LINE)
@@ -1472,8 +1578,6 @@
 
         swapped = remote(part, theirs, swap_sems[0], swap_sems[1], me.other())
         swapped.start()
-        next(window_steps)
-        next(outw)
         next(ffn)
         next(window_steps)
         next(window_steps, None)
@@ -1495,9 +1599,13 @@
             copy.start()
             copy.wait()
 
-        next(kvw_steps)
         next(outw)
         next(query)
+        next(ffn)
+        next(more)
+        next(kvw_steps)
+        next(query)
+        next(outw)
 
         swapped.wait()
 
@@ -1544,10 +1652,12 @@
         def _(k):
             gain_send(k).start()
 
+        next(more)
         next(kvw_steps)
         next(query)
+        next(more)
         next(kvw_steps)
-        for step in (ffn, outw, query, kvw_steps):
+        for step in lines + [ffn, outw, query, more, kvw_steps]:
             for _ in step:
                 pass
         mine = kv_done.at[me.t]
@@ -1576,26 +1686,29 @@
         5,
         [
             middle_low, out_full, mixed_low, queries, kv_all, log_total, normed, query_full, kv_full,
-            ffn_kept, ffn_passed, small_terms, middle_grad, inputs,
+            ffn_term, ffn_total, small_terms, middle_grad, inputs,
             window_marks[None], own_marks[:, None], turn_cos, turn_sin, gain_one[None],
         ],
         [
             (ffn_shape, bf16),
             ((LINE, rows, heads * HD), bf16),
-            ((LINE, rows, heads * HD), bf16),
+            ((2, LINE, rows, heads * HD // 2), bf16),
             ((2, LINE, kv_size, HD), bf16),
             (inputs.shape, f32),
             ((RING, vector_rows, LANES), bf16),
             (term_shape, bf16),
-            (term_shape, bf16),
+            ((2,) + term_shape[:-1] + (heads * HD // 2,), bf16),
             ((LINE, 4, kv_size, HD), bf16),
-            (kept_shape, bf16),
-            (ffn_shape, bf16),
         ]
-        + scatter_buffers(rows, heads * HD) * 2
-        + scatter_buffers(kv_size, HD),
+        + scatter_buffers(rows, heads * HD)
+        + scatter_buffers(kv_size, HD)
+        + scatter_buffers(rows, block)
+        + scatter_buffers(rows, heads * HD // 2) * 2,
         [
-            FFN_SEMS,
+            LINE_SEMS,
+            LINE_SEMS,
+            SCATTER_SEMS,
+            SCATTER_SEMS,
             SCATTER_SEMS,
             SCATTER_SEMS,
             SCATTER_SEMS,
@@ -1644,7 +1757,8 @@
     )
     ffn_grad = shrink(ffn_grad.astype(f32), 1, groups)
     out_grad = shrink(jnp.sum(out_done.astype(f32), axis=0), 0, groups).T
-    query_grad = shrink(jnp.sum(query_done.astype(f32), axis=0), 0, groups)
+    query_sum = jnp.sum(query_done.astype(f32), axis=1)
+    query_grad = shrink(jnp.concatenate([query_sum[0], query_sum[1]], axis=1), 0, groups)
     kv_sums = jnp.sum(kv_done.astype(f32), axis=1)
     small_sums = lax.dynamic_index_in_dim(kv_sums[:, rows:], t, 0, keepdims=False)
     kv_grad = jnp.concatenate([kv_sums[0, :rows], kv_sums[1, :rows]], axis=1)

time: 832 us -> 765 us (0.919)
  matrix products: 88.8 us -> 5.66 us
  Pallas kernels: 665 us -> 692 us
    dot_general x11 -> x2, matrix products: 88.8 us -> 5.66 us  [dot(): lax.dot_general(a, b, (((ca,), (cb,)), ((), ())), preferred_element_type=...]
    pallas_call x4, Pallas kernels: 665 us -> 692 us  [transfer(): pl.pallas_call(kernel, out_shape=[jax.ShapeDtypeStruct(shape, dtype) for...]
where the time goes in v5:
time: 765 us; the launch traced here: 756 us
  Pallas kernels  692 us (90%)
  other arithmetic  31.9 us (4%)
  local copies, waits for them, and re-layouts  25.5 us (3%)
    pallas_call x4, Pallas kernels, transfer(): pl.pallas_call(kernel, out_shape=[jax.ShapeDtypeStruct(shape, dtype) for...  692 us

profile of v5, /device:TPU:0, one launch (start us, length us, event | category | flops | bytes accessed | tf_op | source)
XLA Modules:
  0.0 755.7 jit_solution(8201315268689289109)
XLA Ops:
  0.9 1.8 fusion.3
  4.7 1.4 fusion.33.refs_2_
  7.6 91.9 %shard_map.220 = (bf16[16,160,1280]{2,1,0:T(8,128)(2,1)}, bf16[16,2,80,512]{3,2,1,0:T(8,128)(2,1)}, bf16[16,2,16,512]{3,2,1,0:T(8,128)(2,1)}, bf16[4,256,2560]{2,1,0:T(8,128)(2,1)}) custom-call(bf16[160,1280]{1,0:T(8,128)(2,1)} %refs_0_.1, bf16[80,512]{1,0:T(8,128)(2,1)} %refs_1_.1, bf16[16,512]{1,0:T(8,128)(2,1)} %fusion.33.refs_2_, bf16[256,2560]{1,0:T(8,128)(2,1)} %refs_3_.1), custom_call_target="tpu_custom_call" | custom-call | tf_op jit(solution)/shard_map/pallas_call | solution.py:763
  101.2 1.1 slice_reduce_fusion.2
  103.8 1.2 slice_reduce_fusion.1
  105.0 1.2 convert_reduce_fusion.5
  108.5 1.4 copy-done.6
  112.2 9.5 %copy.46 = bf16[1280,2560]{1,0:T(8,128)(2,1)} copy(bf16[1280,2560]{0,1:T(8,128)(2,1)} %bitcast.77) | data formatting | bytes 13107200 | tf_op jit(solution)/shard_map/dot_general | solution.py:846
  121.7 4.8 fusion.8
  126.8 1.1 copy.50.refs_4_.refs_3_
  127.9 236.5 %shard_map.221 = (bf16[16,256,512]{2,1,0:T(8,128)(2,1)}, bf16[16,160,1280]{2,1,0:T(8,128)(2,1)}, bf16[3,16,160,1024]{3,2,1,0:T(8,128)(2,1)}, bf16[256,1280]{1,0:...) custom-call(bf16[256,512]{1,0:T(8,128)(2,1)} %pad_maximum_fusion.1.refs_0_, ...), custom_call_target="tpu_custom_call" | custom-call | tf_op jit(solution)/shard_map/pallas_call | solution.py:763
  364.4 2.0 multiply_reduce_fusion
  366.4 138.7 %shard_map.222 = (bf16[256,2560]{1,0:T(8,128)(2,1)}, bf16[256,2560]{1,0:T(8,128)(2,1)}, bf16[3,4,160,1024]{3,2,1,0:T(8,128)(2,1)}, bf16[16,1024]{1,0:T(8,128)(2,...) custom-call(bf16[4,256,2560]{2,1,0:T(8,128)(2,1)} %get-tuple-element, ...), custom_call_target="tpu_custom_call" | custom-call | tf_op jit(solution)/shard_map/pallas_call | solution.py:763
  505.2 3.2 fusion.6
  508.4 4.2 fusion.54
  514.4 1.2 convert_element_type.188.refs_0_
  515.6 224.4 %shard_map.223 = (bf16[3,4,160,1024]{3,2,1,0:T(8,128)(2,1)}, bf16[4,160,1280]{2,1,0:T(8,128)(2,1)}, bf16[2,4,160,640]{3,2,1,0:T(8,128)(2,1)}, bf16[2,4,192,256]{...) custom-call(bf16[256,2560]{1,0:T(8,128)(2,1)} %convert_element_type., ...), custom_call_target="tpu_custom_call" | custom-call | tf_op jit(solution)/shard_map/pallas_call | solution.py:763
  740.0 1.0 convert_reduce_fusion.4
  741.7 1.3 convert_reduce_fusion.3
  744.8 1.2 slice_bitcast_fusion.3
  747.7 1.1 convert_reduce_fusion
  749.2 1.6 convert_bitcast_fusion
  751.4 2.6 slice.157
  754.2 1.5 copy.70
  (98 shorter events, 18.9 us)
Async XLA Ops:
  0.9 107.2 %copy-start.2 = (bf16[256,2560]{1,0:T(8,128)(2,1)S(1)}, bf16[256,2560]{1,0:T(8,128)(2,1)}, u32[]{:S(2)}) copy-start(bf16[256,2560]{1,0:T(8,128)(2,1)} %refs_13_.1) | copy-start | bytes 3932164
  108.1 1.7 copy-start.6
  109.8 11.9 %copy-start.3 = (bf16[256,2560]{1,0:T(8,128)(2,1)}, bf16[256,2560]{1,0:T(8,128)(2,1)S(1)}, u32[]{:S(2)}) copy-start(bf16[256,2560]{1,0:T(8,128)(2,1)S(1)} %fusion.5.refs_6_) | copy-start | bytes 3932164
  505.1 3.2 copy-start.1
  505.2 3.3 copy-start.4
  508.4 4.4 copy-start.10
  508.4 4.4 copy-start.11
  512.6 1.8 copy-start
  740.0 6.0 copy-start.9
  746.0 1.7 copy-start.8
  746.2 2.7 copy-start.5
  751.4 2.9 copy-start.7

commit v6 on v5

--- a/solution.py
+++ b/solution.py
@@ -881,9 +881,17 @@
     scale_factor = HD ** (-0.5)
     assert tokens * RING == SEQ_LEN and lax.axis_size("tensor") == 2
 
-    kv_own = grow(key_value_weight, 0, groups)
+    def own_features(x):
+        if groups == 1:
+            return x
+        both = lax.all_gather(x, "tensor", axis=0)
+        both = lax.all_gather(both, "seq", axis=0, axis_index_groups=group_lists(groups))
+        both = both.reshape((2, -1) + x.shape[1:])
+        return lax.dynamic_index_in_dim(both, t, 0, keepdims=False)
+
+    kv_own = own_features(key_value_weight)
     kv_rows, columns = kv_own.shape
-    vectors = [grow(v, 0, groups) for v in (attn_gain, out_bias, mlp_gain, down_bias)]
+    vectors = [own_features(v) for v in (attn_gain, out_bias, mlp_gain, down_bias)]
     hidden_bias = grow(gate_up_bias, 1, groups)
     marks = jnp.stack([segment_ids // 256, segment_ids % 256]).astype(bf16)
 
@@ -903,91 +911,58 @@
     gate_up_own = grow(gate_up_weight, 1, groups)
     down_own = grow(down_weight.T, 0, groups)
     rows = query_own.shape[0]
-
-    def first_steps(me, ins, outs, sems):
-        def both(n):
-            mine = outs[n].at[:, me.t]
-            for _ in gather_rows(me, ins[n], mine, sems[n]):
-                yield
-            copy = remote(mine, mine, sems[4][0].at[n], sems[4][1].at[n], me.other())
-            copy.start()
-            yield True
-            copy.wait()
-
-        return [
-            both(2),
-            both(1),
-            gather_rows(me, ins[0], outs[0], sems[0]),
-            spread(me, ins[3], outs[3], sems[3]),
-        ]
-
-    query_full, kv_full, smalls, cot_all = transfer(
-        0,
-        [query_own, kv_own, small, cotangent],
-        [
-            ((RING,) + query_own.shape, bf16),
-            ((RING, 2) + kv_own.shape, bf16),
-            ((RING, 2) + small.shape, bf16),
-            ((LINE,) + cotangent.shape, bf16),
-        ],
-        [
-            GATHER_SEMS,
-            GATHER_SEMS,
-            GATHER_SEMS,
-            SPREAD_SEMS,
-            [pltpu.SemaphoreType.DMA((3,)), pltpu.SemaphoreType.DMA((3,))],
-        ],
-        first_steps,
-    )
-    query_full = query_full.reshape(width, heads * HD)
-    if groups > 1:
-        kv_full = kv_full.reshape(RING, 2, groups, kv_rows // groups, columns).swapaxes(1, 2)
-    kv_full = kv_full.reshape(width, columns)
-
-    def vector(row, count, order):
-        piece = smalls[:, :, row, :count].reshape(RING, 2, groups, count // groups)
-        return jnp.transpose(piece, order).reshape(-1).astype(f32)
-
-    gain_one, bias_out, gain_two, bias_down = (
-        vector(i, kv_rows, (0, 2, 1, 3)) for i in range(4)
-    )
-    bias_gate_up = jnp.stack(
-        [vector(4 + i, hidden_bias.shape[1], (2, 0, 1, 3)) for i in range(2)]
-    )
-    bias_local = lax.dynamic_slice_in_dim(bias_gate_up, t * hidden_half + block_start, block, 1)
-    all_marks = smalls[:, 0, 6:8, :tokens].astype(f32)
-    all_marks = (all_marks[:, 0] * 256.0 + all_marks[:, 1]).reshape(-1)
-    window_marks = lax.dynamic_slice_in_dim(all_marks, first_block * tokens, span, 0)
-    own_marks = lax.dynamic_slice_in_dim(all_marks, r * tokens, tokens, 0)
-
-    stream = inputs.astype(f32)
     places = r * tokens + jnp.arange(tokens, dtype=jnp.int32)
-    normed = normalize(stream, gain_one).astype(bf16)
-    query_lin = dot(normed, query_full)
-    queries = (rotate(query_lin, places, heads, 1.0) * scale_factor).astype(bf16)
-    key_value = dot(normed, kv_full)
-    keys_own = rotate(key_value[:, :HD], places, 1, 1.0).astype(bf16)
-    values_own = key_value[:, HD:].astype(bf16)
-    own_block = jnp.concatenate([keys_own, values_own], axis=1)
-
-    def second_steps(me, ins, outs, groups_in):
-        own_kv, own_out, own_gate_up, own_down, q_in, x_in, vec, marks_row, marks_column = ins
-        kv_all, out_all, ffn_all, mixed_out, log_out, middle_out, normed_out = outs
-        kv_sems, out_sems, ffn_sems, spread_sems, swap_sems, scratch = groups_in
-        qs, win, weight, mask, mixed, part, theirs, x, middle, normed_two, logs, loads = scratch
+    frequency = 10000.0 ** (-jnp.arange(HD // 4, dtype=f32) / (HD // 4))
+    angles = places.astype(f32)[:, None] * frequency[None, :]
+    turn_cos = jnp.concatenate([jnp.cos(angles), jnp.cos(angles)], axis=1)
+    turn_sin = jnp.concatenate([-jnp.sin(angles), jnp.sin(angles)], axis=1)
+    own_marks = segment_ids.astype(f32)[:, None]
+    feature = jnp.arange(width)[None, :]
+    pick_device = (feature // kv_rows == jnp.arange(2 * RING)[:, None]).astype(bf16)
+    pick_entry = (feature % kv_rows == jnp.arange(LANES)[:, None]).astype(bf16)
+
+    def first_steps(me, ins, outs, groups_in):
+        (
+            own_query, own_kvw, own_small, own_out, own_gate_up, own_down, x_in, cot_in,
+            marks_column, cos2, sin2, device_of, entry_of,
+        ) = ins
+        (
+            query_all, kvw_all, small_all, kv_all, out_all, ffn_all, cot_out, mixed_out, log_out,
+            middle_out, normed_two_out, queries_out, normed_out, vec_out, marks_out,
+        ) = outs
+        (
+            query_sems, kvw_sems, small_sems, kv_sems, out_sems, ffn_sems, cot_sems, spread_sems,
+            swap_sems, scratch,
+        ) = groups_in
+        (
+            qs, win, weight, kvw, mask, mixed, part, theirs, x, middle, normed, normed_two, logs,
+            small, small_wide, vec, marks_row, kv_low, loads,
+        ) = scratch
 
         def load(n, src, dst):
             return pltpu.make_async_copy(src, dst, loads.at[n])
 
+        def turn(v):
+            first = v[:, : HD // 2]
+            turned = first * cos2[...] + pltpu.roll(first, HD // 4, 1) * sin2[...]
+            return jnp.concatenate([turned, v[:, HD // 2 :]], axis=1)
+
         def columns_of(source, lead):
             def piece(place):
-                start = jnp.minimum(place * block, hidden_half - block)
-                at = pl.ds(pl.multiple_of(start, LANES), block)
+                at = jnp.minimum(place * block, hidden_half - block)
+                at = pl.ds(pl.multiple_of(at, LANES), block)
                 return source.at[:, :, at] if lead else source.at[:, at]
 
             return piece
 
-        keys = gather_rows(me, own_kv, kv_all, kv_sems)
+        def share(n, ref):
+            mine = ref.at[:, me.t]
+            return remote(mine, mine, swap_sems[0].at[n], swap_sems[1].at[n], me.other())
+
+        smalls = gather_rows(me, own_small, small_all.at[:, me.t], small_sems)
+        kvws = gather_rows(me, own_kvw, kvw_all.at[:, me.t], kvw_sems)
+        queries = gather_rows(me, own_query, query_all, query_sems)
+        keys = gather_rows(me, kv_low, kv_all, kv_sems)
         outw = gather_rows(me, own_out, out_all, out_sems)
         ffn = gather_pieces(
             me,
@@ -995,58 +970,105 @@
             ffn_all,
             ffn_sems,
         )
-        next(keys)
-        load(0, q_in, qs).start()
-        load(1, x_in, x).start()
-        next(outw)
+        cot = spread(me, cot_in, cot_out, cot_sems)
+        load(0, x_in, x).start()
+        for n in range(5):
+            next(smalls)
+            next(kvws)
+            next(queries)
+            if n == 3:
+                next(outw)
+        next(ffn)
+        for _ in smalls:
+            pass
+        share(0, small_all).start()
+        for _ in kvws:
+            pass
+        share(1, kvw_all).start()
+        share(0, small_all).wait()
+        load(1, small_all, small).start()
+        load(1, small_all, small).wait()
+        small_wide[...] = small[...].reshape(small_wide.shape).astype(f32)
+        vec[...] = jnp.zeros(vec.shape, f32)
+        for i in range(4):
+            piece = small_wide[:, i, :LANES].astype(bf16)
+            spread_out = dot(piece, device_of[...], 0, 0) * entry_of[...].astype(f32)
+            vec[i : i + 1] = jnp.sum(spread_out, axis=0, keepdims=True)
         start = jnp.maximum(me.r - reach, 0)
         row_places = me.r * tokens + lax.broadcasted_iota(jnp.int32, (tokens, 1), 0)
 
         @pl.loop(0, reach + 1)
         def _(i):
             at = pl.ds(pl.multiple_of(i * tokens, tokens), tokens)
+            high = small_wide[2 * (start + i), 6:7, :tokens]
+            low = small_wide[2 * (start + i), 7:8, :tokens]
+            key_marks = high * 256.0 + low
+            marks_row[:, at] = key_marks
             key_places = (start + i) * tokens + lax.broadcasted_iota(jnp.int32, (1, tokens), 1)
             gap = row_places - key_places
-            seen = (gap >= 0) & (gap < W) & (marks_column[...] == marks_row[:, at])
+            seen = (gap >= 0) & (gap < W) & (marks_column[...] == key_marks)
             mask[:, at] = jnp.where(seen, 0.0, -1e30)
 
+        load(1, vec, vec_out).start()
+        load(2, marks_row, marks_out).start()
+        load(0, x_in, x).wait()
+
+        @pl.loop(0, tokens // 16)
+        def _(i):
+            at = pl.ds(pl.multiple_of(i * 16, 16), 16)
+            value = x[at].astype(f32)
+            scale = lax.rsqrt(jnp.mean(value * value, axis=1, keepdims=True) + epsilon)
+            normed[at] = (value * scale * vec[0:1]).astype(bf16)
+
+        load(0, normed, normed_out).start()
+        share(1, kvw_all).wait()
+        load(3, kvw_all, kvw).start()
+        load(3, kvw_all, kvw).wait()
+        both = dot(normed[...], kvw[...].reshape(width, 2 * HD))
+        kv_low[:, :HD] = turn(both[:, :HD]).astype(bf16)
+        kv_low[:, HD:] = both[:, HD:].astype(bf16)
         next(keys)
-        next(keys)
-        next(ffn)
-        for _ in range(3):
-            next(keys)
-        next(outw)
-        next(keys, None)
-        window = load(2, kv_all.at[pl.ds(start, reach + 1)], win)
-        window.start()
-        load(0, q_in, qs).wait()
-        window.wait()
+        for _ in queries:
+            pass
+        load(3, query_all, weight).start()
+        load(3, query_all, weight).wait()
 
         @pl.loop(0, heads)
         def _(h):
             at = pl.ds(pl.multiple_of(h * HD, HD), HD)
-            both = win[...].reshape(span, 2 * HD)
-            scores = dot(qs[:, at], both[:, :HD], 1, 1) + mask[...]
+            value = dot(normed[...], weight[:, :, at].reshape(width, HD))
+            qs[:, at] = (turn(value) * scale_factor).astype(bf16)
+
+        load(4, qs, queries_out).start()
+        for _ in range(3):
+            next(outw)
+            next(keys)
+        for _ in keys:
+            pass
+        load(3, kv_all.at[pl.ds(start, reach + 1)], win).start()
+        load(3, kv_all.at[pl.ds(start, reach + 1)], win).wait()
+
+        @pl.loop(0, heads)
+        def _(h):
+            at = pl.ds(pl.multiple_of(h * HD, HD), HD)
+            window = win[...].reshape(span, 2 * HD)
+            scores = dot(qs[:, at], window[:, :HD], 1, 1) + mask[...]
             top = jnp.max(scores, axis=1, keepdims=True)
             exponent = jnp.exp(scores - top)
             total = jnp.sum(exponent, axis=1, keepdims=True)
-            blend = dot(exponent.astype(bf16), both[:, HD:])
+            blend = dot(exponent.astype(bf16), window[:, HD:])
             mixed[:, at] = (blend / total).astype(bf16)
             logs[h] = top + jnp.log(total)
-            for i in range(1, heads):
-
-                @pl.when(h == i)
-                def _():
-                    next(outw if i < 4 else ffn)
-
+
+        load(5, mixed, mixed_out).start()
+        load(6, logs, log_out).start()
+        next(ffn)
+        next(outw)
         next(ffn)
         for _ in outw:
             pass
-        load(3, mixed, mixed_out).start()
-        load(4, logs, log_out).start()
-        weights = load(2, out_all, weight)
-        weights.start()
-        weights.wait()
+        load(3, out_all, weight).start()
+        load(3, out_all, weight).wait()
 
         @pl.loop(0, LINE)
         def _(i):
@@ -1054,103 +1076,120 @@
             piece = weight[pl.ds(4 * i, 4)].reshape(4 * rows, heads * HD)
             part[:, at] = dot(mixed[...], piece, 1, 1).astype(bf16)
 
-        swapped = remote(part, theirs, swap_sems[0], swap_sems[1], me.other())
+        swapped = remote(part, theirs, swap_sems[0].at[2], swap_sems[1].at[2], me.other())
         swapped.start()
-        load(1, x_in, x).wait()
         swapped.wait()
 
         @pl.loop(0, tokens // 16)
         def _(i):
             at = pl.ds(pl.multiple_of(i * 16, 16), 16)
-            total = x[at].astype(f32) + (part[at].astype(f32) + theirs[at].astype(f32)) + vec[0:1]
+            total = x[at].astype(f32) + (part[at].astype(f32) + theirs[at].astype(f32)) + vec[1:2]
             middle[at] = total
             scale = lax.rsqrt(jnp.mean(total * total, axis=1, keepdims=True) + epsilon)
-            normed_two[at] = (total * scale * vec[1:2]).astype(bf16)
-
-        out = spread(me, normed_two, normed_out, spread_sems)
+            normed_two[at] = (total * scale * vec[2:3]).astype(bf16)
+
+        out = spread(me, normed_two, normed_two_out, spread_sems)
         next(out)
-        load(0, middle, middle_out).start()
+        load(7, middle, middle_out).start()
         next(ffn)
         next(out)
         next(ffn)
         next(out)
         next(out)
-        next(out)
-        for step in (ffn, out):
+        next(cot)
+        next(ffn)
+        for _ in range(3):
+            next(cot)
+        for step in (ffn, out, cot):
             for _ in step:
                 pass
-        load(3, mixed, mixed_out).wait()
-        load(4, logs, log_out).wait()
-        load(0, middle, middle_out).wait()
+        for n, src, dst in (
+            (0, normed, normed_out),
+            (1, vec, vec_out),
+            (2, marks_row, marks_out),
+            (4, qs, queries_out),
+            (5, mixed, mixed_out),
+            (6, logs, log_out),
+            (7, middle, middle_out),
+        ):
+            load(n, src, dst).wait()
         return []
 
-    kv_all, out_full, ffn_full, mixed_low, log_total, middle, normed_all = transfer(
-        1,
+    query_shape = (tokens, heads * HD)
+    (
+        query_full, kv_full, smalls, kv_all, out_full, ffn_full, cot_all, mixed_low, log_total,
+        middle, normed_all, queries, normed, vec, window_marks,
+    ) = transfer(
+        0,
         [
-            own_block,
-            out_own,
-            gate_up_own,
-            down_own,
-            queries,
-            inputs,
-            jnp.stack([bias_out, gain_two]),
-            window_marks[None],
-            own_marks[:, None],
+            query_own, kv_own, small, out_own, gate_up_own, down_own, inputs, cotangent,
+            own_marks, turn_cos, turn_sin, pick_device, pick_entry,
         ],
         [
-            ((RING,) + own_block.shape, bf16),
+            ((RING,) + query_own.shape, bf16),
+            ((RING, 2) + kv_own.shape, bf16),
+            ((RING, 2) + small.shape, bf16),
+            ((RING, tokens, 2 * HD), bf16),
             ((RING,) + out_own.shape, bf16),
             ((3, RING, rows, block), bf16),
-            (queries.shape, bf16),
+            ((LINE,) + inputs.shape, bf16),
+            (query_shape, bf16),
             ((heads, tokens, 1), f32),
             (inputs.shape, f32),
             ((LINE,) + inputs.shape, bf16),
+            (query_shape, bf16),
+            (inputs.shape, bf16),
+            ((8, width), f32),
+            ((1, span), f32),
         ],
         [
             GATHER_SEMS,
             GATHER_SEMS,
+            GATHER_SEMS,
+            GATHER_SEMS,
+            GATHER_SEMS,
             PIECE_SEMS,
             SPREAD_SEMS,
-            SWAP_SEMS,
+            SPREAD_SEMS,
+            [pltpu.SemaphoreType.DMA((3,)), pltpu.SemaphoreType.DMA((3,))],
             [
-                pltpu.VMEM(queries.shape, bf16),
+                pltpu.VMEM(query_shape, bf16),
                 pltpu.VMEM((reach + 1, tokens, 2 * HD), bf16),
                 pltpu.VMEM((RING,) + out_own.shape, bf16),
+                pltpu.VMEM((RING, 2) + kv_own.shape, bf16),
                 pltpu.VMEM((tokens, span), f32),
-                pltpu.VMEM(queries.shape, bf16),
+                pltpu.VMEM(query_shape, bf16),
                 pltpu.VMEM(inputs.shape, bf16),
                 pltpu.VMEM(inputs.shape, bf16),
                 pltpu.VMEM(inputs.shape, bf16),
                 pltpu.VMEM(inputs.shape, f32),
                 pltpu.VMEM(inputs.shape, bf16),
+                pltpu.VMEM(inputs.shape, bf16),
                 pltpu.VMEM((heads, tokens, 1), f32),
-                pltpu.SemaphoreType.DMA((5,)),
+                pltpu.VMEM((RING, 2) + small.shape, bf16),
+                pltpu.VMEM((2 * RING,) + small.shape, f32),
+                pltpu.VMEM((8, width), f32),
+                pltpu.VMEM((1, span), f32),
+                pltpu.VMEM((tokens, 2 * HD), bf16),
+                pltpu.SemaphoreType.DMA((8,)),
             ],
         ],
-        second_steps,
-        near=(6, 7, 8),
+        first_steps,
+        near=(8, 9, 10, 11, 12),
     )
+    query_full = query_full.reshape(width, heads * HD)
+    kv_full = kv_full.reshape(width, columns)
     out_full = out_full.reshape(width, heads * HD)
     ffn_full = ffn_full.reshape(3, width, block)
-    key_places = first_block * tokens + jnp.arange(span, dtype=jnp.int32)
-    key_gap = places[:, None] - key_places[None, :]
-    visible = (key_gap >= 0) & (key_gap < W) & (own_marks[:, None] == window_marks[None, :])
-    window = lax.dynamic_slice_in_dim(
-        kv_all.reshape(RING * tokens, 2 * HD), first_block * tokens, span, 0
-    )
-    key_win = window[:, :HD]
-    value_win = window[:, HD:]
-    query_heads = queries.reshape(tokens, heads, HD)
-
-    def both_cores(number, part):
-        (theirs,) = transfer(
-            number,
-            [part],
-            [(part.shape, bf16)],
-            [SWAP_SEMS],
-            lambda me, ins, outs, sems: [swap(me, ins[0], outs[0], sems[0])],
-        )
-        return part.astype(f32) + theirs.astype(f32)
+    gain_one, _, gain_two, bias_down = (vec[i] for i in range(4))
+    stream = inputs.astype(f32)
+
+    def hidden_vector(row):
+        piece = smalls[:, :, row, : hidden_bias.shape[1]].reshape(RING, 2, groups, -1)
+        return jnp.transpose(piece, (2, 0, 1, 3)).reshape(-1).astype(f32)
+
+    bias_gate_up = jnp.stack([hidden_vector(4 + i) for i in range(2)])
+    bias_local = lax.dynamic_slice_in_dim(bias_gate_up, t * hidden_half + block_start, block, 1)
 
     ours = (jnp.arange(block) >= block_skip).astype(f32)[None, :]
     part_rows = 4 * rows
@@ -1347,7 +1386,7 @@
 
     half_shape = (2, 3, LINE, rows // 2, block)
     normed_two_grad, mlp_out, ffn_total, hidden_bias_part, bias_theirs, ffn_term = transfer(
-        4,
+        1,
         [normed_all, cot_all, ffn_full, bias_local, ours],
         [
             ((tokens, width), bf16),
@@ -1420,10 +1459,6 @@
         [widen(vector_terms), widen(bias_terms), jnp.zeros((RING, 27, HD), f32)], axis=1
     ).astype(bf16)
 
-    frequency = 10000.0 ** (-jnp.arange(HD // 4, dtype=f32) / (HD // 4))
-    angles = places.astype(f32)[:, None] * frequency[None, :]
-    turn_cos = jnp.concatenate([jnp.cos(angles), jnp.cos(angles)], axis=1)
-    turn_sin = jnp.concatenate([-jnp.sin(angles), jnp.sin(angles)], axis=1)
     chunk = 3 if (reach + 1) % 3 == 0 else 1
     pieces = (reach + 1) // chunk
     kv_size = rows + small_terms.shape[1]
@@ -1683,11 +1718,11 @@
     half = (2, 2, LINE, rows // 2, heads * HD)
     kv_half = (2, 2, LINE, kv_size // 2, HD)
     ffn_done, out_done, query_done, kv_done, input_grad, gain_all = transfer(
-        5,
+        2,
         [
             middle_low, out_full, mixed_low, queries, kv_all, log_total, normed, query_full, kv_full,
             ffn_term, ffn_total, small_terms, middle_grad, inputs,
-            window_marks[None], own_marks[:, None], turn_cos, turn_sin, gain_one[None],
+            window_marks, own_marks, turn_cos, turn_sin, gain_one[None],
         ],
         [
             (ffn_shape, bf16),

time: 765 us -> 733 us (0.958)
  local copies, waits for them, and re-layouts: 25.5 us -> 13 us
  Pallas kernels: 692 us -> 684 us
    dot_general x1 -> x0, local copies, waits for them, and re-layouts: 9.53 us -> none  [dot(): lax.dot_general(a, b, (((ca,), (cb,)), ((), ())), preferred_element_type=...]
    pallas_call x4 -> x3, Pallas kernels: 692 us -> 684 us  [transfer(): pl.pallas_call(kernel, out_shape=[jax.ShapeDtypeStruct(shape, dtype) for...]
where the time goes in v6:
time: 733 us; the launch traced here: 724 us
  Pallas kernels  684 us (93%)
  other arithmetic  26.1 us (4%)
  local copies, waits for them, and re-layouts  13 us (2%)
    pallas_call x3, Pallas kernels, transfer(): pl.pallas_call(kernel, out_shape=[jax.ShapeDtypeStruct(shape, dtype) for...  684 us

profile of v6, /device:TPU:0, one launch (start us, length us, event | category | flops | bytes accessed | tf_op | source)
XLA Modules:
  0.0 723.9 jit_solution(2420700703729125219)
XLA Ops:
  0.9 0.8 fusion.50
  2.3 0.7 fusion.39
  3.0 1.4 fusion.25.refs_2_
  4.4 0.8 copy.27.refs_8_.refs_15_
  6.4 0.8 pad_maximum_fusion.1
  7.3 0.9 fusion.4.refs_12_
  8.2 321.0 %shard_map.220 = (bf16[16,160,1280]{2,1,0:T(8,128)(2,1)}, bf16[16,2,80,512]{3,2,1,0:T(8,128)(2,1)}, bf16[16,2,16,512]{3,2,1,0:T(8,128)(2,1)}, bf16[16,256,512]{2...) custom-call(bf16[160,1280]{1,0:T(8,128)(2,1)} %refs_0_.1, ...), custom_call_target="tpu_custom_call" | custom-call | tf_op jit(solution)/shard_map/pallas_call | solution.py:763
  329.3 2.0 multiply_reduce_fusion
  331.3 1.2 slice_reduce_fusion.1
  333.4 1.7 slice_reduce_fusion.2
  335.0 138.1 %shard_map.221 = (bf16[256,2560]{1,0:T(8,128)(2,1)}, bf16[256,2560]{1,0:T(8,128)(2,1)}, bf16[3,4,160,1024]{3,2,1,0:T(8,128)(2,1)}, bf16[16,1024]{1,0:T(8,128)(2,...) custom-call(bf16[4,256,2560]{2,1,0:T(8,128)(2,1)} %get-tuple-element, ...), custom_call_target="tpu_custom_call" | custom-call | tf_op jit(solution)/shard_map/pallas_call | solution.py:763
  473.1 3.2 fusion.3
  476.4 4.2 fusion.48
  481.6 0.8 fusion.10.refs_11_
  482.4 1.2 convert_element_type.104.refs_0_
  483.6 224.6 %shard_map.222 = (bf16[3,4,160,1024]{3,2,1,0:T(8,128)(2,1)}, bf16[4,160,1280]{2,1,0:T(8,128)(2,1)}, bf16[2,4,160,640]{3,2,1,0:T(8,128)(2,1)}, bf16[2,4,192,256]{...) custom-call(bf16[256,2560]{1,0:T(8,128)(2,1)} %convert_element_type., ...), custom_call_target="tpu_custom_call" | custom-call | tf_op jit(solution)/shard_map/pallas_call | solution.py:763
  708.1 1.0 convert_reduce_fusion.4
  709.8 1.3 convert_reduce_fusion.3
  712.9 1.2 slice_bitcast_fusion.3
  714.4 0.9 pad_maximum_fusion
  715.8 1.1 convert_reduce_fusion
  717.3 1.6 convert_bitcast_fusion
  719.5 2.6 slice.97
  722.4 1.5 copy.45
  (64 shorter events, 8.3 us)
Async XLA Ops:
  473.1 3.2 copy-start.1
  473.1 3.3 copy-start.2
  476.4 4.3 copy-start.7
  476.4 4.4 copy-start.8
  480.6 1.8 copy-start
  708.1 6.0 copy-start.6
  714.1 1.7 copy-start.5
  714.4 2.7 copy-start.3
  719.5 2.9 copy-start.4

commit v7 on v6

--- a/solution.py
+++ b/solution.py
@@ -1045,6 +1045,8 @@
             next(keys)
         for _ in keys:
             pass
+        next(ffn)
+        next(ffn)
         load(3, kv_all.at[pl.ds(start, reach + 1)], win).start()
         load(3, kv_all.at[pl.ds(start, reach + 1)], win).wait()
 
@@ -1062,11 +1064,10 @@
 
         load(5, mixed, mixed_out).start()
         load(6, logs, log_out).start()
-        next(ffn)
         next(outw)
-        next(ffn)
         for _ in outw:
             pass
+        next(ffn)
         load(3, out_all, weight).start()
         load(3, out_all, weight).wait()
 
@@ -1091,10 +1092,10 @@
         out = spread(me, normed_two, normed_two_out, spread_sems)
         next(out)
         load(7, middle, middle_out).start()
+        next(out)
         next(ffn)
         next(out)
         next(ffn)
-        next(out)
         next(out)
         next(cot)
         next(ffn)
@@ -1614,6 +1615,9 @@
         swapped = remote(part, theirs, swap_sems[0], swap_sems[1], me.other())
         swapped.start()
         next(ffn)
+        next(outw)
+        next(query)
+        next(ffn)
         next(window_steps)
         next(window_steps, None)
 
@@ -1634,13 +1638,10 @@
             copy.start()
             copy.wait()
 
+        next(more)
+        next(kvw_steps)
         next(outw)
         next(query)
-        next(ffn)
-        next(more)
-        next(kvw_steps)
-        next(query)
-        next(outw)
 
         swapped.wait()
 

time: 733 us -> 709 us (0.967)
  Pallas kernels: 684 us -> 664 us
    pallas_call x3, Pallas kernels: 684 us -> 664 us  [transfer(): pl.pallas_call(kernel, out_shape=[jax.ShapeDtypeStruct(shape, dtype) for...]
where the time goes in v7:
time: 709 us; the launch traced here: 704 us
  Pallas kernels  664 us (94%)
  other arithmetic  26.1 us (4%)
  local copies, waits for them, and re-layouts  13 us (2%)
    pallas_call x3, Pallas kernels, transfer(): pl.pallas_call(kernel, out_shape=[jax.ShapeDtypeStruct(shape, dtype) for...  664 us

profile of v7, /device:TPU:0, one launch (start us, length us, event | category | flops | bytes accessed | tf_op | source)
XLA Modules:
  0.0 704.3 jit_solution(13874079781545110035)
XLA Ops:
  0.9 0.8 fusion.50
  2.3 0.7 fusion.39
  3.0 1.4 fusion.25.refs_2_
  4.4 0.8 copy.27.refs_8_.refs_15_
  6.4 0.8 pad_maximum_fusion.1
  7.3 0.9 fusion.4.refs_12_
  8.2 315.4 %shard_map.220 = (bf16[16,160,1280]{2,1,0:T(8,128)(2,1)}, bf16[16,2,80,512]{3,2,1,0:T(8,128)(2,1)}, bf16[16,2,16,512]{3,2,1,0:T(8,128)(2,1)}, bf16[16,256,512]{2...) custom-call(bf16[160,1280]{1,0:T(8,128)(2,1)} %refs_0_.1, ...), custom_call_target="tpu_custom_call" | custom-call | tf_op jit(solution)/shard_map/pallas_call | solution.py:763
  323.7 2.0 multiply_reduce_fusion
  325.7 1.2 slice_reduce_fusion.1
  327.8 1.7 slice_reduce_fusion.2
  329.4 140.7 %shard_map.221 = (bf16[256,2560]{1,0:T(8,128)(2,1)}, bf16[256,2560]{1,0:T(8,128)(2,1)}, bf16[3,4,160,1024]{3,2,1,0:T(8,128)(2,1)}, bf16[16,1024]{1,0:T(8,128)(2,...) custom-call(bf16[4,256,2560]{2,1,0:T(8,128)(2,1)} %get-tuple-element, ...), custom_call_target="tpu_custom_call" | custom-call | tf_op jit(solution)/shard_map/pallas_call | solution.py:763
  470.1 3.2 fusion.3
  473.4 4.2 fusion.48
  478.6 0.8 fusion.10.refs_11_
  479.4 1.2 convert_element_type.104.refs_0_
  480.5 208.1 %shard_map.222 = (bf16[3,4,160,1024]{3,2,1,0:T(8,128)(2,1)}, bf16[4,160,1280]{2,1,0:T(8,128)(2,1)}, bf16[2,4,160,640]{3,2,1,0:T(8,128)(2,1)}, bf16[2,4,192,256]{...) custom-call(bf16[256,2560]{1,0:T(8,128)(2,1)} %convert_element_type., ...), custom_call_target="tpu_custom_call" | custom-call | tf_op jit(solution)/shard_map/pallas_call | solution.py:763
  688.6 1.0 convert_reduce_fusion.4
  690.3 1.3 convert_reduce_fusion.3
  693.4 1.2 slice_bitcast_fusion.3
  694.9 0.9 pad_maximum_fusion
  696.3 1.1 convert_reduce_fusion
  697.8 1.6 convert_bitcast_fusion
  700.0 2.6 slice.97
  702.8 1.5 copy.45
  (64 shorter events, 8.3 us)
Async XLA Ops:
  470.1 3.2 copy-start.1
  470.1 3.3 copy-start.2
  473.4 4.3 copy-start.7
  473.4 4.4 copy-start.8
  477.6 1.8 copy-start
  688.6 6.0 copy-start.6
  694.6 1.7 copy-start.5
  694.8 2.7 copy-start.3
  700.0 2.9 copy-start.4

commit v8 on v7

--- a/solution.py
+++ b/solution.py
@@ -978,7 +978,7 @@
             next(queries)
             if n == 3:
                 next(outw)
-        next(ffn)
+                next(ffn)
         for _ in smalls:
             pass
         share(0, small_all).start()

time: 709 us -> 704 us (level)
  no operation moved by 1% of the time
where the time goes in v8:
time: 704 us; the launch traced here: 700 us
  Pallas kernels  660 us (94%)
  other arithmetic  26.1 us (4%)
  local copies, waits for them, and re-layouts  13 us (2%)
    pallas_call x3, Pallas kernels, transfer(): pl.pallas_call(kernel, out_shape=[jax.ShapeDtypeStruct(shape, dtype) for...  660 us

profile of v8, /device:TPU:0, one launch (start us, length us, event | category | flops | bytes accessed | tf_op | source)
XLA Modules:
  0.0 700.4 jit_solution(12625054767568482813)
XLA Ops:
  0.9 0.8 fusion.50
  2.3 0.7 fusion.39
  3.0 1.4 fusion.25.refs_2_
  4.4 0.8 copy.27.refs_8_.refs_15_
  6.4 0.8 pad_maximum_fusion.1
  7.3 0.9 fusion.4.refs_12_
  8.2 312.9 %shard_map.220 = (bf16[16,160,1280]{2,1,0:T(8,128)(2,1)}, bf16[16,2,80,512]{3,2,1,0:T(8,128)(2,1)}, bf16[16,2,16,512]{3,2,1,0:T(8,128)(2,1)}, bf16[16,256,512]{2...) custom-call(bf16[160,1280]{1,0:T(8,128)(2,1)} %refs_0_.1, ...), custom_call_target="tpu_custom_call" | custom-call | tf_op jit(solution)/shard_map/pallas_call | solution.py:763
  321.2 2.0 multiply_reduce_fusion
  323.2 1.2 slice_reduce_fusion.1
  325.3 1.7 slice_reduce_fusion.2
  326.9 138.1 %shard_map.221 = (bf16[256,2560]{1,0:T(8,128)(2,1)}, bf16[256,2560]{1,0:T(8,128)(2,1)}, bf16[3,4,160,1024]{3,2,1,0:T(8,128)(2,1)}, bf16[16,1024]{1,0:T(8,128)(2,...) custom-call(bf16[4,256,2560]{2,1,0:T(8,128)(2,1)} %get-tuple-element, ...), custom_call_target="tpu_custom_call" | custom-call | tf_op jit(solution)/shard_map/pallas_call | solution.py:763
  465.1 3.2 fusion.3
  468.4 4.2 fusion.48
  473.5 0.8 fusion.10.refs_11_
  474.3 1.2 convert_element_type.104.refs_0_
  475.5 209.2 %shard_map.222 = (bf16[3,4,160,1024]{3,2,1,0:T(8,128)(2,1)}, bf16[4,160,1280]{2,1,0:T(8,128)(2,1)}, bf16[2,4,160,640]{3,2,1,0:T(8,128)(2,1)}, bf16[2,4,192,256]{...) custom-call(bf16[256,2560]{1,0:T(8,128)(2,1)} %convert_element_type., ...), custom_call_target="tpu_custom_call" | custom-call | tf_op jit(solution)/shard_map/pallas_call | solution.py:763
  684.7 1.0 convert_reduce_fusion.4
  686.3 1.3 convert_reduce_fusion.3
  689.5 1.2 slice_bitcast_fusion.3
  691.0 0.9 pad_maximum_fusion
  692.4 1.1 convert_reduce_fusion
  693.9 1.6 convert_bitcast_fusion
  696.0 2.6 slice.97
  698.9 1.5 copy.45
  (64 shorter events, 8.3 us)
Async XLA Ops:
  465.1 3.2 copy-start.1
  465.1 3.3 copy-start.2
  468.4 4.3 copy-start.7
  468.4 4.4 copy-start.8
  472.5 1.8 copy-start
  684.7 6.0 copy-start.6
  690.7 1.7 copy-start.5
  690.9 2.7 copy-start.3
  696.0 2.9 copy-start.4
